TPU v7x, 32 devices: a whole 2x2x4 slice. The times are simulated.
32 devices in a mesh: band: 16 (over z, y, x), canvas: 2 (over core).
Axes of the slice: x: 2, y: 2, z: 4, core: 2. Of those that a mesh axis runs over, the one named last changes fastest.
Arguments:
- inputs: bfloat16 [2, 64, 64, 512], P('canvas', 'band'), may hold values from -13 to 13
- crop_ids: int32 [2, 64, 64], P('canvas'), may hold values from 0 to 36, as said below
- cotangent: bfloat16 [2, 64, 64, 512], P('canvas', 'band'), may hold values from -6 to 6
- norm1_gain: bfloat16 [512], P(('band', 'canvas')), may hold values from 0.5 to 1.5
- norm1_shift: bfloat16 [512], P(('band', 'canvas')), may hold values from -3 to 3
- conv1_weight: bfloat16 [4608, 512], P(('band', 'canvas')), may hold values from -0.09375 to 0.09375
- conv1_bias: bfloat16 [512], P(('band', 'canvas')), may hold values from -3 to 3
- norm2_gain: bfloat16 [512], P(('band', 'canvas')), may hold values from 0.5 to 1.5
- norm2_shift: bfloat16 [512], P(('band', 'canvas')), may hold values from -3 to 3
- conv2_weight: bfloat16 [4608, 512], P(('band', 'canvas')), may hold values from -0.09375 to 0.09375
- conv2_bias: bfloat16 [512], P(('band', 'canvas')), may hold values from -3 to 3
- norm3_gain: bfloat16 [512], P(('band', 'canvas')), may hold values from 0.5 to 1.5
- norm3_shift: bfloat16 [512], P(('band', 'canvas')), may hold values from -3 to 3
- query_weight: bfloat16 [512, 512], P(('band', 'canvas')), may hold values from -0.25 to 0.25
- query_bias: bfloat16 [512], P(('band', 'canvas')), may hold values from -3 to 3
- key_weight: bfloat16 [512, 512], P(('band', 'canvas')), may hold values from -0.25 to 0.25
- value_weight: bfloat16 [512, 512], P(('band', 'canvas')), may hold values from -0.25 to 0.25
- value_bias: bfloat16 [512], P(('band', 'canvas')), may hold values from -1.25 to 1.25
- out_weight: bfloat16 [512, 512], P(('band', 'canvas')), may hold values from -4 to 4
- out_bias: bfloat16 [512], P(('band', 'canvas')), may hold values from -3 to 3
Outputs:
- output: bfloat16 [2, 64, 64, 512], P('canvas', 'band')
- input_grad: float32 [2, 64, 64, 512], P('canvas', 'band')
- norm1_gain_grad: float32 [512], P(('band', 'canvas'))
- norm1_shift_grad: float32 [512], P(('band', 'canvas'))
- conv1_weight_grad: float32 [4608, 512], P(('band', 'canvas'))
- conv1_bias_grad: float32 [512], P(('band', 'canvas'))
- norm2_gain_grad: float32 [512], P(('band', 'canvas'))
- norm2_shift_grad: float32 [512], P(('band', 'canvas'))
- conv2_weight_grad: float32 [4608, 512], P(('band', 'canvas'))
- conv2_bias_grad: float32 [512], P(('band', 'canvas'))
- norm3_gain_grad: float32 [512], P(('band', 'canvas'))
- norm3_shift_grad: float32 [512], P(('band', 'canvas'))
- query_weight_grad: float32 [512, 512], P(('band', 'canvas'))
- query_bias_grad: float32 [512], P(('band', 'canvas'))
- key_weight_grad: float32 [512, 512], P(('band', 'canvas'))
- value_weight_grad: float32 [512, 512], P(('band', 'canvas'))
- value_bias_grad: float32 [512], P(('band', 'canvas'))
- out_weight_grad: float32 [512, 512], P(('band', 'canvas'))
- out_bias_grad: float32 [512], P(('band', 'canvas'))
Inputs may be any that keep to these rules, and one draw needn't show every extreme that they name: `crop_ids`: each canvas is cut into strips of 16 columns; a crop is a rectangle of a strip's full width and consecutive rows, at most 32 rows, except that in each canvas one strip drawn from the seed is a single crop of all 64 rows with number 37 - 1.
All inputs are finite; a program needn't handle non-finite values.
Results may differ from a plain program's by a relative error of at most 0.015.
Values may be sent and summed in bfloat16 or wider, within the bound.
A program may use at most 192 MiB of HBM per device.

v0:
```python
import functools
import types

import jax
import jax.numpy as jnp
from jax import lax
from jax.experimental import pallas as pl
from jax.experimental.pallas import tpu as pltpu
from jax.sharding import PartitionSpec as P

GROUPS = 32


EPS = 1e-06
HIGH = lax.Precision.HIGHEST
NEG = -1e30


def extended(cells, sides, width):
    for axis, dim in sides:
        count = lax.axis_size(axis)
        ends = count - 1
        head = lax.slice_in_dim(cells, 0, width, axis=dim)
        tail = lax.slice_in_dim(cells, cells.shape[dim] - width, cells.shape[dim], axis=dim)
        cells = jnp.concatenate(
            [
                lax.ppermute(tail, axis, [(i, (i + 1) % count) for i in range(ends)]),
                cells,
                lax.ppermute(head, axis, [((i + 1) % count, i) for i in range(ends)]),
            ],
            axis=dim,
        )
    return cells


def rim_rows(field):
    return extended(field, (("band", 1),), 1)


def crop_sums(pair):
    return lax.psum((pair[0], pair[1]), "band")


def as_float(member):
    return member.astype(jnp.float32)


def group_fold(per_channel):
    shape = per_channel.shape
    return jnp.sum(per_channel.reshape(shape[0], shape[1], GROUPS, shape[2] // GROUPS), axis=-1)


def spread_back(stat, onehot, channels):
    widened = jnp.repeat(stat, channels // GROUPS, axis=-1)
    return jnp.einsum("btk,bkc->btc", onehot, widened, precision=HIGH)


def norm_forward(field, onehot, counts, gain_vec, shift_vec):
    channels = field.shape[-1]
    first_sum = group_fold(jnp.einsum("btk,btc->bkc", onehot, field, precision=HIGH))
    square_sum = group_fold(jnp.einsum("btk,btc->bkc", onehot, field * field, precision=HIGH))
    first_sum, square_sum = crop_sums((first_sum, square_sum))
    crop_mean = first_sum / counts
    inverse = lax.rsqrt(square_sum / counts - crop_mean * crop_mean + EPS)
    rstd_pix = spread_back(inverse, onehot, channels)
    centred = (field - spread_back(crop_mean, onehot, channels)) * rstd_pix
    return (centred * gain_vec + shift_vec, centred, rstd_pix)


def norm_backward(grad_in, centred, rstd_pix, gain_vec, onehot, counts):
    channels = grad_in.shape[-1]
    scaled = grad_in * gain_vec
    first_sum = group_fold(jnp.einsum("btk,btc->bkc", onehot, scaled, precision=HIGH))
    second_sum = group_fold(jnp.einsum("btk,btc->bkc", onehot, scaled * centred, precision=HIGH))
    first_sum, second_sum = crop_sums((first_sum, second_sum))
    field_grad = rstd_pix * (
        scaled
        - spread_back(first_sum / counts, onehot, channels)
        - centred * spread_back(second_sum / counts, onehot, channels)
    )
    return (field_grad, jnp.sum(grad_in * centred, axis=(0, 1)), jnp.sum(grad_in, axis=(0, 1)))


def patches(field, crop_rim, crop_mid):
    canvas_count, rim_count, canvas_width, channels = field.shape
    band_rows = rim_count - 2
    padded = jnp.pad(field, ((0, 0), (0, 0), (1, 1), (0, 0)))
    tap_list = []
    for shift_r in range(3):
        for shift_c in range(3):
            neighbour = padded[:, shift_r : shift_r + band_rows, shift_c : shift_c + canvas_width]
            same_crop = (
                crop_rim[:, shift_r : shift_r + band_rows, shift_c : shift_c + canvas_width]
                == crop_mid
            )
            tap_list.append(jnp.where(same_crop[..., None], neighbour, jnp.zeros_like(neighbour)))
    return jnp.concatenate(tap_list, axis=-1).reshape(
        canvas_count * band_rows * canvas_width, 9 * channels
    )


def flipped(weight):
    channels = weight.shape[1]
    return (
        weight.reshape(9, channels, channels)[::-1]
        .transpose(0, 2, 1)
        .reshape(9 * channels, channels)
    )


def silu_slope(normed):
    sigmoid_val = jax.nn.sigmoid(normed)
    return sigmoid_val * (1.0 + normed * (1.0 - sigmoid_val))


def on_device(
    inputs,
    crop_ids,
    cotangent,
    norm1_gain,
    norm1_shift,
    conv1_weight,
    conv1_bias,
    norm2_gain,
    norm2_shift,
    conv2_weight,
    conv2_bias,
    norm3_gain,
    norm3_shift,
    query_weight,
    query_bias,
    key_weight,
    value_weight,
    value_bias,
    out_weight,
    out_bias,
):
    canvas_count, band_rows, canvas_width, channels = inputs.shape
    height = crop_ids.shape[1]
    pixel_count = band_rows * canvas_width
    crop_total = canvas_width // 16 * 9 + 1
    score_scale = channels ** (-0.5)
    grid_shape = (canvas_count, band_rows, canvas_width, channels)
    start_row = lax.axis_index("band") * band_rows
    crop_pad = jnp.pad(crop_ids, ((0, 0), (1, 1), (1, 1)), constant_values=-1)
    crop_rim = lax.dynamic_slice_in_dim(crop_pad, start_row, band_rows + 2, 1)
    crop_mid = crop_rim[:, 1:-1, 1:-1]
    own_crop = crop_mid.reshape(canvas_count, pixel_count)
    crop_flat = crop_ids.reshape(canvas_count, height * canvas_width)
    labels = jnp.arange(crop_total, dtype=jnp.int32)
    onehot = (own_crop[:, :, None] == labels[None, None, :]).astype(jnp.float32)
    counts = jnp.maximum(
        jnp.sum((crop_flat[:, :, None] == labels[None, None, :]).astype(jnp.float32), axis=1)
        * (channels // GROUPS),
        1.0,
    )[:, :, None]
    res_shards = (
        conv1_weight,
        conv2_weight,
        norm1_gain,
        norm1_shift,
        conv1_bias,
        norm2_gain,
        norm2_shift,
        conv2_bias,
    )
    attn_shards = (
        query_weight,
        key_weight,
        value_weight,
        out_weight,
        query_bias,
        value_bias,
        out_bias,
        norm3_gain,
        norm3_shift,
    )
    res_full = (
        lax.all_gather(res_shards[0], ("band", "canvas"), axis=0, tiled=True),
        lax.all_gather(res_shards[1], ("band", "canvas"), axis=0, tiled=True),
        lax.all_gather(res_shards[2], ("band", "canvas"), axis=0, tiled=True),
        lax.all_gather(res_shards[3], ("band", "canvas"), axis=0, tiled=True),
        lax.all_gather(res_shards[4], ("band", "canvas"), axis=0, tiled=True),
        lax.all_gather(res_shards[5], ("band", "canvas"), axis=0, tiled=True),
        lax.all_gather(res_shards[6], ("band", "canvas"), axis=0, tiled=True),
        lax.all_gather(res_shards[7], ("band", "canvas"), axis=0, tiled=True),
    )
    attn_full = (
        lax.all_gather(attn_shards[0], ("band", "canvas"), axis=0, tiled=True),
        lax.all_gather(attn_shards[1], ("band", "canvas"), axis=0, tiled=True),
        lax.all_gather(attn_shards[2], ("band", "canvas"), axis=0, tiled=True),
        lax.all_gather(attn_shards[3], ("band", "canvas"), axis=0, tiled=True),
        lax.all_gather(attn_shards[4], ("band", "canvas"), axis=0, tiled=True),
        lax.all_gather(attn_shards[5], ("band", "canvas"), axis=0, tiled=True),
        lax.all_gather(attn_shards[6], ("band", "canvas"), axis=0, tiled=True),
        lax.all_gather(attn_shards[7], ("band", "canvas"), axis=0, tiled=True),
        lax.all_gather(attn_shards[8], ("band", "canvas"), axis=0, tiled=True),
    )
    conv_one, conv_two, gain_one, shift_one, bias_one, gain_two, shift_two, bias_two = res_full
    (
        query_full,
        key_full,
        value_full,
        out_full,
        query_add,
        value_add,
        out_add,
        gain_three,
        shift_three,
    ) = attn_full
    flat_input = inputs.astype(jnp.float32).reshape(canvas_count, pixel_count, channels)
    normed_one, centred_one, rstd_one = norm_forward(
        flat_input, onehot, counts, as_float(gain_one), as_float(shift_one)
    )
    act_one = jax.nn.silu(normed_one).astype(jnp.bfloat16)
    cols_one = patches(rim_rows(act_one.reshape(grid_shape)), crop_rim, crop_mid)
    conv_first = (
        jnp.dot(cols_one, conv_one, preferred_element_type=jnp.float32) + as_float(bias_one)
    ).reshape(flat_input.shape)
    normed_two, centred_two, rstd_two = norm_forward(
        conv_first, onehot, counts, as_float(gain_two), as_float(shift_two)
    )
    act_two = jax.nn.silu(normed_two).astype(jnp.bfloat16)
    cols_two = patches(rim_rows(act_two.reshape(grid_shape)), crop_rim, crop_mid)
    conv_second = (
        jnp.dot(cols_two, conv_two, preferred_element_type=jnp.float32) + as_float(bias_two)
    ).reshape(flat_input.shape)
    residual = flat_input + conv_second
    normed_three, centred_three, rstd_three = norm_forward(
        residual, onehot, counts, as_float(gain_three), as_float(shift_three)
    )
    hidden = normed_three.astype(jnp.bfloat16)
    queries = (
        jnp.einsum("btc,cd->btd", hidden, query_full, preferred_element_type=jnp.float32)
        + as_float(query_add)
    ).astype(jnp.bfloat16)
    keys_own = jnp.einsum(
        "btc,cd->btd", hidden, key_full, preferred_element_type=jnp.float32
    ).astype(jnp.bfloat16)
    values_own = (
        jnp.einsum("btc,cd->btd", hidden, value_full, preferred_element_type=jnp.float32)
        + as_float(value_add)
    ).astype(jnp.bfloat16)
    row_top = jnp.full((canvas_count, pixel_count), NEG, jnp.float32)
    key_piece = lax.all_gather(keys_own, "band", axis=1, tiled=True)
    value_piece = lax.all_gather(values_own, "band", axis=1, tiled=True)
    piece_crop = crop_flat
    same_crop = own_crop[:, :, None] == piece_crop[:, None, :]
    scores = (
        jnp.einsum("btc,bnc->btn", queries, key_piece, preferred_element_type=jnp.float32)
        * score_scale
    )
    scores = jnp.where(same_crop, scores, NEG)
    new_top = jnp.maximum(row_top, jnp.max(scores, axis=-1))
    weight = jnp.where(same_crop, jnp.exp(scores - new_top[:, :, None]), 0.0)
    row_total = jnp.sum(weight, axis=-1)
    weighted_sum = jnp.einsum(
        "btn,bnc->btc", weight.astype(jnp.bfloat16), value_piece, preferred_element_type=jnp.float32
    )
    row_top, row_total, weighted_sum = (new_top, row_total, weighted_sum)
    mixed_rows = weighted_sum / row_total[:, :, None]
    log_total = row_top + jnp.log(row_total)
    mixed_low = mixed_rows.astype(jnp.bfloat16)
    output = (
        residual
        + jnp.einsum("btc,cd->btd", mixed_low, out_full, preferred_element_type=jnp.float32)
        + as_float(out_add)
    )
    grad_out = cotangent.reshape(canvas_count, pixel_count, channels)
    grad_float = grad_out.astype(jnp.float32)
    out_grad = jnp.einsum("btc,btd->cd", mixed_low, grad_out, preferred_element_type=jnp.float32)
    out_add_grad = jnp.sum(grad_float, axis=(0, 1))
    mixed_grad = jnp.einsum(
        "btd,cd->btc", grad_out, out_full, preferred_element_type=jnp.float32
    ).astype(jnp.bfloat16)
    row_delta = jnp.sum(mixed_grad.astype(jnp.float32) * mixed_rows, axis=-1)
    all_lse, all_delta = (
        lax.all_gather(log_total, "band", axis=1, tiled=True),
        lax.all_gather(row_delta, "band", axis=1, tiled=True),
    )
    shards_in = (
        lax.all_gather(keys_own, "band", axis=1, tiled=True),
        lax.all_gather(values_own, "band", axis=1, tiled=True),
    )
    key_piece = shards_in[0]
    piece_crop = crop_flat
    same_crop = own_crop[:, :, None] == piece_crop[:, None, :]
    scores = (
        jnp.einsum("btc,bnc->btn", queries, key_piece, preferred_element_type=jnp.float32)
        * score_scale
    )
    attn_prob = jnp.where(same_crop, jnp.exp(scores - log_total[:, :, None]), 0.0)
    prob_grad = jnp.einsum(
        "btc,bnc->btn", mixed_grad, shards_in[1], preferred_element_type=jnp.float32
    )
    score_grad = (attn_prob * (prob_grad - row_delta[:, :, None])).astype(jnp.bfloat16)
    query_grad = (
        jnp.einsum("btn,bnc->btc", score_grad, key_piece, preferred_element_type=jnp.float32)
        * score_scale
    )
    shards_in = (
        lax.all_gather(queries, "band", axis=1, tiled=True),
        lax.all_gather(mixed_grad, "band", axis=1, tiled=True),
    )
    query_piece = shards_in[0]
    grad_piece = shards_in[1]
    piece_crop = crop_flat
    same_crop = piece_crop[:, :, None] == own_crop[:, None, :]
    scores = (
        jnp.einsum("bnc,btc->bnt", query_piece, keys_own, preferred_element_type=jnp.float32)
        * score_scale
    )
    attn_prob = jnp.where(same_crop, jnp.exp(scores - all_lse[:, :, None]), 0.0)
    value_term = jnp.einsum(
        "bnt,bnc->btc",
        attn_prob.astype(jnp.bfloat16),
        grad_piece,
        preferred_element_type=jnp.float32,
    )
    prob_grad = jnp.einsum(
        "bnc,btc->bnt", grad_piece, values_own, preferred_element_type=jnp.float32
    )
    score_grad = (attn_prob * (prob_grad - all_delta[:, :, None])).astype(jnp.bfloat16)
    key_term = (
        jnp.einsum("bnt,bnc->btc", score_grad, query_piece, preferred_element_type=jnp.float32)
        * score_scale
    )
    key_term, value_term = (key_term, value_term)
    query_low = query_grad.astype(jnp.bfloat16)
    key_low = key_term.astype(jnp.bfloat16)
    value_low = value_term.astype(jnp.bfloat16)
    query_w_grad = jnp.einsum("btc,btd->cd", hidden, query_low, preferred_element_type=jnp.float32)
    key_w_grad = jnp.einsum("btc,btd->cd", hidden, key_low, preferred_element_type=jnp.float32)
    value_w_grad = jnp.einsum("btc,btd->cd", hidden, value_low, preferred_element_type=jnp.float32)
    query_add_grad = jnp.sum(query_low.astype(jnp.float32), axis=(0, 1))
    value_add_grad = jnp.sum(value_low.astype(jnp.float32), axis=(0, 1))
    hidden_grad = (
        jnp.einsum("btd,cd->btc", query_low, query_full, preferred_element_type=jnp.float32)
        + jnp.einsum("btd,cd->btc", key_low, key_full, preferred_element_type=jnp.float32)
        + jnp.einsum("btd,cd->btc", value_low, value_full, preferred_element_type=jnp.float32)
    )
    resid_part, gain_three_grad, shift_three_grad = norm_backward(
        hidden_grad, centred_three, rstd_three, as_float(gain_three), onehot, counts
    )
    resid_grad = grad_float + resid_part
    second_low = resid_grad.astype(jnp.bfloat16)
    conv_two_grad = jnp.einsum(
        "pk,pc->kc", cols_two, second_low.reshape(-1, channels), preferred_element_type=jnp.float32
    )
    bias_two_grad = jnp.sum(second_low.astype(jnp.float32), axis=(0, 1))
    act_two_grad = jnp.dot(
        patches(rim_rows(second_low.reshape(grid_shape)), crop_rim, crop_mid),
        flipped(conv_two),
        preferred_element_type=jnp.float32,
    ).reshape(flat_input.shape)
    first_conv_grad, gain_two_grad, shift_two_grad = norm_backward(
        act_two_grad * silu_slope(normed_two),
        centred_two,
        rstd_two,
        as_float(gain_two),
        onehot,
        counts,
    )
    first_low = first_conv_grad.astype(jnp.bfloat16)
    conv_one_grad = jnp.einsum(
        "pk,pc->kc", cols_one, first_low.reshape(-1, channels), preferred_element_type=jnp.float32
    )
    bias_one_grad = jnp.sum(first_low.astype(jnp.float32), axis=(0, 1))
    act_one_grad = jnp.dot(
        patches(rim_rows(first_low.reshape(grid_shape)), crop_rim, crop_mid),
        flipped(conv_one),
        preferred_element_type=jnp.float32,
    ).reshape(flat_input.shape)
    field_part, gain_one_grad, shift_one_grad = norm_backward(
        act_one_grad * silu_slope(normed_one),
        centred_one,
        rstd_one,
        as_float(gain_one),
        onehot,
        counts,
    )
    input_grad = resid_grad + field_part
    res_grads = (
        lax.psum_scatter(conv_one_grad, ("band", "canvas"), scatter_dimension=0, tiled=True),
        lax.psum_scatter(conv_two_grad, ("band", "canvas"), scatter_dimension=0, tiled=True),
        lax.psum_scatter(gain_one_grad, ("band", "canvas"), scatter_dimension=0, tiled=True),
        lax.psum_scatter(shift_one_grad, ("band", "canvas"), scatter_dimension=0, tiled=True),
        lax.psum_scatter(bias_one_grad, ("band", "canvas"), scatter_dimension=0, tiled=True),
        lax.psum_scatter(gain_two_grad, ("band", "canvas"), scatter_dimension=0, tiled=True),
        lax.psum_scatter(shift_two_grad, ("band", "canvas"), scatter_dimension=0, tiled=True),
        lax.psum_scatter(bias_two_grad, ("band", "canvas"), scatter_dimension=0, tiled=True),
    )
    attn_grads = (
        lax.psum_scatter(query_w_grad, ("band", "canvas"), scatter_dimension=0, tiled=True),
        lax.psum_scatter(key_w_grad, ("band", "canvas"), scatter_dimension=0, tiled=True),
        lax.psum_scatter(value_w_grad, ("band", "canvas"), scatter_dimension=0, tiled=True),
        lax.psum_scatter(out_grad, ("band", "canvas"), scatter_dimension=0, tiled=True),
        lax.psum_scatter(query_add_grad, ("band", "canvas"), scatter_dimension=0, tiled=True),
        lax.psum_scatter(value_add_grad, ("band", "canvas"), scatter_dimension=0, tiled=True),
        lax.psum_scatter(out_add_grad, ("band", "canvas"), scatter_dimension=0, tiled=True),
        lax.psum_scatter(gain_three_grad, ("band", "canvas"), scatter_dimension=0, tiled=True),
        lax.psum_scatter(shift_three_grad, ("band", "canvas"), scatter_dimension=0, tiled=True),
    )
    return (
        output.reshape(grid_shape).astype(jnp.bfloat16),
        input_grad.reshape(grid_shape),
        res_grads[2],
        res_grads[3],
        res_grads[0],
        res_grads[4],
        res_grads[5],
        res_grads[6],
        res_grads[1],
        res_grads[7],
        attn_grads[7],
        attn_grads[8],
        attn_grads[0],
        attn_grads[4],
        attn_grads[1],
        attn_grads[2],
        attn_grads[5],
        attn_grads[3],
        attn_grads[6],
    )


MESH = pl.DeviceIdType.MESH
F32 = jnp.float32
LOW = jnp.bfloat16
STRIP = 16
LANES = 128
MEMBERS = 4
VECTORS = 11


def dot(a, b):
    return lax.dot_general(a, b, (((1,), (0,)), ((), ())), preferred_element_type=F32)


def dot_t(a, b):
    return lax.dot_general(a, b, (((1,), (1,)), ((), ())), preferred_element_type=F32)


def exact(a, b):
    return lax.dot_general(a, b, (((1,), (0,)), ((), ())), precision=HIGH, preferred_element_type=F32)


def remote(src, dst, send, recv, device):
    return pltpu.make_async_remote_copy(
        src_ref=src, dst_ref=dst, send_sem=send, recv_sem=recv, device_id=device, device_id_type=MESH
    )


def iota(shape, axis):
    return lax.broadcasted_iota(jnp.int32, shape, axis)


def loop(count, body):
    lax.fori_loop(0, count, lambda i, carry: (body(i), carry)[1], 0)


def at8(i, step):
    return pl.ds(pl.multiple_of(i * step, step), step)


def sigmoid(u):
    return 1.0 / (1.0 + jnp.exp(-u))


def strip_kernel(dims, names, *refs):
    r = types.SimpleNamespace(**dict(zip(names, refs)))
    height, bands, canvases, channels, band_rows = dims
    pixels = height * STRIP
    own_px = pixels // MEMBERS
    devices = bands * canvases
    groups = devices // MEMBERS
    shard = 9 * channels // devices
    block = shard * MEMBERS
    eighths = height // 8
    n_tiles = channels // LANES

    b = lax.axis_index("band")
    c = lax.axis_index("canvas")
    me = canvases * b + c
    q = b // 2
    xi = lax.rem(b, 2)
    k = 2 * xi + c
    z = b // 4
    y = lax.rem(q, 2)
    canvas = lax.rem(q, canvases)
    strip = q // canvases
    other = 1 - c
    bx = b + 1 - 2 * xi
    by = b + 2 - 4 * y
    k_sib = 2 * xi + other
    k_x = 2 * (1 - xi) + c
    k_diag = 2 * (1 - xi) + other
    sib, xdev, ydev = (b, other), (bx, c), (by, c)
    lines = groups // 2

    def zband(j):
        return lax.rem(b + 4 * j, bands)

    def zq(j):
        return lax.rem(z + j, lines)

    def lanes(i):
        return pl.ds(pl.multiple_of(i * LANES, LANES), LANES)

    barrier = pltpu.get_barrier_semaphore()

    def greet(i):
        @pl.when(i != me)
        def _():
            pl.semaphore_signal(barrier, inc=1, device_id=(i // canvases, lax.rem(i, canvases)), device_id_type=MESH)

    loop(devices, greet)
    pl.semaphore_wait(barrier, devices - 1)

    sends = []

    def start(copy):
        copy.start()
        sends.append(copy)
        return copy

    start(remote(r.crops.at[0], r.crop_in, r.s_crop.at[0], r.s_crop.at[1], sib))
    crop_copy = pltpu.make_async_copy(r.crops.at[0], r.crop_own, r.s_crop.at[2])
    crop_copy.start()

    def spread(src, dst, ssem, rsem):
        def one(i):
            s = i // MEMBERS
            kk = lax.rem(i, MEMBERS)
            tb = 2 * (s * canvases + c) + kk // 2
            tc = lax.rem(kk, 2)
            piece = src.at[0, :, pl.ds(pl.multiple_of(STRIP * s, STRIP), STRIP), lanes(kk)]
            place = dst.at[pl.ds(band_rows * b, band_rows)]
            mine = jnp.logical_and(tb == b, tc == c)

            @pl.when(mine)
            def _():
                pltpu.make_async_copy(piece, place, rsem).start()

            @pl.when(jnp.logical_not(mine))
            def _():
                remote(piece, place, ssem.at[i], rsem, (tb, tc)).start()

        loop(MEMBERS * (channels // LANES), one)

    def spread_sent(src, dst, ssem):
        def one(i):
            s = i // MEMBERS
            kk = lax.rem(i, MEMBERS)
            tb = 2 * (s * canvases + c) + kk // 2
            tc = lax.rem(kk, 2)
            piece = src.at[0, :, pl.ds(pl.multiple_of(STRIP * s, STRIP), STRIP), lanes(kk)]
            place = dst.at[pl.ds(band_rows * b, band_rows)]

            @pl.when(jnp.logical_not(jnp.logical_and(tb == b, tc == c)))
            def _():
                remote(piece, place, ssem.at[i], ssem.at[i], (tb, tc)).wait_send()

        loop(MEMBERS * (channels // LANES), one)

    def wait_local(ref, sem):
        pltpu.make_async_copy(ref, ref, sem).wait()

    spread(r.x, r.xs, r.s_xs, r.r_xs.at[0])

    vec_copy = pltpu.make_async_copy(r.vec, r.vecs.at[me], r.r_vec.at[0])
    vec_copy.start()

    def vec_send(i):
        @pl.when(i != me)
        def _():
            remote(
                r.vec, r.vecs.at[me], r.s_vec.at[i], r.r_vec.at[0],
                (i // canvases, lax.rem(i, canvases)),
            ).start()

    loop(devices, vec_send)

    def weight_first(w, wc, ssem, rsem):
        place = wc.at[pl.ds(pl.multiple_of(shard * me, 16), shard)]
        for kk in range(MEMBERS):
            piece = w.at[:, kk * LANES : (kk + 1) * LANES]

            @pl.when(k == kk)
            def _():
                pltpu.make_async_copy(piece, place, rsem.at[0]).start()

            @pl.when(k != kk)
            def _():
                remote(piece, place, ssem.at[kk], rsem.at[0], (2 * q + kk // 2, kk % 2)).start()

    def weight_first_sent(w, wc, ssem, rsem):
        place = wc.at[pl.ds(pl.multiple_of(shard * me, 16), shard)]
        for kk in range(MEMBERS):
            piece = w.at[:, kk * LANES : (kk + 1) * LANES]

            @pl.when(k != kk)
            def _():
                remote(piece, place, ssem.at[kk], rsem.at[0], (2 * q + kk // 2, kk % 2)).wait_send()

    def wblock(wc, group):
        return wc.at[pl.ds(pl.multiple_of(block * group, 16), block)]

    def weight_second(wc, ssem, rsem):
        own = wblock(wc, q)
        wait_local(own, rsem.at[0])
        for j in range(1, lines):
            start(remote(own, own, ssem.at[MEMBERS + j], rsem.at[j], (zband(j), c)))
        start(remote(own, own, ssem.at[MEMBERS], rsem.at[lines], ydev))

    def weight_third(wc, ssem, rsem):
        for j in range(1, lines):
            came = wblock(wc, 2 * zq(lines - j) + y)
            remote(came, came, ssem.at[0], rsem.at[j], ydev).wait_recv()
            start(remote(came, came, ssem.at[MEMBERS + lines + j - 1], rsem.at[lines + j], ydev))

    def weight_fourth(wc, ssem, rsem):
        for j in range(lines):
            came = wblock(wc, 2 * zq(lines - j) + 1 - y)
            remote(came, came, ssem.at[0], rsem.at[lines + j], ydev).wait_recv()

    weight_first(r.w1, r.w1c, r.s_w1, r.r_w1)
    weight_first(r.w2, r.w2c, r.s_w2, r.r_w2)
    for m, shard_ref in enumerate((r.wq, r.wk, r.wv, r.wo)):
        pltpu.make_async_copy(shard_ref, r.aw.at[k, q, 16 * m : 16 * m + 16], r.r_aw.at[0]).start()

    weight_second(r.w1c, r.s_w1, r.r_w1)
    spread(r.g, r.gs, r.s_gs, r.r_gs.at[0])

    crop_copy.wait()
    remote(r.crops.at[0], r.crop_in, r.s_crop.at[0], r.s_crop.at[1], sib).wait_recv()
    canvas_v = jnp.full((height, r.crop_own.shape[1]), canvas, jnp.int32)
    ids = jnp.where(canvas_v == c, r.crop_own[...], r.crop_in[...]).astype(F32)
    width = ids.shape[1]
    of_strip = iota((height, width), 1) == STRIP * strip
    id_col = jnp.sum(jnp.where(of_strip, ids, 0.0), axis=1, keepdims=True)
    pick = (iota((8, width), 1) == STRIP * strip).astype(LOW)
    id_row = lax.dot_general(pick, ids.astype(LOW), (((1,), (1,)), ((), ())), preferred_element_type=F32)
    same = (id_col == id_row[0:1, :]).astype(F32)
    r.same[...] = same
    r.inv_n[...] = 1.0 / jnp.maximum(
        exact(same, jnp.full((height, LANES), float(STRIP * STRIP), F32)), 1.0
    )
    row_i, row_j = iota((height, height), 0), iota((height, height), 1)
    r.below[...] = jnp.broadcast_to(
        jnp.sum(jnp.where(row_j == row_i + 1, same, 0.0), axis=1, keepdims=True), (height, LANES)
    )
    r.above[...] = jnp.broadcast_to(
        jnp.sum(jnp.where(row_j == row_i - 1, same, 0.0), axis=1, keepdims=True), (height, LANES)
    )
    own_rows = iota((own_px, height), 1) == iota((own_px, height), 0) // STRIP + own_px // STRIP * k
    own_ids = dot(own_rows.astype(LOW), ids.astype(LOW))
    own_col = jnp.sum(
        jnp.where(iota((own_px, width), 1) == STRIP * strip, own_ids, 0.0), axis=1, keepdims=True
    )
    r.id_own[...] = jnp.broadcast_to(own_col, (own_px, LANES))
    stretch = (iota((height, pixels), 1) // STRIP == iota((height, pixels), 0)).astype(LOW)
    r.id_all[...] = dot(id_row.astype(LOW), stretch)
    group_fold_mat = (iota((LANES, LANES), 0) // STRIP == iota((LANES, LANES), 1) // STRIP).astype(F32)
    r.fold[...] = group_fold_mat
    r.vg[...] = jnp.zeros(r.vg.shape, F32)
    wide = r.y.shape[1]
    for edge in (0, pixels + STRIP):
        r.y[edge : edge + STRIP, :] = jnp.zeros((STRIP, wide), F32)
        r.ebuf[edge : edge + STRIP, :] = jnp.zeros((STRIP, LANES), F32)

    wait_local(r.vecs, r.r_vec.at[0])
    per = LANES // (channels // devices)
    for tile in range(n_tiles):
        total = r.vecs[tile * per].astype(F32)
        for i in range(1, per):
            total = total + r.vecs[tile * per + i].astype(F32)
        r.vfull[:, tile * LANES : (tile + 1) * LANES] = total

    def mine_vec(row):
        return r.vfull[row : row + 1, lanes(k)]

    def fold(rows):
        return exact(exact(r.same[...], rows), r.fold[...])

    def row_sums(v):
        return jnp.sum(v.reshape(8, STRIP, LANES), axis=1)

    def spread_rows(ref, i):
        return jnp.broadcast_to(ref[at8(i, 8), :].reshape(8, 1, LANES), (8, STRIP, LANES)).reshape(LANES, LANES)

    def norm_stats(load, which):
        def body(i):
            v = load(i)
            r.t1[at8(i, 8), :] = row_sums(v)
            r.t2[at8(i, 8), :] = row_sums(v * v)

        loop(eighths, body)
        mean = fold(r.t1[...]) * r.inv_n[...]
        var = fold(r.t2[...]) * r.inv_n[...] - mean * mean
        r.mean[which] = mean
        r.rstd[which] = lax.rsqrt(var + EPS)

    def xhat_of(load, which, i):
        mean = spread_rows(r.mean.at[which], i)
        rstd = spread_rows(r.rstd.at[which], i)
        return (load(i) - mean) * rstd, rstd

    def norm_back(load_e, load_v, which, gain, gain_row, finish):
        def body(i):
            e = load_e(i)
            xh, _ = xhat_of(load_v, which, i)
            r.t1[at8(i, 8), :] = row_sums(e)
            r.t2[at8(i, 8), :] = row_sums(e * xh)

        loop(eighths, body)
        t1, t2 = r.t1[...], r.t2[...]
        r.vg[gain_row : gain_row + 1, lanes(k)] = jnp.sum(t2, axis=0, keepdims=True)
        r.vg[gain_row + 1 : gain_row + 2, lanes(k)] = jnp.sum(t1, axis=0, keepdims=True)
        r.m1[...] = fold(t1 * gain) * r.inv_n[...]
        r.m2[...] = fold(t2 * gain) * r.inv_n[...]

        def out(i):
            xh, rstd = xhat_of(load_v, which, i)
            finish(i, rstd * (load_e(i) * gain - spread_rows(r.m1, i) - xh * spread_rows(r.m2, i)))

        loop(eighths, out)

    def gather_start(buf, ssem, rsem):
        own = buf.at[:, lanes(k)]
        start(remote(own, own, ssem.at[1], rsem.at[1], xdev))
        start(remote(own, own, ssem.at[0], rsem.at[0], sib))

    def gather_relay(buf, ssem, rsem):
        came = buf.at[:, lanes(k_x)]
        remote(came, came, ssem.at[1], rsem.at[1], xdev).wait_recv()
        start(remote(came, came, ssem.at[2], rsem.at[2], sib))

    def gather_done(buf, ssem, rsem):
        came = buf.at[:, lanes(k_sib)]
        remote(came, came, ssem.at[0], rsem.at[0], sib).wait_recv()
        came = buf.at[:, lanes(k_diag)]
        remote(came, came, ssem.at[2], rsem.at[2], sib).wait_recv()

    def reduce_start(part, came, ssem, rsem):
        start(remote(part(k_diag), came.at[1], ssem.at[1], rsem.at[1], sib))
        start(remote(part(k_sib), came.at[0], ssem.at[0], rsem.at[0], sib))

    def reduce_relay(part, came, mix, add, ssem, rsem):
        remote(part(k_diag), came.at[1], ssem.at[1], rsem.at[1], sib).wait_recv()
        add(mix)
        start(remote(mix, came.at[2], ssem.at[2], rsem.at[2], xdev))

    def reduce_done(part, came, mix, ssem, rsem):
        remote(part(k_sib), came.at[0], ssem.at[0], rsem.at[0], sib).wait_recv()
        remote(mix, came.at[2], ssem.at[2], rsem.at[2], xdev).wait_recv()

    column = lax.rem(iota((LANES, LANES), 0), STRIP)
    not_first, not_last = column != 0, column != STRIP - 1

    def conv_wide(wc, wf):
        for t in range(9):
            wf[:, t * LANES : (t + 1) * LANES] = wc[t * channels : (t + 1) * channels, :]

    def conv_turned(wc, wt):
        for t in range(9):
            wt[t * LANES : (t + 1) * LANES, :] = wc[(8 - t) * channels : (9 - t) * channels, :].T

    def conv(act, wf, bias, out):
        def multiply(i):
            r.y[pl.ds(pl.multiple_of(STRIP + 256 * i, 16), 256), :] = dot(act[at8(i, 256), :], wf[...])

        loop(pixels // 256, multiply)

        def gather_taps(i):
            up = spread_rows(r.above, i)
            down = spread_rows(r.below, i)

            def tap(dr, dc):
                at = pl.multiple_of(LANES * i + STRIP * (1 + dr), 16)
                t = 3 * (dr + 1) + dc + 1
                return r.y[pl.ds(at, LANES), t * LANES : (t + 1) * LANES]

            def side(dc):
                return tap(0, dc) + up * tap(-1, dc) + down * tap(1, dc)

            left = jnp.where(not_first, pltpu.roll(side(-1), 1, 0), 0.0)
            right = jnp.where(not_last, pltpu.roll(side(1), LANES - 1, 0), 0.0)
            out(i, side(0) + left + right + bias)

        loop(eighths, gather_taps)

    def taps_of_e():
        def body(i):
            up = spread_rows(r.above, i)
            down = spread_rows(r.below, i)
            for dr in (-1, 0, 1):
                at = pl.multiple_of(LANES * i + STRIP * (1 + dr), 16)
                v = r.ebuf[pl.ds(at, LANES), :]
                if dr == -1:
                    v = v * up
                if dr == 1:
                    v = v * down
                t = 3 * (dr + 1)
                rows = at8(i, LANES)
                r.ecat[rows, t * LANES : (t + 1) * LANES] = jnp.where(
                    not_first, pltpu.roll(v, 1, 0), 0.0
                ).astype(LOW)
                r.ecat[rows, (t + 1) * LANES : (t + 2) * LANES] = v.astype(LOW)
                r.ecat[rows, (t + 2) * LANES : (t + 3) * LANES] = jnp.where(
                    not_last, pltpu.roll(v, LANES - 1, 0), 0.0
                ).astype(LOW)

        loop(eighths, body)

    def conv_back(wt, part):
        def body(i):
            part[at8(i, 256), :] = dot(r.ecat[at8(i, 256), :], wt[...]).astype(LOW)

        loop(pixels // 256, body)

    def weight_grad(act_t, dw):
        half = channels // 2
        for i in range(2):
            wide_out = dot(act_t[i * half : (i + 1) * half, :], r.ecat[...])
            for t in range(9):
                at = (8 - t) * channels + i * half
                dw[at : at + half, :] = wide_out[:, t * LANES : (t + 1) * LANES].astype(LOW)

    def grad_first(dw, ry, ssem, rsem):
        for j in range(lines):
            zz = zq(j + 1)
            start(remote(wblock(dw, 2 * zz + 1 - y), ry.at[j], ssem.at[j], rsem.at[j], ydev))

    def grad_second(dw, ry, rz, sy, ssem, rsem):
        for j in range(lines):
            zz = zq(j + 1)
            remote(wblock(dw, 2 * zz + 1 - y), ry.at[j], ssem.at[j], rsem.at[j], ydev).wait_recv()

            def add(i):
                at = pl.multiple_of(block * (2 * zz + y) + shard * i, 16)
                sy[j, at8(i, shard), :] = (
                    dw[pl.ds(at, shard), :].astype(F32) + ry[j, at8(i, shard), :].astype(F32)
                ).astype(LOW)

            loop(MEMBERS, add)
            if j + 1 < lines:
                start(remote(sy.at[j], rz.at[j], ssem.at[lines + j], rsem.at[lines + j], (zband(j + 1), c)))

    def grad_third(sy, rz, fx, out, ssem, rsem):
        for j in range(lines - 1):
            remote(sy.at[j], rz.at[j], ssem.at[lines + j], rsem.at[lines + j], (zband(j + 1), c)).wait_recv()

        def add(i):
            total = sy[lines - 1, at8(i, shard), :].astype(F32)
            for j in range(lines - 1):
                total = total + rz[j, at8(i, shard), :].astype(F32)
            fx[at8(i, shard), :] = total

        loop(MEMBERS, add)
        for kk in range(MEMBERS):
            piece = fx.at[kk * shard : (kk + 1) * shard]
            place = out.at[:, lanes(k)]

            @pl.when(k == kk)
            def _():
                pltpu.make_async_copy(piece, place, rsem.at[2 * lines]).start()

            @pl.when(k != kk)
            def _():
                remote(
                    piece, place, ssem.at[2 * lines + kk], rsem.at[2 * lines], (2 * q + kk // 2, kk % 2)
                ).start()

    def grad_done(fx, out, ssem, rsem):
        wait_local(out, rsem.at[2 * lines])
        for kk in range(MEMBERS):
            piece = fx.at[kk * shard : (kk + 1) * shard]

            @pl.when(k != kk)
            def _():
                remote(
                    piece, out.at[:, lanes(k)], ssem.at[2 * lines + kk], rsem.at[2 * lines],
                    (2 * q + kk // 2, kk % 2),
                ).wait_send()

    wait_local(r.xs, r.r_xs.at[0])

    def load_x(i):
        return r.xs[at8(i, 8)].reshape(LANES, LANES).astype(F32)

    norm_stats(load_x, 0)
    gain1, shift1 = mine_vec(0), mine_vec(1)

    def act1(i):
        xh, _ = xhat_of(load_x, 0, i)
        u = xh * gain1 + shift1
        r.h1[at8(i, LANES), lanes(k)] = (u * sigmoid(u)).astype(LOW)

    loop(eighths, act1)
    gather_start(r.h1, r.s_h1, r.r_h1)
    weight_third(r.w1c, r.s_w1, r.r_w1)
    weight_second(r.w2c, r.s_w2, r.r_w2)
    gather_relay(r.h1, r.s_h1, r.r_h1)
    wait_local(r.gs, r.r_gs.at[0])

    def low_g(i):
        r.gall[at8(i, LANES), lanes(k)] = r.gs[at8(i, 8)].reshape(LANES, LANES)

    loop(eighths, low_g)

    own_aw = r.aw.at[k, q]
    wait_local(own_aw, r.r_aw.at[0])
    for j in range(1, lines):
        start(remote(own_aw, own_aw, r.s_aw.at[j], r.r_aw.at[j], (zband(j), c)))
    start(remote(own_aw, own_aw, r.s_aw.at[0], r.r_aw.at[lines], ydev))

    weight_fourth(r.w1c, r.s_w1, r.r_w1)
    conv_wide(r.w1c, r.wf)
    gather_done(r.h1, r.s_h1, r.r_h1)

    def put_c1(i, v):
        r.c1[at8(i, LANES), :] = v

    conv(r.h1, r.wf, mine_vec(2), put_c1)

    def load_c1(i):
        return r.c1[at8(i, LANES), :]

    norm_stats(load_c1, 1)
    gain2, shift2 = mine_vec(3), mine_vec(4)

    def act2(i):
        xh, _ = xhat_of(load_c1, 1, i)
        u = xh * gain2 + shift2
        r.h2[at8(i, LANES), lanes(k)] = (u * sigmoid(u)).astype(LOW)

    loop(eighths, act2)
    gather_start(r.h2, r.s_h2, r.r_h2)
    weight_third(r.w2c, r.s_w2, r.r_w2)
    gather_relay(r.h2, r.s_h2, r.r_h2)
    gather_start(r.gall, r.s_ga, r.r_ga)
    for j in range(1, lines):
        came = r.aw.at[k, 2 * zq(lines - j) + y]
        remote(came, came, r.s_aw.at[0], r.r_aw.at[j], ydev).wait_recv()
        start(remote(came, came, r.s_aw.at[lines + j], r.r_aw.at[lines + j], ydev))
    weight_fourth(r.w2c, r.s_w2, r.r_w2)
    conv_wide(r.w2c, r.wf)
    gather_done(r.h2, r.s_h2, r.r_h2)

    def put_r(i, v):
        total = v + load_x(i)
        r.res[at8(i, LANES), :] = total
        r.resl[at8(i, LANES), :] = total.astype(LOW)

    conv(r.h2, r.wf, mine_vec(5), put_r)

    def load_r(i):
        return r.res[at8(i, LANES), :]

    norm_stats(load_r, 2)
    gain3, shift3 = mine_vec(6), mine_vec(7)

    def act3(i):
        xh, _ = xhat_of(load_r, 2, i)
        r.hn[at8(i, LANES), lanes(k)] = (xh * gain3 + shift3).astype(LOW)

    loop(eighths, act3)
    gather_start(r.hn, r.s_hn, r.r_hn)

    def rows_of(i):
        return pl.ds(pl.multiple_of(own_px * i, own_px), own_px)

    def swap_start(src, dst, ssem, rsem, to_lanes):
        for kk in range(MEMBERS):
            if to_lanes:
                piece, place = src.at[rows_of(kk)], dst.at[:, lanes(k)]
            else:
                piece, place = src.at[:, kk * LANES : (kk + 1) * LANES], dst.at[rows_of(k)]

            @pl.when(k == kk)
            def _():
                pltpu.make_async_copy(piece, place, rsem.at[0]).start()

            @pl.when(k != kk)
            def _():
                remote(piece, place, ssem.at[kk], rsem.at[0], (2 * q + kk // 2, kk % 2)).start()

    def swap_sent(src, dst, ssem, rsem, to_lanes):
        for kk in range(MEMBERS):
            if to_lanes:
                piece, place = src.at[rows_of(kk)], dst.at[:, lanes(k)]
            else:
                piece, place = src.at[:, kk * LANES : (kk + 1) * LANES], dst.at[rows_of(k)]

            @pl.when(k != kk)
            def _():
                remote(piece, place, ssem.at[kk], rsem.at[0], (2 * q + kk // 2, kk % 2)).wait_send()

    for j in range(lines):
        came = r.aw.at[k, 2 * zq(lines - j) + 1 - y]
        remote(came, came, r.s_aw.at[0], r.r_aw.at[lines + j], ydev).wait_recv()
    own = r.aw.at[k]
    start(remote(own, own, r.s_aw.at[2 * lines + 1], r.r_aw.at[2 * lines + 1], xdev))
    start(remote(own, own, r.s_aw.at[2 * lines], r.r_aw.at[2 * lines], sib))
    gather_relay(r.hn, r.s_hn, r.r_hn)
    gather_relay(r.gall, r.s_ga, r.r_ga)
    swap_start(r.resl, r.rown, r.s_rs, r.r_rs, True)
    conv_turned(r.w2c, r.wt2)
    conv_turned(r.w1c, r.wt1)
    came = r.aw.at[k_x]
    remote(came, came, r.s_aw.at[0], r.r_aw.at[2 * lines + 1], xdev).wait_recv()
    start(remote(came, came, r.s_aw.at[2 * lines + 2], r.r_aw.at[2 * lines + 2], sib))
    r.h2t[...] = r.h2[...].T
    r.h1t[...] = r.h1[...].T
    gather_done(r.hn, r.s_hn, r.r_hn)
    gather_done(r.gall, r.s_ga, r.r_ga)
    came = r.aw.at[k_sib]
    remote(came, came, r.s_aw.at[0], r.r_aw.at[2 * lines], sib).wait_recv()
    came = r.aw.at[k_diag]
    remote(came, came, r.s_aw.at[0], r.r_aw.at[2 * lines + 2], sib).wait_recv()
    for m in range(4):
        for gq in range(groups):
            for kk in range(MEMBERS):
                at = 16 * (MEMBERS * gq + kk)
                r.wa[m, at : at + 16, :] = r.aw[kk, gq, 16 * m : 16 * m + 16, :]

    scale = float(channels) ** -0.5
    chunk = 128
    own_base = own_px * k

    def project(i):
        rows = at8(i, 256)
        hn = r.hn[rows, :]
        r.ka[rows, :] = dot(hn, r.wa[1]).astype(LOW)
        r.va[rows, :] = (dot(hn, r.wa[2]) + r.vfull[9:10, :]).astype(LOW)
        r.qa[rows, :] = (dot(hn, r.wa[0]) + r.vfull[8:9, :]).astype(LOW)
        r.goa[rows, :] = dot_t(r.gall[rows, :], r.wa[3]).astype(LOW)

    loop(pixels // 256, project)

    def mask_of(i):
        return r.id_own[at8(i, chunk), 0:1] == r.id_all[0:1, :]

    def own_chunk(i):
        return pl.ds(pl.multiple_of(own_base + chunk * i, chunk), chunk)

    def attend(i):
        mask = mask_of(i)
        s = jnp.where(mask, dot_t(r.qa[own_chunk(i), :], r.ka[...]) * scale, NEG)
        top = jnp.max(s, axis=1, keepdims=True)
        p = jnp.where(mask, jnp.exp(s - top), 0.0)
        total = jnp.sum(p, axis=1, keepdims=True)
        p = p / total
        r.prob[at8(i, chunk), :] = p
        o = dot(p.astype(LOW), r.va[...])
        r.a[at8(i, chunk), :] = o.astype(LOW)
        delta = jnp.sum(r.goa[own_chunk(i), :].astype(F32) * o, axis=1, keepdims=True)
        lane = iota((chunk, LANES), 1)
        r.ld[at8(i, chunk), :] = jnp.where(lane == 0, top + jnp.log(total), delta)

    loop(own_px // chunk, attend)
    r.ldt[...] = r.ld[...].T[0:8, :]
    r.ldall[k] = r.ldt[...]
    for kk in range(MEMBERS):

        @pl.when(k != kk)
        def _():
            remote(
                r.ldt, r.ldall.at[k], r.s_ld.at[kk], r.r_ld.at[k], (2 * q + kk // 2, kk % 2)
            ).start()

    def query_back(i):
        dp = dot_t(r.goa[own_chunk(i), :], r.va[...])
        ds = (r.prob[at8(i, chunk), :] * (dp - r.ld[at8(i, chunk), 1:2])).astype(LOW)
        r.dq[at8(i, chunk), :] = (dot(ds, r.ka[...]) * scale).astype(LOW)

    loop(own_px // chunk, query_back)

    for kk in range(MEMBERS):

        @pl.when(k != kk)
        def _():
            remote(
                r.ldt, r.ldall.at[kk], r.s_ld.at[kk], r.r_ld.at[kk], (2 * q + kk // 2, kk % 2)
            ).wait_recv()

    def key_back(i):
        mask = mask_of(i)
        lse = jnp.concatenate([r.ldall[j, 0:1, :] for j in range(MEMBERS)], axis=1)
        delta = jnp.concatenate([r.ldall[j, 1:2, :] for j in range(MEMBERS)], axis=1)
        s = dot_t(r.ka[own_chunk(i), :], r.qa[...]) * scale - lse
        p = jnp.where(mask, jnp.exp(jnp.where(mask, s, 0.0)), 0.0)
        r.dv[at8(i, chunk), :] = dot(p.astype(LOW), r.goa[...]).astype(LOW)
        dp = dot_t(r.va[own_chunk(i), :], r.goa[...])
        ds = (p * (dp - delta)).astype(LOW)
        r.dk[at8(i, chunk), :] = (dot(ds, r.qa[...]) * scale).astype(LOW)

    loop(own_px // chunk, key_back)

    r.dhn[...] = (
        dot_t(r.dq[...], r.wa[0]) + dot_t(r.dk[...], r.wa[1]) + dot_t(r.dv[...], r.wa[2])
    ).astype(LOW)
    swap_start(r.dhn, r.dhs, r.s_dh, r.r_dh, False)

    r.vg[8:9, :] = jnp.sum(r.dq[...].astype(F32), axis=0, keepdims=True)
    r.vg[9:10, :] = jnp.sum(r.dv[...].astype(F32), axis=0, keepdims=True)
    own_all = rows_of(k)
    r.hnt[...] = r.hn[own_all, :].T
    r.at[...] = r.a[...].T
    for m, (left, right) in enumerate(((r.hnt, r.dq), (r.hnt, r.dk), (r.hnt, r.dv), (r.at, None))):
        grad = dot(left[...], r.gall[own_all, :] if right is None else right[...]).astype(LOW)
        for gq in range(groups):
            for kk in range(MEMBERS):
                at = 16 * (MEMBERS * gq + kk)
                r.da[kk, gq, 16 * m : 16 * m + 16, :] = grad[at : at + 16, :]

    def attn_part(i):
        return r.da.at[i]

    reduce_start(attn_part, r.dac, r.s_da, r.r_da)

    wait_local(r.rown, r.r_rs.at[0])
    r.outl[...] = (
        (r.rown[...].astype(F32) + dot(r.a[...], r.wa[3]) + r.vfull[10:11, :])
        .astype(LOW)
        .reshape(r.outl.shape)
    )
    bands_of_mine = own_px // STRIP // band_rows

    def out_copy(i, local):
        piece = r.outl.at[i * band_rows : (i + 1) * band_rows]
        place = r.out.at[0, :, pl.ds(pl.multiple_of(STRIP * strip, STRIP), STRIP), :]
        tb = bands_of_mine * k + i
        if local:
            return pltpu.make_async_copy(piece, place, r.r_out.at[0])
        return remote(piece, place, r.s_out.at[i], r.r_out.at[0], (tb, canvas))

    def out_is_mine(i):
        return jnp.logical_and(bands_of_mine * k + i == b, canvas == c)

    for i in range(bands_of_mine):

        @pl.when(out_is_mine(i))
        def _():
            out_copy(i, True).start()

        @pl.when(jnp.logical_not(out_is_mine(i)))
        def _():
            out_copy(i, False).start()

    wait_local(r.dhs, r.r_dh.at[0])

    def load_dhn(i):
        return r.dhs[at8(i, LANES), :].astype(F32)

    def padded(i):
        return pl.ds(pl.multiple_of(LANES * i + STRIP, 16), LANES)

    def put_dr(i, v):
        total = v + r.gs[at8(i, 8)].reshape(LANES, LANES).astype(F32)
        r.dres[at8(i, LANES), :] = total
        r.ebuf[padded(i), :] = total.astype(LOW).astype(F32)

    norm_back(load_dhn, load_r, 2, gain3, 6, put_dr)

    def bias_grad(row, load):
        def body(i):
            r.t1[at8(i, 8), :] = row_sums(load(i))

        loop(eighths, body)
        r.vg[row : row + 1, lanes(k)] = jnp.sum(r.t1[...], axis=0, keepdims=True)

    def load_e(i):
        return r.ebuf[padded(i), :]

    taps_of_e()
    conv_back(r.wt2, r.part2)

    def conv_part(ref):
        return lambda i: ref.at[:, lanes(i)]

    def adder(part, came):
        def add(mix):
            def body(i):
                rows = at8(i, LANES)
                mix[rows, :] = (
                    part[rows, lanes(k_x)].astype(F32) + came[1, rows, :].astype(F32)
                ).astype(LOW)

            loop(eighths, body)

        return add

    reduce_start(conv_part(r.part2), r.came2, r.s_p2, r.r_p2)
    bias_grad(5, load_e)
    reduce_relay(
        conv_part(r.part2), r.came2, r.mix2, adder(r.part2, r.came2), r.s_p2, r.r_p2
    )
    weight_grad(r.h2t, r.dw2)
    grad_first(r.dw2, r.ry2, r.s_g2, r.r_g2)

    def attn_add(mix):
        def body(i):
            mix[i] = (r.da[k_x, i].astype(F32) + r.dac[1, i].astype(F32)).astype(LOW)

        loop(groups, body)

    reduce_relay(attn_part, r.dac, r.damix, attn_add, r.s_da, r.r_da)
    bias_grad(10, lambda i: r.gs[at8(i, 8)].reshape(LANES, LANES).astype(F32))
    reduce_done(conv_part(r.part2), r.came2, r.mix2, r.s_p2, r.r_p2)

    def summed(part, came):
        def load(i):
            rows = at8(i, LANES)
            return (
                part[rows, lanes(k)].astype(F32)
                + came[0, rows, :].astype(F32)
                + came[2, rows, :].astype(F32)
            )

        return load

    def slope(load_v, which, gain, shift, load_dh):
        def body(i):
            xh, _ = xhat_of(load_v, which, i)
            u = xh * gain + shift
            s = sigmoid(u)
            r.du[at8(i, LANES), :] = load_dh(i) * (s * (1.0 + u * (1.0 - s)))

        loop(eighths, body)

    def load_du(i):
        return r.du[at8(i, LANES), :]

    def put_e1(i, v):
        r.ebuf[padded(i), :] = v.astype(LOW).astype(F32)

    slope(load_c1, 1, gain2, shift2, summed(r.part2, r.came2))
    norm_back(load_du, load_c1, 1, gain2, 3, put_e1)
    taps_of_e()
    conv_back(r.wt1, r.part1)
    reduce_start(conv_part(r.part1), r.came1, r.s_p1, r.r_p1)
    bias_grad(2, load_e)
    reduce_relay(
        conv_part(r.part1), r.came1, r.mix1, adder(r.part1, r.came1), r.s_p1, r.r_p1
    )
    weight_grad(r.h1t, r.dw1)
    grad_first(r.dw1, r.ry1, r.s_g1, r.r_g1)

    reduce_done(attn_part, r.dac, r.damix, r.s_da, r.r_da)

    def attn_sum(i):
        r.das[i] = (
            r.da[k, i].astype(F32) + r.dac[0, i].astype(F32) + r.dac[2, i].astype(F32)
        ).astype(LOW)

    loop(groups, attn_sum)
    for j in range(lines):
        start(
            remote(r.das.at[2 * zq(j + 1) + 1 - y], r.ay.at[j], r.s_ag.at[j], r.r_ag.at[j], ydev)
        )
    reduce_done(conv_part(r.part1), r.came1, r.mix1, r.s_p1, r.r_p1)

    slope(load_x, 0, gain1, shift1, summed(r.part1, r.came1))

    def put_dx(i, v):
        total = v + r.dres[at8(i, LANES), :]
        r.dxs[at8(i, 8)] = total.astype(LOW).reshape(8, STRIP, LANES)

    norm_back(load_du, load_x, 0, gain1, 0, put_dx)

    def dx_copy(i, local):
        piece = r.dxs.at[pl.ds(band_rows * i, band_rows)]
        place = r.dxi.at[:, pl.ds(pl.multiple_of(STRIP * strip, STRIP), STRIP), lanes(k)]
        if local:
            return pltpu.make_async_copy(piece, place, r.r_dx.at[0])
        return remote(piece, place, r.s_dx.at[i], r.r_dx.at[0], (i, canvas))

    def dx_send(i):
        mine = jnp.logical_and(i == b, canvas == c)

        @pl.when(mine)
        def _():
            dx_copy(i, True).start()

        @pl.when(jnp.logical_not(mine))
        def _():
            dx_copy(i, False).start()

    loop(bands, dx_send)
    r.vgin[me] = r.vg[:, lanes(me // per)]

    def vg_copy(i):
        return remote(
            r.vg.at[:, lanes(i // per)], r.vgin.at[me], r.s_vg.at[i], r.r_vg.at[me],
            (i // canvases, lax.rem(i, canvases)),
        )

    def vg_send(i):
        @pl.when(i != me)
        def _():
            vg_copy(i).start()

    loop(devices, vg_send)

    grad_second(r.dw2, r.ry2, r.rz2, r.sy2, r.s_g2, r.r_g2)
    for j in range(lines):
        zz = zq(j + 1)
        remote(r.das.at[2 * zz + 1 - y], r.ay.at[j], r.s_ag.at[j], r.r_ag.at[j], ydev).wait_recv()
        r.asum[j] = (r.das[2 * zz + y].astype(F32) + r.ay[j].astype(F32)).astype(LOW)
        if j + 1 < lines:
            start(
                remote(
                    r.asum.at[j], r.az.at[j], r.s_ag.at[lines + j], r.r_ag.at[lines + j],
                    (zband(j + 1), c),
                )
            )
    grad_second(r.dw1, r.ry1, r.rz1, r.sy1, r.s_g1, r.r_g1)
    grad_third(r.sy2, r.rz2, r.fx2, r.dw2out, r.s_g2, r.r_g2)

    wait_local(r.dxi, r.r_dx.at[0])
    r.dx[...] = r.dxi[...].astype(F32)[None]

    total = r.asum[lines - 1].astype(F32)
    for j in range(lines - 1):
        remote(
            r.asum.at[j], r.az.at[j], r.s_ag.at[lines + j], r.r_ag.at[lines + j], (zband(j + 1), c)
        ).wait_recv()
        total = total + r.az[j].astype(F32)
    for m, ref in enumerate((r.dwq, r.dwk, r.dwv, r.dwo)):
        ref[...] = total[16 * m : 16 * m + 16, :]

    def vg_wait(i):
        @pl.when(i != me)
        def _():
            remote(
                r.vg.at[:, lanes(i // per)], r.vgin.at[i], r.s_vg.at[i], r.r_vg.at[i],
                (i // canvases, lax.rem(i, canvases)),
            ).wait()

    loop(devices, vg_wait)
    total = r.vgin[0]
    for i in range(1, devices):
        total = total + r.vgin[i]
    piece = LANES // per
    turn = (iota((LANES, LANES), 0) == iota((LANES, LANES), 1) + piece * lax.rem(me, per)).astype(F32)
    r.dvec[...] = exact(total, turn)

    grad_third(r.sy1, r.rz1, r.fx1, r.dw1out, r.s_g1, r.r_g1)
    wait_local(r.out, r.r_out.at[0])
    grad_done(r.fx2, r.dw2out, r.s_g2, r.r_g2)
    grad_done(r.fx1, r.dw1out, r.s_g1, r.r_g1)

    for copy in sends:
        copy.wait_send()
    spread_sent(r.x, r.xs, r.s_xs)
    spread_sent(r.g, r.gs, r.s_gs)

    def vec_sent(i):
        @pl.when(i != me)
        def _():
            remote(
                r.vec, r.vecs.at[me], r.s_vec.at[i], r.r_vec.at[0],
                (i // canvases, lax.rem(i, canvases)),
            ).wait_send()

    loop(devices, vec_sent)
    weight_first_sent(r.w1, r.w1c, r.s_w1, r.r_w1)
    weight_first_sent(r.w2, r.w2c, r.s_w2, r.r_w2)
    swap_sent(r.resl, r.rown, r.s_rs, r.r_rs, True)
    swap_sent(r.dhn, r.dhs, r.s_dh, r.r_dh, False)
    for kk in range(MEMBERS):

        @pl.when(k != kk)
        def _():
            remote(
                r.ldt, r.ldall.at[k], r.s_ld.at[kk], r.r_ld.at[k], (2 * q + kk // 2, kk % 2)
            ).wait_send()

    for i in range(bands_of_mine):

        @pl.when(jnp.logical_not(out_is_mine(i)))
        def _():
            out_copy(i, False).wait_send()

    def dx_sent(i):
        @pl.when(jnp.logical_not(jnp.logical_and(i == b, canvas == c)))
        def _():
            dx_copy(i, False).wait_send()

    loop(bands, dx_sent)


def strips_on_device(dims, *args):
    height, bands, canvases, channels, band_rows = dims
    (
        inputs, crop_ids, cotangent, norm1_gain, norm1_shift, conv1_weight, conv1_bias, norm2_gain,
        norm2_shift, conv2_weight, conv2_bias, norm3_gain, norm3_shift, query_weight, query_bias,
        key_weight, value_weight, value_bias, out_weight, out_bias,
    ) = args
    width = inputs.shape[2]
    devices = bands * canvases
    own = channels // devices
    per = LANES // own
    pixels = height * STRIP
    own_px = pixels // MEMBERS
    groups = devices // MEMBERS
    lines = groups // 2
    shard = 9 * channels // devices
    block = MEMBERS * shard
    me = canvases * lax.axis_index("band") + lax.axis_index("canvas")
    stacked = jnp.stack(
        [
            norm1_gain, norm1_shift, conv1_bias, norm2_gain, norm2_shift, conv2_bias, norm3_gain,
            norm3_shift, query_bias, value_bias, out_bias,
        ]
    )
    stacked = jnp.pad(stacked, ((0, 16 - VECTORS), (0, 0)))
    at_lane = jnp.arange(LANES, dtype=jnp.int32)[None, :] // own == lax.rem(me, per)
    vec = jnp.where(at_lane, jnp.tile(stacked, (1, per)), jnp.zeros((), LOW))

    hbm = pl.BlockSpec(memory_space=pl.ANY)
    vmem = pl.BlockSpec(memory_space=pltpu.VMEM)
    operands = dict(
        x=inputs, crops=crop_ids, g=cotangent, w1=conv1_weight, w2=conv2_weight,
        wq=query_weight, wk=key_weight, wv=value_weight, wo=out_weight, vec=vec,
    )
    grid = (1, band_rows, width, channels)
    outs = dict(
        out=(grid, LOW, hbm),
        dx=(grid, F32, vmem),
        dw1out=((shard, channels), F32, hbm),
        dw2out=((shard, channels), F32, hbm),
        dwq=((own, channels), F32, vmem),
        dwk=((own, channels), F32, vmem),
        dwv=((own, channels), F32, vmem),
        dwo=((own, channels), F32, vmem),
        dvec=((16, LANES), F32, vmem),
    )
    nine = 9 * LANES
    buffers = dict(
        crop_in=((height, width), jnp.int32),
        crop_own=((height, width), jnp.int32),
        xs=((height, STRIP, LANES), LOW),
        gs=((height, STRIP, LANES), LOW),
        vecs=((devices, 16, LANES), LOW),
        vfull=((16, channels), F32),
        w1c=((9 * channels, LANES), LOW),
        w2c=((9 * channels, LANES), LOW),
        wf=((channels, nine), LOW),
        wt1=((nine, channels), LOW),
        wt2=((nine, channels), LOW),
        aw=((MEMBERS, groups, 64, channels), LOW),
        wa=((4, channels, channels), LOW),
        same=((height, height), F32),
        inv_n=((height, LANES), F32),
        above=((height, LANES), F32),
        below=((height, LANES), F32),
        id_own=((own_px, LANES), F32),
        id_all=((8, pixels), F32),
        fold=((LANES, LANES), F32),
        t1=((height, LANES), F32),
        t2=((height, LANES), F32),
        m1=((height, LANES), F32),
        m2=((height, LANES), F32),
        mean=((3, height, LANES), F32),
        rstd=((3, height, LANES), F32),
        y=((pixels + 2 * STRIP, nine), F32),
        ebuf=((pixels + 2 * STRIP, LANES), F32),
        ecat=((pixels, nine), LOW),
        h1=((pixels, channels), LOW),
        h2=((pixels, channels), LOW),
        hn=((pixels, channels), LOW),
        gall=((pixels, channels), LOW),
        h1t=((channels, pixels), LOW),
        h2t=((channels, pixels), LOW),
        c1=((pixels, LANES), F32),
        res=((pixels, LANES), F32),
        resl=((pixels, LANES), LOW),
        rown=((own_px, channels), LOW),
        qa=((pixels, channels), LOW),
        ka=((pixels, channels), LOW),
        va=((pixels, channels), LOW),
        goa=((pixels, channels), LOW),
        prob=((own_px, pixels), F32),
        a=((own_px, channels), LOW),
        ld=((own_px, LANES), F32),
        ldt=((8, own_px), F32),
        ldall=((MEMBERS, 8, own_px), F32),
        dq=((own_px, channels), LOW),
        dk=((own_px, channels), LOW),
        dv=((own_px, channels), LOW),
        dhn=((own_px, channels), LOW),
        dhs=((pixels, LANES), LOW),
        hnt=((channels, own_px), LOW),
        at=((channels, own_px), LOW),
        outl=((own_px // STRIP, STRIP, channels), LOW),
        da=((MEMBERS, groups, 64, channels), LOW),
        dac=((3, groups, 64, channels), LOW),
        damix=((groups, 64, channels), LOW),
        das=((groups, 64, channels), LOW),
        ay=((lines, 64, channels), LOW),
        asum=((lines, 64, channels), LOW),
        az=((lines - 1, 64, channels), LOW),
        dres=((pixels, LANES), F32),
        du=((pixels, LANES), F32),
        part2=((pixels, channels), LOW),
        came2=((3, pixels, LANES), LOW),
        mix2=((pixels, LANES), LOW),
        part1=((pixels, channels), LOW),
        came1=((3, pixels, LANES), LOW),
        mix1=((pixels, LANES), LOW),
        dw1=((9 * channels, LANES), LOW),
        dw2=((9 * channels, LANES), LOW),
        ry1=((lines, block, LANES), LOW),
        ry2=((lines, block, LANES), LOW),
        sy1=((lines, block, LANES), LOW),
        sy2=((lines, block, LANES), LOW),
        rz1=((lines - 1, block, LANES), LOW),
        rz2=((lines - 1, block, LANES), LOW),
        fx1=((block, LANES), F32),
        fx2=((block, LANES), F32),
        dxs=((height, STRIP, LANES), LOW),
        dxi=((band_rows, width, channels), LOW),
        vg=((16, channels), F32),
        vgin=((devices, 16, LANES), F32),
    )
    n_spread = MEMBERS * (channels // LANES)
    n_w = MEMBERS + 2 * lines
    semaphores = dict(
        s_crop=3, s_xs=n_spread, r_xs=1, s_gs=n_spread, r_gs=1, s_vec=devices, r_vec=1,
        s_w1=n_w, r_w1=n_w, s_w2=n_w, r_w2=n_w, s_aw=2 * lines + 3, r_aw=2 * lines + 3,
        s_h1=3, r_h1=3, s_h2=3, r_h2=3, s_hn=3, r_hn=3, s_ga=3, r_ga=3,
        s_rs=4, r_rs=1, s_ld=4, r_ld=4, s_dh=4, r_dh=1, s_da=3, r_da=3,
        s_out=4, r_out=1, s_p2=3, r_p2=3, s_p1=3, r_p1=3,
        s_g1=2 * lines + 4, r_g1=2 * lines + 1, s_g2=2 * lines + 4, r_g2=2 * lines + 1,
        s_ag=2 * lines, r_ag=2 * lines, s_dx=bands, r_dx=1, s_vg=devices, r_vg=devices,
    )
    names = (*operands, *outs, *buffers, *semaphores)
    results = pl.pallas_call(
        functools.partial(strip_kernel, dims, names),
        out_shape=[jax.ShapeDtypeStruct(shape, kind) for shape, kind, _ in outs.values()],
        in_specs=[hbm] * len(operands),
        out_specs=[spec for _, _, spec in outs.values()],
        scratch_shapes=[pltpu.VMEM(shape, kind) for shape, kind in buffers.values()]
        + [pltpu.SemaphoreType.DMA((count,)) for count in semaphores.values()],
        compiler_params=pltpu.CompilerParams(
            collective_id=0, has_side_effects=True, vmem_limit_bytes=60 * 1024 * 1024
        ),
    )(*operands.values())
    out, dx, dw1, dw2, dwq, dwk, dwv, dwo, dvec = results
    v = [dvec[i, :own] for i in range(VECTORS)]
    return (
        out, dx, v[0], v[1], dw1, v[2], v[3], v[4], dw2, v[5], v[6], v[7], dwq, v[8], dwk, dwv, v[9], dwo, v[10],
    )


def solution(mesh):
    sharded = P(("band", "canvas"))
    rows = P(("band", "canvas"), None)
    field = P("canvas", "band", None, None)
    placed = (
        field, P("canvas", None, None), field, sharded, sharded, rows, sharded, sharded, sharded, rows,
        sharded, sharded, sharded, rows, sharded, rows, rows, sharded, rows, sharded,
    )
    out_placed = (
        field, field, sharded, sharded, rows, sharded, sharded, sharded, rows, sharded, sharded, sharded,
        rows, sharded, rows, rows, sharded, rows, sharded,
    )
    bands, canvases = mesh.shape["band"], mesh.shape["canvas"]

    def step(*args):
        _, height, width, channels = args[0].shape
        fits = (
            canvases == 2
            and width // STRIP * canvases * MEMBERS == bands * canvases
            and channels == MEMBERS * LANES
            and channels % (bands * canvases) == 0
            and height % bands == 0
            and height * STRIP == 1024
            and bands % 4 == 0
            and height // bands == height // MEMBERS // 4
        )
        body = on_device
        if fits:
            body = functools.partial(strips_on_device, (height, bands, canvases, channels, height // bands))
        return jax.shard_map(body, mesh=mesh, in_specs=placed, out_specs=out_placed, check_vma=False)(*args)

    return step
```

profile of v0, /device:TPU:25, one launch (start us, length us, event | category | flops | bytes accessed | tf_op | source)
XLA Modules:
  0.0 188.7 jit_solution(10559424161472456790)
XLA Ops:
  0.7 0.0 copy-start.14
  0.7 0.0 copy-start.15
  0.8 0.5 copy-done.14
  1.3 0.0 copy-done.15
  1.3 0.0 copy-done.16
  1.4 0.0 copy-done.17
  1.4 0.0 copy-done.10
  1.4 0.0 copy-done.11
  1.4 0.0 copy-done.12
  1.4 0.0 copy-done.13
  1.4 0.0 copy-done.7
  1.5 0.0 copy-done.8
  1.5 0.0 copy-done.9
  1.5 0.1 stack.47
  1.6 0.1 tile.10
  1.7 0.6 broadcast_select_fusion.refs_9_
  2.3 177.3 %shard_map.339 = (bf16[1,4,64,512]{3,2,1,0:T(8,128)(2,1)}, f32[1,4,64,512]{3,2,1,0:T(8,128)}, f32[144,512]{1,0:T(8,128)}, f32[144,512]{1,0:T(8,128)}, f32[16,512...) custom-call(bf16[1,4,64,512]{3,2,1,0:T(8,128)(2,1)} %refs_0_.1, ...), custom_call_target="tpu_custom_call" | custom-call | tf_op jit(solution)/shard_map/pallas_call | solution.py:1541
  179.6 1.5 slice_bitcast_fusion
  181.2 1.7 copy.47
  182.8 0.8 copy.48
  183.6 0.3 copy-done.2
  184.0 0.7 copy.49
  184.7 0.4 copy-done.1
  185.0 0.7 copy.50
  185.8 0.0 copy-done.6
  185.8 0.6 copy.51
  186.4 0.2 copy-done.5
  186.6 0.6 copy.52
  187.2 0.2 copy-done.4
  187.3 0.6 copy.53
  188.0 0.2 copy-done.3
  188.1 0.6 copy.54
  (20 shorter events, 0.1 us)
Async XLA Ops:
  0.7 0.7 copy-start.14
  0.7 0.7 copy-start.15
  0.7 0.7 copy-start.16
  0.7 0.7 copy-start.17
  0.7 0.7 copy-start.10
  0.7 0.7 copy-start.11
  0.7 0.7 copy-start.12
  0.8 0.7 copy-start.13
  0.8 0.7 copy-start.7
  0.8 0.7 copy-start.8
  0.8 0.7 copy-start.9
  179.6 3.2 %copy-start = (f32[1,4,64,512]{3,2,1,0:T(8,128)S(1)}, f32[1,4,64,512]{3,2,1,0:T(8,128)}, u32[]{:S(2)}) copy-start(f32[1,4,64,512]{3,2,1,0:T(8,128)} %get-tuple-element.68) | copy-start | bytes 1572868
  182.8 1.1 copy-start.2
  184.0 1.1 copy-start.1
  185.0 0.8 copy-start.6
  185.8 0.8 copy-start.5
  186.6 0.8 copy-start.4
  187.3 0.8 copy-start.3
where the time goes:
time: 192 us; the launch traced here: 189 us
  Pallas kernels  177 us (92%)
  local copies, waits for them, and re-layouts  9.99 us (5%)
    pallas_call x1, Pallas kernels, strips_on_device(): pl.pallas_call(functools.partial(strip_kernel, dims, names), out_shape=[j...  177 us
    unnamed x44, local copies, waits for them, and re-layouts  8.27 us

commit v1 on v0

--- a/solution.py
+++ b/solution.py
@@ -495,7 +495,8 @@
     k_sib = 2 * xi + other
     k_x = 2 * (1 - xi) + c
     k_diag = 2 * (1 - xi) + other
-    sib, xdev, ydev = (b, other), (bx, c), (by, c)
+    sib, xdev, ydev, diag = (b, other), (bx, c), (by, c), (bx, other)
+    others = ((k_x, xdev), (k_diag, diag), (k_sib, sib))
     lines = groups // 2
 
     def zband(j):
@@ -510,127 +511,173 @@
     barrier = pltpu.get_barrier_semaphore()
 
     def greet(i):
-        @pl.when(i != me)
-        def _():
-            pl.semaphore_signal(barrier, inc=1, device_id=(i // canvases, lax.rem(i, canvases)), device_id_type=MESH)
-
-    loop(devices, greet)
+        to = lax.rem(me + 1 + i, devices)
+        pl.semaphore_signal(barrier, inc=1, device_id=(to // canvases, lax.rem(to, canvases)), device_id_type=MESH)
+
+    loop(devices - 1, greet)
     pl.semaphore_wait(barrier, devices - 1)
 
     sends = []
 
     def start(copy):
         copy.start()
-        sends.append(copy)
-        return copy
+        sends.append((None, copy))
+
+    def start_if(condition, make):
+        def go():
+            make().start()
+
+        pl.when(condition)(go)
+        sends.append((condition, make))
 
     start(remote(r.crops.at[0], r.crop_in, r.s_crop.at[0], r.s_crop.at[1], sib))
     crop_copy = pltpu.make_async_copy(r.crops.at[0], r.crop_own, r.s_crop.at[2])
     crop_copy.start()
 
+    def spread_piece(src, dst, ssem, rsem, i):
+        s = lax.rem(i // MEMBERS + strip, channels // LANES)
+        kk = lax.rem(i + k, MEMBERS)
+        tb = 2 * (s * canvases + c) + kk // 2
+        tc = lax.rem(kk, 2)
+        piece = src.at[0, :, pl.ds(pl.multiple_of(STRIP * s, STRIP), STRIP), lanes(kk)]
+        place = dst.at[pl.ds(band_rows * b, band_rows)]
+        mine = jnp.logical_and(tb == b, tc == c)
+        return (
+            mine,
+            pltpu.make_async_copy(piece, place, rsem),
+            remote(piece, place, ssem.at[i], rsem, (tb, tc)),
+        )
+
     def spread(src, dst, ssem, rsem):
         def one(i):
-            s = i // MEMBERS
-            kk = lax.rem(i, MEMBERS)
-            tb = 2 * (s * canvases + c) + kk // 2
-            tc = lax.rem(kk, 2)
-            piece = src.at[0, :, pl.ds(pl.multiple_of(STRIP * s, STRIP), STRIP), lanes(kk)]
-            place = dst.at[pl.ds(band_rows * b, band_rows)]
-            mine = jnp.logical_and(tb == b, tc == c)
-
-            @pl.when(mine)
-            def _():
-                pltpu.make_async_copy(piece, place, rsem).start()
-
-            @pl.when(jnp.logical_not(mine))
-            def _():
-                remote(piece, place, ssem.at[i], rsem, (tb, tc)).start()
+            mine, here, there = spread_piece(src, dst, ssem, rsem, i)
+            pl.when(mine)(here.start)
+            pl.when(jnp.logical_not(mine))(there.start)
 
         loop(MEMBERS * (channels // LANES), one)
 
-    def spread_sent(src, dst, ssem):
+    def spread_sent(src, dst, ssem, rsem):
         def one(i):
-            s = i // MEMBERS
-            kk = lax.rem(i, MEMBERS)
-            tb = 2 * (s * canvases + c) + kk // 2
-            tc = lax.rem(kk, 2)
-            piece = src.at[0, :, pl.ds(pl.multiple_of(STRIP * s, STRIP), STRIP), lanes(kk)]
-            place = dst.at[pl.ds(band_rows * b, band_rows)]
-
-            @pl.when(jnp.logical_not(jnp.logical_and(tb == b, tc == c)))
-            def _():
-                remote(piece, place, ssem.at[i], ssem.at[i], (tb, tc)).wait_send()
+            mine, _, there = spread_piece(src, dst, ssem, rsem, i)
+            pl.when(jnp.logical_not(mine))(there.wait_send)
 
         loop(MEMBERS * (channels // LANES), one)
 
     def wait_local(ref, sem):
         pltpu.make_async_copy(ref, ref, sem).wait()
 
-    spread(r.x, r.xs, r.s_xs, r.r_xs.at[0])
-
+    def weight_first(w, wc, ssem, rsem):
+        place = wc.at[pl.ds(pl.multiple_of(shard * me, 16), shard)]
+        for n, (kk, device) in enumerate(others):
+            start(remote(w.at[:, lanes(kk)], place, ssem.at[n], rsem.at[0], device))
+        pltpu.make_async_copy(w.at[:, lanes(k)], place, rsem.at[0]).start()
+
+    def wblock(wc, group):
+        return wc.at[pl.ds(pl.multiple_of(block * group, 16), block)]
+
+    class Passage:
+        def __init__(self, place, parts, ssem, rsem):
+            self.place, self.parts, self.ssem, self.rsem = place, parts, ssem, rsem
+            self.used = 0
+
+        def send(self, condition, zs, ys, part, slot, device):
+            sem = self.ssem.at[self.used]
+            self.used += 1
+
+            def make():
+                piece = self.place(zs, ys, part)
+                return remote(piece, piece, sem, self.rsem.at[slot], device)
+
+            if condition is None:
+                start(make())
+            else:
+                start_if(condition, make)
+
+        def came(self, zs, part):
+            return zs * self.parts + part
+
+        def own(self):
+            for part in range(self.parts):
+                self.send(z < lines - 1, z, y, part, self.came(z, part), (b + 4, c))
+                self.send(z > 0, z, y, part, self.came(z, part), (b - 4, c))
+                self.send(None, z, y, part, self.came(lines + z, part), ydev)
+
+        def step(self, t, part):
+            for side in (1, -1):
+                zs = z - side * t
+                there = zs >= 0 if side == 1 else zs < lines
+                zs = jnp.clip(zs, 0, lines - 1)
+                more = z < lines - 1 if side == 1 else z > 0
+
+                def wait(zs=zs):
+                    piece = self.place(zs, y, part)
+                    remote(piece, piece, self.ssem.at[0], self.rsem.at[self.came(zs, part)], ydev).wait_recv()
+
+                pl.when(there)(wait)
+                if t < lines - 1:
+                    self.send(
+                        jnp.logical_and(there, more), zs, y, part, self.came(zs, part), (b + 4 * side, c)
+                    )
+                self.send(there, zs, y, part, self.came(lines + zs, part), ydev)
+
+        def steps(self, t):
+            for part in range(self.parts):
+                self.step(t, part)
+
+        def done(self):
+            for zs in range(lines):
+                for part in range(self.parts):
+                    piece = self.place(zs, 1 - y, part)
+                    remote(
+                        piece, piece, self.ssem.at[0], self.rsem.at[self.came(lines + zs, part)], ydev
+                    ).wait_recv()
+
+    def rows_passage(wc, ssem, rsem):
+        def place(zs, ys, part):
+            return wc.at[pl.ds(pl.multiple_of(block * (2 * zs + ys) + block // 2 * part, 16), block // 2)]
+
+        return Passage(place, 2, ssem, rsem)
+
+    pass1 = rows_passage(r.w1c, r.s_v1, r.r_v1)
+    pass2 = rows_passage(r.w2c, r.s_v2, r.r_v2)
+    passa = Passage(lambda zs, ys, part: r.aw.at[k, 2 * zs + ys], 1, r.s_va, r.r_va)
+
+    def attn_third():
+        own = r.aw.at[k]
+        start(remote(own, own, r.s_aw.at[2 * lines + 1], r.r_aw.at[2 * lines + 1], xdev))
+        start(remote(own, own, r.s_aw.at[2 * lines], r.r_aw.at[2 * lines], sib))
+
+    def attn_fourth():
+        came = r.aw.at[k_x]
+        remote(came, came, r.s_aw.at[0], r.r_aw.at[2 * lines + 1], xdev).wait_recv()
+        start(remote(came, came, r.s_aw.at[2 * lines + 2], r.r_aw.at[2 * lines + 2], sib))
+
+    def attn_fifth():
+        came = r.aw.at[k_sib]
+        remote(came, came, r.s_aw.at[0], r.r_aw.at[2 * lines], sib).wait_recv()
+        came = r.aw.at[k_diag]
+        remote(came, came, r.s_aw.at[0], r.r_aw.at[2 * lines + 2], sib).wait_recv()
+
+    for m, shard_ref in enumerate((r.wq, r.wk, r.wv, r.wo)):
+        pltpu.make_async_copy(shard_ref, r.aw.at[k, q, 16 * m : 16 * m + 16], r.r_aw.at[0]).start()
+    weight_first(r.w1, r.w1c, r.s_w1, r.r_w1)
     vec_copy = pltpu.make_async_copy(r.vec, r.vecs.at[me], r.r_vec.at[0])
     vec_copy.start()
 
-    def vec_send(i):
-        @pl.when(i != me)
-        def _():
-            remote(
-                r.vec, r.vecs.at[me], r.s_vec.at[i], r.r_vec.at[0],
-                (i // canvases, lax.rem(i, canvases)),
-            ).start()
-
-    loop(devices, vec_send)
-
-    def weight_first(w, wc, ssem, rsem):
-        place = wc.at[pl.ds(pl.multiple_of(shard * me, 16), shard)]
-        for kk in range(MEMBERS):
-            piece = w.at[:, kk * LANES : (kk + 1) * LANES]
-
-            @pl.when(k == kk)
-            def _():
-                pltpu.make_async_copy(piece, place, rsem.at[0]).start()
-
-            @pl.when(k != kk)
-            def _():
-                remote(piece, place, ssem.at[kk], rsem.at[0], (2 * q + kk // 2, kk % 2)).start()
-
-    def weight_first_sent(w, wc, ssem, rsem):
-        place = wc.at[pl.ds(pl.multiple_of(shard * me, 16), shard)]
-        for kk in range(MEMBERS):
-            piece = w.at[:, kk * LANES : (kk + 1) * LANES]
-
-            @pl.when(k != kk)
-            def _():
-                remote(piece, place, ssem.at[kk], rsem.at[0], (2 * q + kk // 2, kk % 2)).wait_send()
-
-    def wblock(wc, group):
-        return wc.at[pl.ds(pl.multiple_of(block * group, 16), block)]
-
-    def weight_second(wc, ssem, rsem):
-        own = wblock(wc, q)
-        wait_local(own, rsem.at[0])
-        for j in range(1, lines):
-            start(remote(own, own, ssem.at[MEMBERS + j], rsem.at[j], (zband(j), c)))
-        start(remote(own, own, ssem.at[MEMBERS], rsem.at[lines], ydev))
-
-    def weight_third(wc, ssem, rsem):
-        for j in range(1, lines):
-            came = wblock(wc, 2 * zq(lines - j) + y)
-            remote(came, came, ssem.at[0], rsem.at[j], ydev).wait_recv()
-            start(remote(came, came, ssem.at[MEMBERS + lines + j - 1], rsem.at[lines + j], ydev))
-
-    def weight_fourth(wc, ssem, rsem):
-        for j in range(lines):
-            came = wblock(wc, 2 * zq(lines - j) + 1 - y)
-            remote(came, came, ssem.at[0], rsem.at[lines + j], ydev).wait_recv()
-
-    weight_first(r.w1, r.w1c, r.s_w1, r.r_w1)
+    def vec_piece(i):
+        to = lax.rem(me + 1 + i, devices)
+        return remote(
+            r.vec, r.vecs.at[me], r.s_vec.at[i], r.r_vec.at[0], (to // canvases, lax.rem(to, canvases))
+        )
+
+    loop(devices - 1, lambda i: vec_piece(i).start())
+    spread(r.x, r.xs, r.s_xs, r.r_xs.at[0])
+    wait_local(r.aw.at[k, q], r.r_aw.at[0])
+    passa.own()
     weight_first(r.w2, r.w2c, r.s_w2, r.r_w2)
-    for m, shard_ref in enumerate((r.wq, r.wk, r.wv, r.wo)):
-        pltpu.make_async_copy(shard_ref, r.aw.at[k, q, 16 * m : 16 * m + 16], r.r_aw.at[0]).start()
-
-    weight_second(r.w1c, r.s_w1, r.r_w1)
-    spread(r.g, r.gs, r.s_gs, r.r_gs.at[0])
+    wait_local(wblock(r.w1c, q), r.r_w1.at[0])
+    pass1.own()
+    passa.steps(1)
 
     crop_copy.wait()
     remote(r.crops.at[0], r.crop_in, r.s_crop.at[0], r.s_crop.at[1], sib).wait_recv()
@@ -664,19 +711,12 @@
     group_fold_mat = (iota((LANES, LANES), 0) // STRIP == iota((LANES, LANES), 1) // STRIP).astype(F32)
     r.fold[...] = group_fold_mat
     r.vg[...] = jnp.zeros(r.vg.shape, F32)
+    r.vq[...] = jnp.zeros(r.vq.shape, F32)
     wide = r.y.shape[1]
     for edge in (0, pixels + STRIP):
         r.y[edge : edge + STRIP, :] = jnp.zeros((STRIP, wide), F32)
         r.ebuf[edge : edge + STRIP, :] = jnp.zeros((STRIP, LANES), F32)
 
-    wait_local(r.vecs, r.r_vec.at[0])
-    per = LANES // (channels // devices)
-    for tile in range(n_tiles):
-        total = r.vecs[tile * per].astype(F32)
-        for i in range(1, per):
-            total = total + r.vecs[tile * per + i].astype(F32)
-        r.vfull[:, tile * LANES : (tile + 1) * LANES] = total
-
     def mine_vec(row):
         return r.vfull[row : row + 1, lanes(k)]
 
@@ -689,13 +729,11 @@
     def spread_rows(ref, i):
         return jnp.broadcast_to(ref[at8(i, 8), :].reshape(8, 1, LANES), (8, STRIP, LANES)).reshape(LANES, LANES)
 
-    def norm_stats(load, which):
-        def body(i):
-            v = load(i)
-            r.t1[at8(i, 8), :] = row_sums(v)
-            r.t2[at8(i, 8), :] = row_sums(v * v)
-
-        loop(eighths, body)
+    def sums(i, first, second):
+        r.t1[at8(i, 8), :] = row_sums(first)
+        r.t2[at8(i, 8), :] = row_sums(second)
+
+    def norm_stats(which):
         mean = fold(r.t1[...]) * r.inv_n[...]
         var = fold(r.t2[...]) * r.inv_n[...] - mean * mean
         r.mean[which] = mean
@@ -706,54 +744,54 @@
         rstd = spread_rows(r.rstd.at[which], i)
         return (load(i) - mean) * rstd, rstd
 
-    def norm_back(load_e, load_v, which, gain, gain_row, finish):
-        def body(i):
-            e = load_e(i)
-            xh, _ = xhat_of(load_v, which, i)
-            r.t1[at8(i, 8), :] = row_sums(e)
-            r.t2[at8(i, 8), :] = row_sums(e * xh)
-
-        loop(eighths, body)
+    def norm_back(load_e, load_v, which, gain, gain_row, finish, turn=lambda n: n):
         t1, t2 = r.t1[...], r.t2[...]
-        r.vg[gain_row : gain_row + 1, lanes(k)] = jnp.sum(t2, axis=0, keepdims=True)
-        r.vg[gain_row + 1 : gain_row + 2, lanes(k)] = jnp.sum(t1, axis=0, keepdims=True)
+        r.vg[gain_row : gain_row + 1, :] = jnp.sum(t2, axis=0, keepdims=True)
+        r.vg[gain_row + 1 : gain_row + 2, :] = jnp.sum(t1, axis=0, keepdims=True)
         r.m1[...] = fold(t1 * gain) * r.inv_n[...]
         r.m2[...] = fold(t2 * gain) * r.inv_n[...]
 
-        def out(i):
+        def out(n):
+            i = turn(n)
             xh, rstd = xhat_of(load_v, which, i)
             finish(i, rstd * (load_e(i) * gain - spread_rows(r.m1, i) - xh * spread_rows(r.m2, i)))
 
         loop(eighths, out)
 
-    def gather_start(buf, ssem, rsem):
-        own = buf.at[:, lanes(k)]
-        start(remote(own, own, ssem.at[1], rsem.at[1], xdev))
-        start(remote(own, own, ssem.at[0], rsem.at[0], sib))
-
-    def gather_relay(buf, ssem, rsem):
-        came = buf.at[:, lanes(k_x)]
-        remote(came, came, ssem.at[1], rsem.at[1], xdev).wait_recv()
-        start(remote(came, came, ssem.at[2], rsem.at[2], sib))
-
-    def gather_done(buf, ssem, rsem):
-        came = buf.at[:, lanes(k_sib)]
-        remote(came, came, ssem.at[0], rsem.at[0], sib).wait_recv()
-        came = buf.at[:, lanes(k_diag)]
-        remote(came, came, ssem.at[2], rsem.at[2], sib).wait_recv()
-
-    def reduce_start(part, came, ssem, rsem):
-        start(remote(part(k_diag), came.at[1], ssem.at[1], rsem.at[1], sib))
-        start(remote(part(k_sib), came.at[0], ssem.at[0], rsem.at[0], sib))
-
-    def reduce_relay(part, came, mix, add, ssem, rsem):
-        remote(part(k_diag), came.at[1], ssem.at[1], rsem.at[1], sib).wait_recv()
-        add(mix)
-        start(remote(mix, came.at[2], ssem.at[2], rsem.at[2], xdev))
-
-    def reduce_done(part, came, mix, ssem, rsem):
-        remote(part(k_sib), came.at[0], ssem.at[0], rsem.at[0], sib).wait_recv()
-        remote(mix, came.at[2], ssem.at[2], rsem.at[2], xdev).wait_recv()
+    def quarter(buf, kk, rows):
+        return buf.at[rows, lanes(kk)]
+
+    def gather_start(buf, ssem, rsem, rows, n):
+        own = quarter(buf, k, rows)
+        start(remote(own, own, ssem.at[3 * n + 1], rsem.at[3 * n + 1], xdev))
+        start(remote(own, own, ssem.at[3 * n], rsem.at[3 * n], sib))
+
+    def gather_relay(buf, ssem, rsem, rows, n):
+        came = quarter(buf, k_x, rows)
+        remote(came, came, ssem.at[3 * n + 1], rsem.at[3 * n + 1], xdev).wait_recv()
+        start(remote(came, came, ssem.at[3 * n + 2], rsem.at[3 * n + 2], sib))
+
+    def gather_done(buf, ssem, rsem, rows, n):
+        came = quarter(buf, k_sib, rows)
+        remote(came, came, ssem.at[3 * n], rsem.at[3 * n], sib).wait_recv()
+        came = quarter(buf, k_diag, rows)
+        remote(came, came, ssem.at[3 * n + 2], rsem.at[3 * n + 2], sib).wait_recv()
+
+    def reduce_start(part, came, ssem, rsem, n=0):
+        start(remote(part(k_diag), came(1), ssem.at[3 * n + 1], rsem.at[3 * n + 1], sib))
+        start(remote(part(k_sib), came(0), ssem.at[3 * n], rsem.at[3 * n], sib))
+
+    def reduce_relay(part, came, mix, add, ssem, rsem, n=0):
+        remote(part(k_diag), came(1), ssem.at[3 * n + 1], rsem.at[3 * n + 1], sib).wait_recv()
+        add()
+        start(remote(mix, came(2), ssem.at[3 * n + 2], rsem.at[3 * n + 2], xdev))
+
+    def reduce_done(part, came, mix, ssem, rsem, n=0):
+        remote(part(k_sib), came(0), ssem.at[3 * n], rsem.at[3 * n], sib).wait_recv()
+        remote(mix, came(2), ssem.at[3 * n + 2], rsem.at[3 * n + 2], xdev).wait_recv()
+
+    def quarter_rows(n):
+        return slice(own_px * n, own_px * (n + 1))
 
     column = lax.rem(iota((LANES, LANES), 0), STRIP)
     not_first, not_last = column != 0, column != STRIP - 1
@@ -766,11 +804,11 @@
         for t in range(9):
             wt[t * LANES : (t + 1) * LANES, :] = wc[(8 - t) * channels : (9 - t) * channels, :].T
 
-    def conv(act, wf, bias, out):
-        def multiply(i):
-            r.y[pl.ds(pl.multiple_of(STRIP + 256 * i, 16), 256), :] = dot(act[at8(i, 256), :], wf[...])
-
-        loop(pixels // 256, multiply)
+    def conv(act, wf, bias, out, ssem, rsem):
+        for n in range(MEMBERS):
+            rows = quarter_rows(n)
+            gather_done(act, ssem, rsem, rows, n)
+            r.y[STRIP + own_px * n : STRIP + own_px * (n + 1), :] = dot(act[rows, :], wf[...])
 
         def gather_taps(i):
             up = spread_rows(r.above, i)
@@ -790,34 +828,66 @@
 
         loop(eighths, gather_taps)
 
-    def taps_of_e():
-        def body(i):
-            up = spread_rows(r.above, i)
-            down = spread_rows(r.below, i)
-            for dr in (-1, 0, 1):
-                at = pl.multiple_of(LANES * i + STRIP * (1 + dr), 16)
-                v = r.ebuf[pl.ds(at, LANES), :]
-                if dr == -1:
-                    v = v * up
-                if dr == 1:
-                    v = v * down
-                t = 3 * (dr + 1)
-                rows = at8(i, LANES)
-                r.ecat[rows, t * LANES : (t + 1) * LANES] = jnp.where(
-                    not_first, pltpu.roll(v, 1, 0), 0.0
+    per_chunk = own_px // LANES
+
+    def loop_chunk(n, body):
+        loop(per_chunk, lambda i: body(i + per_chunk * n))
+
+    def taps_of_e(i):
+        up = spread_rows(r.above, i)
+        down = spread_rows(r.below, i)
+        for dr in (-1, 0, 1):
+            at = pl.multiple_of(LANES * i + STRIP * (1 + dr), 16)
+            v = r.ebuf[pl.ds(at, LANES), :]
+            if dr == -1:
+                v = v * up
+            if dr == 1:
+                v = v * down
+            t = 3 * (dr + 1)
+            rows = at8(i, LANES)
+            r.ecat[rows, t * LANES : (t + 1) * LANES] = jnp.where(
+                not_first, pltpu.roll(v, 1, 0), 0.0
+            ).astype(LOW)
+            r.ecat[rows, (t + 1) * LANES : (t + 2) * LANES] = v.astype(LOW)
+            r.ecat[rows, (t + 2) * LANES : (t + 3) * LANES] = jnp.where(
+                not_last, pltpu.roll(v, LANES - 1, 0), 0.0
+            ).astype(LOW)
+
+    def conv_back(wt, part, came, mix, ssem, rsem):
+        def of(n):
+            rows = quarter_rows(n)
+            return (
+                lambda kk: part.at[rows, lanes(kk)],
+                lambda slot: came.at[slot, rows, :],
+                mix.at[rows, :],
+            )
+
+        def relay(n):
+            rows = quarter_rows(n)
+            piece, slot, mixed = of(n)
+
+            def add():
+                mix[rows, :] = (
+                    part[rows, lanes(k_x)].astype(F32) + came[1, rows, :].astype(F32)
                 ).astype(LOW)
-                r.ecat[rows, (t + 1) * LANES : (t + 2) * LANES] = v.astype(LOW)
-                r.ecat[rows, (t + 2) * LANES : (t + 3) * LANES] = jnp.where(
-                    not_last, pltpu.roll(v, LANES - 1, 0), 0.0
-                ).astype(LOW)
-
-        loop(eighths, body)
-
-    def conv_back(wt, part):
-        def body(i):
-            part[at8(i, 256), :] = dot(r.ecat[at8(i, 256), :], wt[...]).astype(LOW)
-
-        loop(pixels // 256, body)
+
+            reduce_relay(piece, slot, mixed, add, ssem, rsem, n)
+
+        for n in range(MEMBERS):
+            rows = quarter_rows(n)
+            loop_chunk(n, taps_of_e)
+            part[rows, :] = dot(r.ecat[rows, :], wt[...]).astype(LOW)
+            piece, slot, mixed = of(n)
+            reduce_start(piece, slot, ssem, rsem, n)
+            if n:
+                relay(n - 1)
+        relay(MEMBERS - 1)
+
+        def done(n):
+            piece, slot, mixed = of(n)
+            reduce_done(piece, slot, mixed, ssem, rsem, n)
+
+        return done
 
     def weight_grad(act_t, dw):
         half = channels // 2
@@ -832,8 +902,8 @@
             zz = zq(j + 1)
             start(remote(wblock(dw, 2 * zz + 1 - y), ry.at[j], ssem.at[j], rsem.at[j], ydev))
 
-    def grad_second(dw, ry, rz, sy, ssem, rsem):
-        for j in range(lines):
+    def grad_second(dw, ry, rz, sy, ssem, rsem, blocks):
+        for j in blocks:
             zz = zq(j + 1)
             remote(wblock(dw, 2 * zz + 1 - y), ry.at[j], ssem.at[j], rsem.at[j], ydev).wait_recv()
 
@@ -855,41 +925,48 @@
             total = sy[lines - 1, at8(i, shard), :].astype(F32)
             for j in range(lines - 1):
                 total = total + rz[j, at8(i, shard), :].astype(F32)
-            fx[at8(i, shard), :] = total
+            fx[at8(i, shard), :] = total.astype(LOW)
 
         loop(MEMBERS, add)
-        for kk in range(MEMBERS):
-            piece = fx.at[kk * shard : (kk + 1) * shard]
-            place = out.at[:, lanes(k)]
-
-            @pl.when(k == kk)
-            def _():
-                pltpu.make_async_copy(piece, place, rsem.at[2 * lines]).start()
-
-            @pl.when(k != kk)
-            def _():
-                remote(
-                    piece, place, ssem.at[2 * lines + kk], rsem.at[2 * lines], (2 * q + kk // 2, kk % 2)
-                ).start()
-
-    def grad_done(fx, out, ssem, rsem):
-        wait_local(out, rsem.at[2 * lines])
-        for kk in range(MEMBERS):
-            piece = fx.at[kk * shard : (kk + 1) * shard]
-
-            @pl.when(k != kk)
-            def _():
-                remote(
-                    piece, out.at[:, lanes(k)], ssem.at[2 * lines + kk], rsem.at[2 * lines],
-                    (2 * q + kk // 2, kk % 2),
-                ).wait_send()
+        place = out.at[:, lanes(k)]
+
+        def piece(kk):
+            return fx.at[pl.ds(pl.multiple_of(shard * kk, 16), shard)]
+
+        pltpu.make_async_copy(piece(k), place, rsem.at[2 * lines]).start()
+        for n, (kk, device) in enumerate(others):
+            start(remote(piece(kk), place, ssem.at[2 * lines + n], rsem.at[2 * lines], device))
+
+    pass1.steps(1)
+    passa.steps(2)
 
     wait_local(r.xs, r.r_xs.at[0])
 
     def load_x(i):
         return r.xs[at8(i, 8)].reshape(LANES, LANES).astype(F32)
 
-    norm_stats(load_x, 0)
+    def sums_x(i):
+        v = load_x(i)
+        sums(i, v, v * v)
+
+    loop(eighths, sums_x)
+    norm_stats(0)
+    wait_local(r.vecs, r.r_vec.at[0])
+    own = channels // devices
+    per = LANES // own
+    row_of, col_of = iota((per * LANES, LANES), 0), iota((per * LANES, LANES), 1)
+    to_place = (col_of == own * (row_of // LANES) + lax.rem(row_of, own)).astype(LOW)
+    of_vector = iota((8, LANES), 1) // own == iota((8, LANES), 0)
+    for tile in range(n_tiles):
+        for half in range(2):
+            parts = [
+                jnp.where(of_vector, jnp.broadcast_to(r.vecs[tile * per + i, half : half + 1, :], (8, LANES)), 0.0)
+                for i in range(per)
+            ]
+            r.vfull[8 * half : 8 * half + 8, tile * LANES : (tile + 1) * LANES] = dot(
+                jnp.concatenate(parts, axis=1).astype(LOW), to_place
+            )
+
     gain1, shift1 = mine_vec(0), mine_vec(1)
 
     def act1(i):
@@ -897,37 +974,34 @@
         u = xh * gain1 + shift1
         r.h1[at8(i, LANES), lanes(k)] = (u * sigmoid(u)).astype(LOW)
 
-    loop(eighths, act1)
-    gather_start(r.h1, r.s_h1, r.r_h1)
-    weight_third(r.w1c, r.s_w1, r.r_w1)
-    weight_second(r.w2c, r.s_w2, r.r_w2)
-    gather_relay(r.h1, r.s_h1, r.r_h1)
-    wait_local(r.gs, r.r_gs.at[0])
-
-    def low_g(i):
-        r.gall[at8(i, LANES), lanes(k)] = r.gs[at8(i, 8)].reshape(LANES, LANES)
-
-    loop(eighths, low_g)
-
-    own_aw = r.aw.at[k, q]
-    wait_local(own_aw, r.r_aw.at[0])
-    for j in range(1, lines):
-        start(remote(own_aw, own_aw, r.s_aw.at[j], r.r_aw.at[j], (zband(j), c)))
-    start(remote(own_aw, own_aw, r.s_aw.at[0], r.r_aw.at[lines], ydev))
-
-    weight_fourth(r.w1c, r.s_w1, r.r_w1)
+    for n in range(MEMBERS):
+        loop_chunk(n, act1)
+        gather_start(r.h1, r.s_h1, r.r_h1, quarter_rows(n), n)
+    passa.steps(3)
+    pass1.steps(2)
+    gather_relay(r.h1, r.s_h1, r.r_h1, quarter_rows(0), 0)
+    gather_relay(r.h1, r.s_h1, r.r_h1, quarter_rows(1), 1)
+    pass1.step(3, 0)
+    gather_relay(r.h1, r.s_h1, r.r_h1, quarter_rows(2), 2)
+    gather_relay(r.h1, r.s_h1, r.r_h1, quarter_rows(3), 3)
+    pass1.step(3, 1)
+    wait_local(wblock(r.w2c, q), r.r_w2.at[0])
+    pass2.own()
+    passa.done()
+    attn_third()
+    pass1.done()
     conv_wide(r.w1c, r.wf)
-    gather_done(r.h1, r.s_h1, r.r_h1)
 
     def put_c1(i, v):
         r.c1[at8(i, LANES), :] = v
-
-    conv(r.h1, r.wf, mine_vec(2), put_c1)
+        sums(i, v, v * v)
+
+    conv(r.h1, r.wf, mine_vec(2), put_c1, r.s_h1, r.r_h1)
 
     def load_c1(i):
         return r.c1[at8(i, LANES), :]
 
-    norm_stats(load_c1, 1)
+    norm_stats(1)
     gain2, shift2 = mine_vec(3), mine_vec(4)
 
     def act2(i):
@@ -935,109 +1009,103 @@
         u = xh * gain2 + shift2
         r.h2[at8(i, LANES), lanes(k)] = (u * sigmoid(u)).astype(LOW)
 
-    loop(eighths, act2)
-    gather_start(r.h2, r.s_h2, r.r_h2)
-    weight_third(r.w2c, r.s_w2, r.r_w2)
-    gather_relay(r.h2, r.s_h2, r.r_h2)
-    gather_start(r.gall, r.s_ga, r.r_ga)
-    for j in range(1, lines):
-        came = r.aw.at[k, 2 * zq(lines - j) + y]
-        remote(came, came, r.s_aw.at[0], r.r_aw.at[j], ydev).wait_recv()
-        start(remote(came, came, r.s_aw.at[lines + j], r.r_aw.at[lines + j], ydev))
-    weight_fourth(r.w2c, r.s_w2, r.r_w2)
-    conv_wide(r.w2c, r.wf)
-    gather_done(r.h2, r.s_h2, r.r_h2)
-
-    def put_r(i, v):
-        total = v + load_x(i)
-        r.res[at8(i, LANES), :] = total
-        r.resl[at8(i, LANES), :] = total.astype(LOW)
-
-    conv(r.h2, r.wf, mine_vec(5), put_r)
-
-    def load_r(i):
-        return r.res[at8(i, LANES), :]
-
-    norm_stats(load_r, 2)
-    gain3, shift3 = mine_vec(6), mine_vec(7)
-
-    def act3(i):
-        xh, _ = xhat_of(load_r, 2, i)
-        r.hn[at8(i, LANES), lanes(k)] = (xh * gain3 + shift3).astype(LOW)
-
-    loop(eighths, act3)
-    gather_start(r.hn, r.s_hn, r.r_hn)
-
-    def rows_of(i):
-        return pl.ds(pl.multiple_of(own_px * i, own_px), own_px)
-
-    def swap_start(src, dst, ssem, rsem, to_lanes):
-        for kk in range(MEMBERS):
-            if to_lanes:
-                piece, place = src.at[rows_of(kk)], dst.at[:, lanes(k)]
-            else:
-                piece, place = src.at[:, kk * LANES : (kk + 1) * LANES], dst.at[rows_of(k)]
-
-            @pl.when(k == kk)
-            def _():
-                pltpu.make_async_copy(piece, place, rsem.at[0]).start()
-
-            @pl.when(k != kk)
-            def _():
-                remote(piece, place, ssem.at[kk], rsem.at[0], (2 * q + kk // 2, kk % 2)).start()
-
-    def swap_sent(src, dst, ssem, rsem, to_lanes):
-        for kk in range(MEMBERS):
-            if to_lanes:
-                piece, place = src.at[rows_of(kk)], dst.at[:, lanes(k)]
-            else:
-                piece, place = src.at[:, kk * LANES : (kk + 1) * LANES], dst.at[rows_of(k)]
-
-            @pl.when(k != kk)
-            def _():
-                remote(piece, place, ssem.at[kk], rsem.at[0], (2 * q + kk // 2, kk % 2)).wait_send()
-
-    for j in range(lines):
-        came = r.aw.at[k, 2 * zq(lines - j) + 1 - y]
-        remote(came, came, r.s_aw.at[0], r.r_aw.at[lines + j], ydev).wait_recv()
-    own = r.aw.at[k]
-    start(remote(own, own, r.s_aw.at[2 * lines + 1], r.r_aw.at[2 * lines + 1], xdev))
-    start(remote(own, own, r.s_aw.at[2 * lines], r.r_aw.at[2 * lines], sib))
-    gather_relay(r.hn, r.s_hn, r.r_hn)
-    gather_relay(r.gall, r.s_ga, r.r_ga)
-    swap_start(r.resl, r.rown, r.s_rs, r.r_rs, True)
-    conv_turned(r.w2c, r.wt2)
-    conv_turned(r.w1c, r.wt1)
-    came = r.aw.at[k_x]
-    remote(came, came, r.s_aw.at[0], r.r_aw.at[2 * lines + 1], xdev).wait_recv()
-    start(remote(came, came, r.s_aw.at[2 * lines + 2], r.r_aw.at[2 * lines + 2], sib))
-    r.h2t[...] = r.h2[...].T
-    r.h1t[...] = r.h1[...].T
-    gather_done(r.hn, r.s_hn, r.r_hn)
-    gather_done(r.gall, r.s_ga, r.r_ga)
-    came = r.aw.at[k_sib]
-    remote(came, came, r.s_aw.at[0], r.r_aw.at[2 * lines], sib).wait_recv()
-    came = r.aw.at[k_diag]
-    remote(came, came, r.s_aw.at[0], r.r_aw.at[2 * lines + 2], sib).wait_recv()
+    for n in range(MEMBERS):
+        loop_chunk(n, act2)
+        gather_start(r.h2, r.s_h2, r.r_h2, quarter_rows(n), n)
+    pass2.steps(1)
+    gather_relay(r.h2, r.s_h2, r.r_h2, quarter_rows(0), 0)
+    gather_relay(r.h2, r.s_h2, r.r_h2, quarter_rows(1), 1)
+    pass2.steps(2)
+    gather_relay(r.h2, r.s_h2, r.r_h2, quarter_rows(2), 2)
+    gather_relay(r.h2, r.s_h2, r.r_h2, quarter_rows(3), 3)
+    attn_fourth()
+    pass2.steps(3)
+    spread(r.g, r.gs, r.s_gs, r.r_gs.at[0])
+    attn_fifth()
     for m in range(4):
         for gq in range(groups):
             for kk in range(MEMBERS):
                 at = 16 * (MEMBERS * gq + kk)
                 r.wa[m, at : at + 16, :] = r.aw[kk, gq, 16 * m : 16 * m + 16, :]
-
+    pass2.done()
+    conv_wide(r.w2c, r.wf)
+
+    def put_r(i, v):
+        total = v + load_x(i)
+        r.res[at8(i, LANES), :] = total
+        r.resl[at8(i, LANES), :] = total.astype(LOW)
+        sums(i, total, total * total)
+
+    conv(r.h2, r.wf, mine_vec(5), put_r, r.s_h2, r.r_h2)
+
+    def load_r(i):
+        return r.res[at8(i, LANES), :]
+
+    norm_stats(2)
+    gain3, shift3 = mine_vec(6), mine_vec(7)
+
+    def act3(i):
+        xh, _ = xhat_of(load_r, 2, i)
+        r.hn[at8(i, LANES), lanes(k)] = (xh * gain3 + shift3).astype(LOW)
+
+    for n in range(MEMBERS):
+        loop_chunk(n, act3)
+        gather_start(r.hn, r.s_hn, r.r_hn, quarter_rows(n), n)
+
+    def rows_of(i):
+        return pl.ds(pl.multiple_of(own_px * i, own_px), own_px)
+
+    def swap_start(src, dst, ssem, rsem, to_lanes):
+        def of(kk):
+            if to_lanes:
+                return src.at[rows_of(kk)], dst.at[:, lanes(k)]
+            return src.at[:, lanes(kk)], dst.at[rows_of(k)]
+
+        for n, (kk, device) in enumerate(others):
+            piece, place = of(kk)
+            start(remote(piece, place, ssem.at[n], rsem.at[0], device))
+        piece, place = of(k)
+        pltpu.make_async_copy(piece, place, rsem.at[0]).start()
+
+    wait_local(r.gs, r.r_gs.at[0])
+
+    def low_g(i):
+        r.gall[at8(i, LANES), lanes(k)] = r.gs[at8(i, 8)].reshape(LANES, LANES)
+
+    loop(eighths, low_g)
+    whole = slice(0, pixels)
+    gather_start(r.gall, r.s_ga, r.r_ga, whole, 0)
+    conv_turned(r.w2c, r.wt2)
+    r.h2t[...] = r.h2[...].T
+    conv_turned(r.w1c, r.wt1)
     scale = float(channels) ** -0.5
     chunk = 128
     own_base = own_px * k
 
-    def project(i):
-        rows = at8(i, 256)
+    own_all = rows_of(k)
+
+    def project(n):
+        rows = quarter_rows(n)
+        gather_done(r.hn, r.s_hn, r.r_hn, rows, n)
         hn = r.hn[rows, :]
         r.ka[rows, :] = dot(hn, r.wa[1]).astype(LOW)
         r.va[rows, :] = (dot(hn, r.wa[2]) + r.vfull[9:10, :]).astype(LOW)
         r.qa[rows, :] = (dot(hn, r.wa[0]) + r.vfull[8:9, :]).astype(LOW)
+
+    for n in range(MEMBERS):
+        gather_relay(r.hn, r.s_hn, r.r_hn, quarter_rows(n), n)
+        if n:
+            project(n - 1)
+    gather_relay(r.gall, r.s_ga, r.r_ga, whole, 0)
+    project(MEMBERS - 1)
+    gather_done(r.gall, r.s_ga, r.r_ga, whole, 0)
+
+    def out_back(i):
+        rows = rows_of(lax.rem(k + i, MEMBERS))
         r.goa[rows, :] = dot_t(r.gall[rows, :], r.wa[3]).astype(LOW)
 
-    loop(pixels // 256, project)
+    out_back(0)
+    swap_start(r.resl, r.rown, r.s_rs, r.r_rs, True)
 
     def mask_of(i):
         return r.id_own[at8(i, chunk), 0:1] == r.id_all[0:1, :]
@@ -1062,13 +1130,53 @@
     loop(own_px // chunk, attend)
     r.ldt[...] = r.ld[...].T[0:8, :]
     r.ldall[k] = r.ldt[...]
-    for kk in range(MEMBERS):
-
-        @pl.when(k != kk)
-        def _():
-            remote(
-                r.ldt, r.ldall.at[k], r.s_ld.at[kk], r.r_ld.at[k], (2 * q + kk // 2, kk % 2)
-            ).start()
+    for n, (kk, device) in enumerate(others):
+        start(remote(r.ldt, r.ldall.at[k], r.s_ld.at[n], r.r_ld.at[n], device))
+
+
+    def attn_piece(m):
+        return (lambda kk: r.da.at[m, kk]), (lambda slot: r.dac.at[m, slot]), r.damix.at[m]
+
+    def attn_grad(m, left, right):
+        grad = dot(left, right).astype(LOW)
+        for gq in range(groups):
+            for kk in range(MEMBERS):
+                at = 16 * (MEMBERS * gq + kk)
+                r.da[m, kk, gq] = grad[at : at + 16, :]
+        piece, slot, mixed = attn_piece(m)
+        reduce_start(piece, slot, r.s_da, r.r_da, m)
+
+    def attn_relay(m):
+        def add():
+            r.damix[m] = (r.da[m, k_x].astype(F32) + r.dac[m, 1].astype(F32)).astype(LOW)
+
+        piece, slot, mixed = attn_piece(m)
+        reduce_relay(piece, slot, mixed, add, r.s_da, r.r_da, m)
+
+    def attn_sum(m):
+        piece, slot, mixed = attn_piece(m)
+        reduce_done(piece, slot, mixed, r.s_da, r.r_da, m)
+        r.das[m] = (
+            (r.da[m, k].astype(F32) + r.dac[m, 0].astype(F32) + r.dac[m, 2].astype(F32))
+            .astype(LOW)
+            .reshape(r.das.shape[1:])
+        )
+        start(remote(r.das.at[m, :, 1 - y], r.ay.at[m], r.s_ag.at[4 * m], r.r_ag.at[4 * m], ydev))
+
+    def attn_along(m):
+        remote(r.das.at[m, :, 1 - y], r.ay.at[m], r.s_ag.at[4 * m], r.r_ag.at[4 * m], ydev).wait_recv()
+        kept = r.das[m, :, pl.ds(y, 1)].reshape(r.ay.shape[1:])
+        r.asum[m] = (kept.astype(F32) + r.ay[m].astype(F32)).astype(LOW)
+        for j in range(1, lines):
+            start(
+                remote(
+                    r.asum.at[m, zq(j)], r.az.at[m, j - 1], r.s_ag.at[4 * m + j], r.r_ag.at[4 * m + j],
+                    (zband(j), c),
+                )
+            )
+
+    r.at[...] = r.a[...].T
+    attn_grad(3, r.at[...], r.gall[own_all, :])
 
     def query_back(i):
         dp = dot_t(r.goa[own_chunk(i), :], r.va[...])
@@ -1076,14 +1184,14 @@
         r.dq[at8(i, chunk), :] = (dot(ds, r.ka[...]) * scale).astype(LOW)
 
     loop(own_px // chunk, query_back)
-
-    for kk in range(MEMBERS):
-
-        @pl.when(k != kk)
-        def _():
-            remote(
-                r.ldt, r.ldall.at[kk], r.s_ld.at[kk], r.r_ld.at[kk], (2 * q + kk // 2, kk % 2)
-            ).wait_recv()
+    attn_relay(3)
+    loop(MEMBERS - 1, lambda i: out_back(i + 1))
+    r.hnt[...] = r.hn[own_all, :].T
+    attn_grad(0, r.hnt[...], r.dq[...])
+
+    for n, (kk, device) in enumerate(others):
+        remote(r.ldt, r.ldall.at[kk], r.s_ld.at[n], r.r_ld.at[n], device).wait_recv()
+    attn_relay(0)
 
     def key_back(i):
         mask = mask_of(i)
@@ -1097,29 +1205,19 @@
         r.dk[at8(i, chunk), :] = (dot(ds, r.qa[...]) * scale).astype(LOW)
 
     loop(own_px // chunk, key_back)
-
     r.dhn[...] = (
         dot_t(r.dq[...], r.wa[0]) + dot_t(r.dk[...], r.wa[1]) + dot_t(r.dv[...], r.wa[2])
     ).astype(LOW)
     swap_start(r.dhn, r.dhs, r.s_dh, r.r_dh, False)
-
-    r.vg[8:9, :] = jnp.sum(r.dq[...].astype(F32), axis=0, keepdims=True)
-    r.vg[9:10, :] = jnp.sum(r.dv[...].astype(F32), axis=0, keepdims=True)
-    own_all = rows_of(k)
-    r.hnt[...] = r.hn[own_all, :].T
-    r.at[...] = r.a[...].T
-    for m, (left, right) in enumerate(((r.hnt, r.dq), (r.hnt, r.dk), (r.hnt, r.dv), (r.at, None))):
-        grad = dot(left[...], r.gall[own_all, :] if right is None else right[...]).astype(LOW)
-        for gq in range(groups):
-            for kk in range(MEMBERS):
-                at = 16 * (MEMBERS * gq + kk)
-                r.da[kk, gq, 16 * m : 16 * m + 16, :] = grad[at : at + 16, :]
-
-    def attn_part(i):
-        return r.da.at[i]
-
-    reduce_start(attn_part, r.dac, r.s_da, r.r_da)
-
+    attn_sum(3)
+
+    r.vq[0:1, :] = jnp.sum(r.dq[...].astype(F32), axis=0, keepdims=True)
+    r.vq[1:2, :] = jnp.sum(r.dv[...].astype(F32), axis=0, keepdims=True)
+    r.vqin[k] = r.vq[:, lanes(k)]
+    for n, (kk, device) in enumerate(others):
+        start(remote(r.vq.at[:, lanes(kk)], r.vqin.at[k], r.s_vq.at[n], r.r_vq.at[n], device))
+    attn_grad(1, r.hnt[...], r.dk[...])
+    attn_grad(2, r.hnt[...], r.dv[...])
     wait_local(r.rown, r.r_rs.at[0])
     r.outl[...] = (
         (r.rown[...].astype(F32) + dot(r.a[...], r.wa[3]) + r.vfull[10:11, :])
@@ -1128,107 +1226,84 @@
     )
     bands_of_mine = own_px // STRIP // band_rows
 
-    def out_copy(i, local):
+    def out_copy(i):
         piece = r.outl.at[i * band_rows : (i + 1) * band_rows]
         place = r.out.at[0, :, pl.ds(pl.multiple_of(STRIP * strip, STRIP), STRIP), :]
         tb = bands_of_mine * k + i
-        if local:
-            return pltpu.make_async_copy(piece, place, r.r_out.at[0])
-        return remote(piece, place, r.s_out.at[i], r.r_out.at[0], (tb, canvas))
-
-    def out_is_mine(i):
-        return jnp.logical_and(bands_of_mine * k + i == b, canvas == c)
+        return (
+            jnp.logical_and(tb == b, canvas == c),
+            pltpu.make_async_copy(piece, place, r.r_out.at[0]),
+            remote(piece, place, r.s_out.at[i], r.r_out.at[0], (tb, canvas)),
+        )
 
     for i in range(bands_of_mine):
-
-        @pl.when(out_is_mine(i))
-        def _():
-            out_copy(i, True).start()
-
-        @pl.when(jnp.logical_not(out_is_mine(i)))
-        def _():
-            out_copy(i, False).start()
-
-    wait_local(r.dhs, r.r_dh.at[0])
-
-    def load_dhn(i):
-        return r.dhs[at8(i, LANES), :].astype(F32)
-
-    def padded(i):
-        return pl.ds(pl.multiple_of(LANES * i + STRIP, 16), LANES)
-
-    def put_dr(i, v):
-        total = v + r.gs[at8(i, 8)].reshape(LANES, LANES).astype(F32)
-        r.dres[at8(i, LANES), :] = total
-        r.ebuf[padded(i), :] = total.astype(LOW).astype(F32)
-
-    norm_back(load_dhn, load_r, 2, gain3, 6, put_dr)
+        mine, here, there = out_copy(i)
+        pl.when(mine)(here.start)
+        pl.when(jnp.logical_not(mine))(there.start)
+    attn_sum(0)
 
     def bias_grad(row, load):
         def body(i):
             r.t1[at8(i, 8), :] = row_sums(load(i))
 
         loop(eighths, body)
-        r.vg[row : row + 1, lanes(k)] = jnp.sum(r.t1[...], axis=0, keepdims=True)
+        r.vg[row : row + 1, :] = jnp.sum(r.t1[...], axis=0, keepdims=True)
+
+    def load_g(i):
+        return r.gs[at8(i, 8)].reshape(LANES, LANES).astype(F32)
+
+    bias_grad(10, load_g)
+    r.h1t[...] = r.h1[...].T
+
+    wait_local(r.dhs, r.r_dh.at[0])
+
+    def load_dhn(i):
+        return r.dhs[at8(i, LANES), :].astype(F32)
+
+    def padded(i):
+        return pl.ds(pl.multiple_of(LANES * i + STRIP, 16), LANES)
+
+    def sums_dhn(i):
+        e = load_dhn(i)
+        xh, _ = xhat_of(load_r, 2, i)
+        sums(i, e, e * xh)
+
+    def put_dr(i, v):
+        total = v + load_g(i)
+        r.dres[at8(i, LANES), :] = total
+        r.ebuf[padded(i), :] = total.astype(LOW).astype(F32)
 
     def load_e(i):
         return r.ebuf[padded(i), :]
 
-    taps_of_e()
-    conv_back(r.wt2, r.part2)
-
-    def conv_part(ref):
-        return lambda i: ref.at[:, lanes(i)]
-
-    def adder(part, came):
-        def add(mix):
-            def body(i):
-                rows = at8(i, LANES)
-                mix[rows, :] = (
-                    part[rows, lanes(k_x)].astype(F32) + came[1, rows, :].astype(F32)
-                ).astype(LOW)
-
-            loop(eighths, body)
-
-        return add
-
-    reduce_start(conv_part(r.part2), r.came2, r.s_p2, r.r_p2)
-    bias_grad(5, load_e)
-    reduce_relay(
-        conv_part(r.part2), r.came2, r.mix2, adder(r.part2, r.came2), r.s_p2, r.r_p2
-    )
+    loop(eighths, sums_dhn)
+    norm_back(load_dhn, load_r, 2, gain3, 6, put_dr)
+    attn_along(3)
+    done2 = conv_back(r.wt2, r.part2, r.came2, r.mix2, r.s_p2, r.r_p2)
+    attn_relay(1)
     weight_grad(r.h2t, r.dw2)
     grad_first(r.dw2, r.ry2, r.s_g2, r.r_g2)
-
-    def attn_add(mix):
+    attn_along(0)
+    bias_grad(5, load_e)
+
+    def slope(load_v, which, gain, shift, part, came, done):
         def body(i):
-            mix[i] = (r.da[k_x, i].astype(F32) + r.dac[1, i].astype(F32)).astype(LOW)
-
-        loop(groups, body)
-
-    reduce_relay(attn_part, r.dac, r.damix, attn_add, r.s_da, r.r_da)
-    bias_grad(10, lambda i: r.gs[at8(i, 8)].reshape(LANES, LANES).astype(F32))
-    reduce_done(conv_part(r.part2), r.came2, r.mix2, r.s_p2, r.r_p2)
-
-    def summed(part, came):
-        def load(i):
             rows = at8(i, LANES)
-            return (
+            dh = (
                 part[rows, lanes(k)].astype(F32)
                 + came[0, rows, :].astype(F32)
                 + came[2, rows, :].astype(F32)
             )
-
-        return load
-
-    def slope(load_v, which, gain, shift, load_dh):
-        def body(i):
             xh, _ = xhat_of(load_v, which, i)
             u = xh * gain + shift
             s = sigmoid(u)
-            r.du[at8(i, LANES), :] = load_dh(i) * (s * (1.0 + u * (1.0 - s)))
-
-        loop(eighths, body)
+            du = dh * (s * (1.0 + u * (1.0 - s)))
+            r.du[rows, :] = du
+            sums(i, du, du * xh)
+
+        for n in range(MEMBERS):
+            done(n)
+            loop_chunk(n, body)
 
     def load_du(i):
         return r.du[at8(i, LANES), :]
@@ -1236,158 +1311,113 @@
     def put_e1(i, v):
         r.ebuf[padded(i), :] = v.astype(LOW).astype(F32)
 
-    slope(load_c1, 1, gain2, shift2, summed(r.part2, r.came2))
+    slope(load_c1, 1, gain2, shift2, r.part2, r.came2, done2)
+    attn_relay(2)
     norm_back(load_du, load_c1, 1, gain2, 3, put_e1)
-    taps_of_e()
-    conv_back(r.wt1, r.part1)
-    reduce_start(conv_part(r.part1), r.came1, r.s_p1, r.r_p1)
-    bias_grad(2, load_e)
-    reduce_relay(
-        conv_part(r.part1), r.came1, r.mix1, adder(r.part1, r.came1), r.s_p1, r.r_p1
-    )
+    done1 = conv_back(r.wt1, r.part1, r.came1, r.mix1, r.s_p1, r.r_p1)
+    attn_sum(1)
+    grad_second(r.dw2, r.ry2, r.rz2, r.sy2, r.s_g2, r.r_g2, range(2))
     weight_grad(r.h1t, r.dw1)
     grad_first(r.dw1, r.ry1, r.s_g1, r.r_g1)
-
-    reduce_done(attn_part, r.dac, r.damix, r.s_da, r.r_da)
-
-    def attn_sum(i):
-        r.das[i] = (
-            r.da[k, i].astype(F32) + r.dac[0, i].astype(F32) + r.dac[2, i].astype(F32)
-        ).astype(LOW)
-
-    loop(groups, attn_sum)
-    for j in range(lines):
-        start(
-            remote(r.das.at[2 * zq(j + 1) + 1 - y], r.ay.at[j], r.s_ag.at[j], r.r_ag.at[j], ydev)
+    bias_grad(2, load_e)
+    grad_second(r.dw2, r.ry2, r.rz2, r.sy2, r.s_g2, r.r_g2, range(2, lines))
+
+    slope(load_x, 0, gain1, shift1, r.part1, r.came1, done1)
+
+    def dx_copy(i):
+        piece = r.dxs.at[pl.ds(band_rows * i, band_rows)]
+        place = r.dx.at[0, :, pl.ds(pl.multiple_of(STRIP * strip, STRIP), STRIP), lanes(k)]
+        return (
+            jnp.logical_and(i == b, canvas == c),
+            pltpu.make_async_copy(piece, place, r.r_dx.at[0]),
+            remote(piece, place, r.s_dx.at[i], r.r_dx.at[0], (i, canvas)),
         )
-    reduce_done(conv_part(r.part1), r.came1, r.mix1, r.s_p1, r.r_p1)
-
-    slope(load_x, 0, gain1, shift1, summed(r.part1, r.came1))
+
+    bands_of_eighth = 8 // band_rows
 
     def put_dx(i, v):
         total = v + r.dres[at8(i, LANES), :]
         r.dxs[at8(i, 8)] = total.astype(LOW).reshape(8, STRIP, LANES)
-
-    norm_back(load_du, load_x, 0, gain1, 0, put_dx)
-
-    def dx_copy(i, local):
-        piece = r.dxs.at[pl.ds(band_rows * i, band_rows)]
-        place = r.dxi.at[:, pl.ds(pl.multiple_of(STRIP * strip, STRIP), STRIP), lanes(k)]
-        if local:
-            return pltpu.make_async_copy(piece, place, r.r_dx.at[0])
-        return remote(piece, place, r.s_dx.at[i], r.r_dx.at[0], (i, canvas))
-
-    def dx_send(i):
-        mine = jnp.logical_and(i == b, canvas == c)
-
-        @pl.when(mine)
-        def _():
-            dx_copy(i, True).start()
-
-        @pl.when(jnp.logical_not(mine))
-        def _():
-            dx_copy(i, False).start()
-
-    loop(bands, dx_send)
-    r.vgin[me] = r.vg[:, lanes(me // per)]
+        for n in range(bands_of_eighth):
+            mine, here, there = dx_copy(bands_of_eighth * i + n)
+            pl.when(mine)(here.start)
+            pl.when(jnp.logical_not(mine))(there.start)
+
+    norm_back(load_du, load_x, 0, gain1, 0, put_dx, lambda n: lax.rem(n + q, eighths))
+    for n, (kk, device) in enumerate(others):
+        came = r.vqin.at[kk]
+        remote(came, came, r.s_vq.at[n], r.r_vq.at[n], device).wait_recv()
+    r.vg[8:10, :] = (r.vqin[0] + r.vqin[1] + r.vqin[2] + r.vqin[3])[0:2, :]
 
     def vg_copy(i):
-        return remote(
-            r.vg.at[:, lanes(i // per)], r.vgin.at[me], r.s_vg.at[i], r.r_vg.at[me],
-            (i // canvases, lax.rem(i, canvases)),
+        to = per * k + lax.rem(i + q, per)
+        return (
+            to == me,
+            pltpu.make_async_copy(r.vg, r.vgin.at[q], r.r_vg.at[q]),
+            remote(r.vg, r.vgin.at[q], r.s_vg.at[i], r.r_vg.at[q], (to // canvases, lax.rem(to, canvases))),
         )
 
     def vg_send(i):
-        @pl.when(i != me)
-        def _():
-            vg_copy(i).start()
-
-    loop(devices, vg_send)
-
-    grad_second(r.dw2, r.ry2, r.rz2, r.sy2, r.s_g2, r.r_g2)
-    for j in range(lines):
-        zz = zq(j + 1)
-        remote(r.das.at[2 * zz + 1 - y], r.ay.at[j], r.s_ag.at[j], r.r_ag.at[j], ydev).wait_recv()
-        r.asum[j] = (r.das[2 * zz + y].astype(F32) + r.ay[j].astype(F32)).astype(LOW)
-        if j + 1 < lines:
-            start(
-                remote(
-                    r.asum.at[j], r.az.at[j], r.s_ag.at[lines + j], r.r_ag.at[lines + j],
-                    (zband(j + 1), c),
-                )
-            )
-    grad_second(r.dw1, r.ry1, r.rz1, r.sy1, r.s_g1, r.r_g1)
-    grad_third(r.sy2, r.rz2, r.fx2, r.dw2out, r.s_g2, r.r_g2)
-
-    wait_local(r.dxi, r.r_dx.at[0])
-    r.dx[...] = r.dxi[...].astype(F32)[None]
-
-    total = r.asum[lines - 1].astype(F32)
-    for j in range(lines - 1):
-        remote(
-            r.asum.at[j], r.az.at[j], r.s_ag.at[lines + j], r.r_ag.at[lines + j], (zband(j + 1), c)
-        ).wait_recv()
-        total = total + r.az[j].astype(F32)
-    for m, ref in enumerate((r.dwq, r.dwk, r.dwv, r.dwo)):
-        ref[...] = total[16 * m : 16 * m + 16, :]
+        mine, here, there = vg_copy(i)
+        pl.when(mine)(here.start)
+        pl.when(jnp.logical_not(mine))(there.start)
+
+    loop(per, vg_send)
+
+    attn_sum(2)
+    attn_along(1)
+    grad_second(r.dw1, r.ry1, r.rz1, r.sy1, r.s_g1, r.r_g1, range(lines))
+    attn_along(2)
+    grad_third(r.sy2, r.rz2, r.fx2, r.dwc.at[shard : 2 * shard], r.s_g2, r.r_g2)
+
+    for m in range(4):
+        total = r.asum[m, pl.ds(z, 1)].astype(F32)
+        for j in range(1, lines):
+            came = r.az.at[m, j - 1]
+            remote(came, came, r.s_ag.at[4 * m + j], r.r_ag.at[4 * m + j], sib).wait_recv()
+            total = total + r.az[m, j - 1].astype(F32)[None]
+        r.dwa[16 * m : 16 * m + 16, :] = total.reshape(16, channels)
 
     def vg_wait(i):
-        @pl.when(i != me)
-        def _():
-            remote(
-                r.vg.at[:, lanes(i // per)], r.vgin.at[i], r.s_vg.at[i], r.r_vg.at[i],
-                (i // canvases, lax.rem(i, canvases)),
-            ).wait()
-
-    loop(devices, vg_wait)
+        wait_local(r.vgin.at[i], r.r_vg.at[i])
+
+    loop(groups, vg_wait)
     total = r.vgin[0]
-    for i in range(1, devices):
+    for i in range(1, groups):
         total = total + r.vgin[i]
-    piece = LANES // per
-    turn = (iota((LANES, LANES), 0) == iota((LANES, LANES), 1) + piece * lax.rem(me, per)).astype(F32)
+    turn = (iota((LANES, LANES), 0) == iota((LANES, LANES), 1) + own * lax.rem(me, per)).astype(F32)
     r.dvec[...] = exact(total, turn)
 
-    grad_third(r.sy1, r.rz1, r.fx1, r.dw1out, r.s_g1, r.r_g1)
+    grad_third(r.sy1, r.rz1, r.fx1, r.dwc.at[0:shard], r.s_g1, r.r_g1)
+    wait_local(r.dx, r.r_dx.at[0])
     wait_local(r.out, r.r_out.at[0])
-    grad_done(r.fx2, r.dw2out, r.s_g2, r.r_g2)
-    grad_done(r.fx1, r.dw1out, r.s_g1, r.r_g1)
-
-    for copy in sends:
-        copy.wait_send()
-    spread_sent(r.x, r.xs, r.s_xs)
-    spread_sent(r.g, r.gs, r.s_gs)
-
-    def vec_sent(i):
-        @pl.when(i != me)
-        def _():
-            remote(
-                r.vec, r.vecs.at[me], r.s_vec.at[i], r.r_vec.at[0],
-                (i // canvases, lax.rem(i, canvases)),
-            ).wait_send()
-
-    loop(devices, vec_sent)
-    weight_first_sent(r.w1, r.w1c, r.s_w1, r.r_w1)
-    weight_first_sent(r.w2, r.w2c, r.s_w2, r.r_w2)
-    swap_sent(r.resl, r.rown, r.s_rs, r.r_rs, True)
-    swap_sent(r.dhn, r.dhs, r.s_dh, r.r_dh, False)
-    for kk in range(MEMBERS):
-
-        @pl.when(k != kk)
-        def _():
-            remote(
-                r.ldt, r.ldall.at[k], r.s_ld.at[kk], r.r_ld.at[k], (2 * q + kk // 2, kk % 2)
-            ).wait_send()
-
+    wait_local(r.dwc.at[shard : 2 * shard], r.r_g2.at[2 * lines])
+    wait_local(r.dwc.at[0:shard], r.r_g1.at[2 * lines])
+
+    def sent(make):
+        make().wait_send()
+
+    for condition, copy in sends:
+        if condition is None:
+            copy.wait_send()
+        else:
+            pl.when(condition)(functools.partial(sent, copy))
+    spread_sent(r.x, r.xs, r.s_xs, r.r_xs.at[0])
+    spread_sent(r.g, r.gs, r.s_gs, r.r_gs.at[0])
+    loop(devices - 1, lambda i: vec_piece(i).wait_send())
+
+    def vg_sent(i):
+        mine, _, there = vg_copy(i)
+        pl.when(jnp.logical_not(mine))(there.wait_send)
+
+    loop(per, vg_sent)
     for i in range(bands_of_mine):
-
-        @pl.when(jnp.logical_not(out_is_mine(i)))
-        def _():
-            out_copy(i, False).wait_send()
+        mine, _, there = out_copy(i)
+        pl.when(jnp.logical_not(mine))(there.wait_send)
 
     def dx_sent(i):
-        @pl.when(jnp.logical_not(jnp.logical_and(i == b, canvas == c)))
-        def _():
-            dx_copy(i, False).wait_send()
+        mine, _, there = dx_copy(i)
+        pl.when(jnp.logical_not(mine))(there.wait_send)
 
     loop(bands, dx_sent)
 
@@ -1402,23 +1432,19 @@
     width = inputs.shape[2]
     devices = bands * canvases
     own = channels // devices
-    per = LANES // own
     pixels = height * STRIP
     own_px = pixels // MEMBERS
     groups = devices // MEMBERS
     lines = groups // 2
     shard = 9 * channels // devices
     block = MEMBERS * shard
-    me = canvases * lax.axis_index("band") + lax.axis_index("canvas")
     stacked = jnp.stack(
         [
             norm1_gain, norm1_shift, conv1_bias, norm2_gain, norm2_shift, conv2_bias, norm3_gain,
             norm3_shift, query_bias, value_bias, out_bias,
         ]
     )
-    stacked = jnp.pad(stacked, ((0, 16 - VECTORS), (0, 0)))
-    at_lane = jnp.arange(LANES, dtype=jnp.int32)[None, :] // own == lax.rem(me, per)
-    vec = jnp.where(at_lane, jnp.tile(stacked, (1, per)), jnp.zeros((), LOW))
+    vec = jnp.pad(stacked, ((0, 16 - VECTORS), (0, 0))).reshape(2, LANES).astype(F32)
 
     hbm = pl.BlockSpec(memory_space=pl.ANY)
     vmem = pl.BlockSpec(memory_space=pltpu.VMEM)
@@ -1429,13 +1455,9 @@
     grid = (1, band_rows, width, channels)
     outs = dict(
         out=(grid, LOW, hbm),
-        dx=(grid, F32, vmem),
-        dw1out=((shard, channels), F32, hbm),
-        dw2out=((shard, channels), F32, hbm),
-        dwq=((own, channels), F32, vmem),
-        dwk=((own, channels), F32, vmem),
-        dwv=((own, channels), F32, vmem),
-        dwo=((own, channels), F32, vmem),
+        dx=(grid, LOW, hbm),
+        dwc=((2 * shard, channels), LOW, hbm),
+        dwa=((4 * own, channels), F32, vmem),
         dvec=((16, LANES), F32, vmem),
     )
     nine = 9 * LANES
@@ -1444,7 +1466,7 @@
         crop_own=((height, width), jnp.int32),
         xs=((height, STRIP, LANES), LOW),
         gs=((height, STRIP, LANES), LOW),
-        vecs=((devices, 16, LANES), LOW),
+        vecs=((devices, 2, LANES), F32),
         vfull=((16, channels), F32),
         w1c=((9 * channels, LANES), LOW),
         w2c=((9 * channels, LANES), LOW),
@@ -1496,13 +1518,13 @@
         hnt=((channels, own_px), LOW),
         at=((channels, own_px), LOW),
         outl=((own_px // STRIP, STRIP, channels), LOW),
-        da=((MEMBERS, groups, 64, channels), LOW),
-        dac=((3, groups, 64, channels), LOW),
-        damix=((groups, 64, channels), LOW),
-        das=((groups, 64, channels), LOW),
-        ay=((lines, 64, channels), LOW),
-        asum=((lines, 64, channels), LOW),
-        az=((lines - 1, 64, channels), LOW),
+        da=((4, MEMBERS, groups, 16, channels), LOW),
+        dac=((4, 3, groups, 16, channels), LOW),
+        damix=((4, groups, 16, channels), LOW),
+        das=((4, lines, 2, 16, channels), LOW),
+        ay=((4, lines, 16, channels), LOW),
+        asum=((4, lines, 16, channels), LOW),
+        az=((4, lines - 1, 16, channels), LOW),
         dres=((pixels, LANES), F32),
         du=((pixels, LANES), F32),
         part2=((pixels, channels), LOW),
@@ -1519,23 +1541,23 @@
         sy2=((lines, block, LANES), LOW),
         rz1=((lines - 1, block, LANES), LOW),
         rz2=((lines - 1, block, LANES), LOW),
-        fx1=((block, LANES), F32),
-        fx2=((block, LANES), F32),
+        fx1=((block, LANES), LOW),
+        fx2=((block, LANES), LOW),
         dxs=((height, STRIP, LANES), LOW),
-        dxi=((band_rows, width, channels), LOW),
-        vg=((16, channels), F32),
-        vgin=((devices, 16, LANES), F32),
+        vg=((16, LANES), F32),
+        vq=((8, channels), F32),
+        vqin=((MEMBERS, 8, LANES), F32),
+        vgin=((groups, 16, LANES), F32),
     )
     n_spread = MEMBERS * (channels // LANES)
-    n_w = MEMBERS + 2 * lines
     semaphores = dict(
         s_crop=3, s_xs=n_spread, r_xs=1, s_gs=n_spread, r_gs=1, s_vec=devices, r_vec=1,
-        s_w1=n_w, r_w1=n_w, s_w2=n_w, r_w2=n_w, s_aw=2 * lines + 3, r_aw=2 * lines + 3,
-        s_h1=3, r_h1=3, s_h2=3, r_h2=3, s_hn=3, r_hn=3, s_ga=3, r_ga=3,
-        s_rs=4, r_rs=1, s_ld=4, r_ld=4, s_dh=4, r_dh=1, s_da=3, r_da=3,
-        s_out=4, r_out=1, s_p2=3, r_p2=3, s_p1=3, r_p1=3,
+        s_w1=3, r_w1=1, s_w2=3, r_w2=1, s_v1=28, r_v1=4 * lines, s_v2=28, r_v2=4 * lines, s_va=14, r_va=2 * lines, s_aw=2 * lines + 3, r_aw=2 * lines + 3,
+        s_h1=12, r_h1=12, s_h2=12, r_h2=12, s_hn=12, r_hn=12, s_ga=3, r_ga=3,
+        s_rs=4, r_rs=1, s_ld=4, r_ld=4, s_dh=4, r_dh=1, s_da=12, r_da=12,
+        s_out=4, r_out=1, s_p2=12, r_p2=12, s_p1=12, r_p1=12,
         s_g1=2 * lines + 4, r_g1=2 * lines + 1, s_g2=2 * lines + 4, r_g2=2 * lines + 1,
-        s_ag=2 * lines, r_ag=2 * lines, s_dx=bands, r_dx=1, s_vg=devices, r_vg=devices,
+        s_ag=16, r_ag=16, s_vq=3, r_vq=3, s_dx=bands, r_dx=1, s_vg=LANES // own, r_vg=groups,
     )
     names = (*operands, *outs, *buffers, *semaphores)
     results = pl.pallas_call(
@@ -1549,10 +1571,13 @@
             collective_id=0, has_side_effects=True, vmem_limit_bytes=60 * 1024 * 1024
         ),
     )(*operands.values())
-    out, dx, dw1, dw2, dwq, dwk, dwv, dwo, dvec = results
+    out, dx, dwc, dwa, dvec = results
     v = [dvec[i, :own] for i in range(VECTORS)]
+    dwc = dwc.astype(F32)
+    dwq, dwk, dwv, dwo = (dwa[own * m : own * (m + 1)] for m in range(4))
     return (
-        out, dx, v[0], v[1], dw1, v[2], v[3], v[4], dw2, v[5], v[6], v[7], dwq, v[8], dwk, dwv, v[9], dwo, v[10],
+        out, dx.astype(F32), v[0], v[1], dwc[:shard], v[2], v[3], v[4], dwc[shard:], v[5], v[6], v[7], dwq, v[8],
+        dwk, dwv, v[9], dwo, v[10],
     )
 
 

time: 192 us -> 156 us (0.81)
  Pallas kernels: 177 us -> 146 us
  local copies, waits for them, and re-layouts: 9.99 us -> 6.18 us
    pallas_call x1, Pallas kernels: 177 us -> 146 us  [strips_on_device(): pl.pallas_call(functools.partial(strip_kernel, dims, names), out_shape=[j...]
    unnamed x44 -> x29, local copies, waits for them, and re-layouts: 8.27 us -> 1.6 us
    slice x0 -> x2, local copies, waits for them, and re-layouts: none -> 2.34 us  [the longest x1 1.46 us: strips_on_device(): dwq, dwk, dwv, dwo = (dwa[own * m:own * (m + 1)] for m in range(4))]
where the time goes in v1:
time: 156 us; the launch traced here: 154 us
  Pallas kernels  146 us (94%)
  local copies, waits for them, and re-layouts  6.18 us (4%)
    pallas_call x1, Pallas kernels, strips_on_device(): pl.pallas_call(functools.partial(strip_kernel, dims, names), out_shape=[j...  146 us

profile of v1, /device:TPU:25, one launch (start us, length us, event | category | flops | bytes accessed | tf_op | source)
XLA Modules:
  0.0 153.8 jit_solution(9520872445211041532)
XLA Ops:
  0.7 0.0 copy-start.10
  0.7 0.0 copy-start.11
  0.7 0.0 copy-start.12
  0.7 0.0 copy-start.13
  0.7 0.0 copy-start.6
  0.7 0.0 copy-start.7
  0.7 0.0 copy-start.8
  0.7 0.0 copy-start.9
  0.7 0.0 copy-start.3
  0.8 0.0 copy-start.4
  0.8 0.0 copy-start.5
  0.8 0.5 copy-done.10
  1.3 0.0 copy-done.11
  1.3 0.0 copy-done.12
  1.3 0.0 copy-done.13
  1.4 0.0 copy-done.6
  1.4 0.0 copy-done.7
  1.4 0.0 copy-done.8
  1.4 0.0 copy-done.9
  1.4 0.0 copy-done.3
  1.4 0.0 copy-done.4
  1.5 0.0 copy-done.5
  1.5 0.1 stack.47
  1.5 0.6 reshape.41.refs_9_
  2.2 146.0 %shard_map.339 = (bf16[1,4,64,512]{3,2,1,0:T(8,128)(2,1)}, bf16[1,4,64,512]{3,2,1,0:T(8,128)(2,1)}, bf16[288,512]{1,0:T(8,128)(2,1)}, f32[64,512]{1,0:T(8,128)}, f32[16,128]{1,0:T(8,128)}) custom-call(bf16[1,4,64,512]{3,2,1,0:T(8,128)(2,1)} %refs_0_.1, s32[1,64,64]{2,1,0:T(8,128)} %refs_1_.1, bf16[1,4,64,512]{3,2,1,0:T(8,128)(2,1)} %refs_2_.1, ...), custom_call_target="tpu_custom_call" | custom-call | tf_op jit(solution)/shard_map/pallas_call | solution.py:1563
  148.2 1.5 %slice_bitcast_fusion = (f32[16]{0:T(128)}, f32[16]{0:T(128)}, f32[16]{0:T(128)}, f32[16]{0:T(128)}, f32[16]{0:T(128)}, /*index=5*/f32[16]{0:T(128)}, f32[16]{0:...) fusion(f32[16,128]{1,0:T(8,128)} %get-tuple-element.26), kind=kLoop, calls=%fused_computation.1 | loop fusion | bytes 1408 | tf_op jit(solution)/shard_map/squeeze | solution.py:1575
  149.8 1.5 fusion.1
  151.2 0.9 fusion
  152.1 0.1 copy-done.1
  152.2 0.9 convert_element_type.15
  153.0 0.1 copy-done.2
  153.1 0.7 copy.40
  (5 shorter events, 0.0 us)
Async XLA Ops:
  0.7 0.7 copy-start.10
  0.7 0.7 copy-start.11
  0.7 0.7 copy-start.12
  0.7 0.7 copy-start.13
  0.7 0.7 copy-start.6
  0.7 0.7 copy-start.7
  0.7 0.7 copy-start.8
  0.7 0.7 copy-start.9
  0.7 0.7 copy-start.3
  0.8 0.7 copy-start.4
  0.8 0.7 copy-start.5
  148.2 3.0 %copy-start = (bf16[288,512]{1,0:T(8,128)(2,1)S(1)}, bf16[288,512]{1,0:T(8,128)(2,1)}, u32[]{:S(2)}) copy-start(bf16[288,512]{1,0:T(8,128)(2,1)} %get-tuple-element.27) | copy-start | bytes 884740
  151.2 1.0 copy-start.1
  152.2 0.9 copy-start.2

commit v2 on v1

--- a/solution.py
+++ b/solution.py
@@ -505,6 +505,10 @@
     def zq(j):
         return lax.rem(z + j, lines)
 
+    z_near, z_far = z + 1 - 2 * lax.rem(z, 2), lax.rem(z + 2, lines)
+    z_last = z_far + 1 - 2 * lax.rem(z_far, 2)
+    near, far = (b + 4 * (z_near - z), c), (b + 4 * (z_far - z), c)
+
     def lanes(i):
         return pl.ds(pl.multiple_of(i * LANES, LANES), LANES)
 
@@ -580,57 +584,46 @@
             self.place, self.parts, self.ssem, self.rsem = place, parts, ssem, rsem
             self.used = 0
 
-        def send(self, condition, zs, ys, part, slot, device):
-            sem = self.ssem.at[self.used]
+        def send(self, zs, part, slot, device):
+            piece = self.place(zs, y, part)
+            start(remote(piece, piece, self.ssem.at[self.used], self.rsem.at[slot * self.parts + part], device))
             self.used += 1
 
-            def make():
-                piece = self.place(zs, ys, part)
-                return remote(piece, piece, sem, self.rsem.at[slot], device)
-
-            if condition is None:
-                start(make())
-            else:
-                start_if(condition, make)
-
-        def came(self, zs, part):
-            return zs * self.parts + part
+        def wait(self, zs, ys, part, slot):
+            piece = self.place(zs, ys, part)
+            sem = self.rsem.at[slot * self.parts + part]
+            remote(piece, piece, self.ssem.at[0], sem, ydev).wait_recv()
 
         def own(self):
             for part in range(self.parts):
-                self.send(z < lines - 1, z, y, part, self.came(z, part), (b + 4, c))
-                self.send(z > 0, z, y, part, self.came(z, part), (b - 4, c))
-                self.send(None, z, y, part, self.came(lines + z, part), ydev)
-
-        def step(self, t, part):
-            for side in (1, -1):
-                zs = z - side * t
-                there = zs >= 0 if side == 1 else zs < lines
-                zs = jnp.clip(zs, 0, lines - 1)
-                more = z < lines - 1 if side == 1 else z > 0
-
-                def wait(zs=zs):
-                    piece = self.place(zs, y, part)
-                    remote(piece, piece, self.ssem.at[0], self.rsem.at[self.came(zs, part)], ydev).wait_recv()
-
-                pl.when(there)(wait)
-                if t < lines - 1:
-                    self.send(
-                        jnp.logical_and(there, more), zs, y, part, self.came(zs, part), (b + 4 * side, c)
-                    )
-                self.send(there, zs, y, part, self.came(lines + zs, part), ydev)
-
-        def steps(self, t):
+                self.send(z, part, 0, far)
             for part in range(self.parts):
-                self.step(t, part)
+                self.send(z, part, 1, near)
+
+        def own_y(self):
+            for part in range(self.parts):
+                self.send(z, part, 3, ydev)
+
+        def from_far(self, part=0):
+            self.wait(z_far, y, part, 0)
+            self.send(z_far, part, 2, near)
+            self.send(z_far, part, 4, ydev)
+
+        def from_near(self, part=0):
+            self.wait(z_near, y, part, 1)
+            self.send(z_near, part, 5, ydev)
+
+        def from_last(self, part=0):
+            self.wait(z_last, y, part, 2)
+            self.send(z_last, part, 6, ydev)
+
+        def from_y(self, slot):
+            for part in range(self.parts):
+                self.wait((z, z_far, z_near, z_last)[slot - 3], 1 - y, part, slot)
 
         def done(self):
-            for zs in range(lines):
-                for part in range(self.parts):
-                    piece = self.place(zs, 1 - y, part)
-                    remote(
-                        piece, piece, self.ssem.at[0], self.rsem.at[self.came(lines + zs, part)], ydev
-                    ).wait_recv()
+            for slot in range(3, 7):
+                self.from_y(slot)
 
     def rows_passage(wc, ssem, rsem):
         def place(zs, ys, part):
@@ -642,25 +635,32 @@
     pass2 = rows_passage(r.w2c, r.s_v2, r.r_v2)
     passa = Passage(lambda zs, ys, part: r.aw.at[k, 2 * zs + ys], 1, r.s_va, r.r_va)
 
+    def attn_across(zs, ys, n):
+        piece = r.aw.at[k, 2 * zs + ys]
+        start(remote(piece, piece, r.s_aw.at[n], r.r_aw.at[1], xdev))
+
     def attn_third():
         own = r.aw.at[k]
-        start(remote(own, own, r.s_aw.at[2 * lines + 1], r.r_aw.at[2 * lines + 1], xdev))
-        start(remote(own, own, r.s_aw.at[2 * lines], r.r_aw.at[2 * lines], sib))
+        start(remote(own, own, r.s_aw.at[8], r.r_aw.at[2], sib))
 
     def attn_fourth():
         came = r.aw.at[k_x]
-        remote(came, came, r.s_aw.at[0], r.r_aw.at[2 * lines + 1], xdev).wait_recv()
-        start(remote(came, came, r.s_aw.at[2 * lines + 2], r.r_aw.at[2 * lines + 2], sib))
+        remote(came, came, r.s_aw.at[0], r.r_aw.at[1], xdev).wait_recv()
+        start(remote(came, came, r.s_aw.at[9], r.r_aw.at[3], sib))
 
     def attn_fifth():
         came = r.aw.at[k_sib]
-        remote(came, came, r.s_aw.at[0], r.r_aw.at[2 * lines], sib).wait_recv()
+        remote(came, came, r.s_aw.at[0], r.r_aw.at[2], sib).wait_recv()
         came = r.aw.at[k_diag]
-        remote(came, came, r.s_aw.at[0], r.r_aw.at[2 * lines + 2], sib).wait_recv()
+        remote(came, came, r.s_aw.at[0], r.r_aw.at[3], sib).wait_recv()
 
     for m, shard_ref in enumerate((r.wq, r.wk, r.wv, r.wo)):
         pltpu.make_async_copy(shard_ref, r.aw.at[k, q, 16 * m : 16 * m + 16], r.r_aw.at[0]).start()
     weight_first(r.w1, r.w1c, r.s_w1, r.r_w1)
+    wait_local(r.aw.at[k, q], r.r_aw.at[0])
+    passa.own()
+    passa.own_y()
+    attn_across(z, y, 0)
     vec_copy = pltpu.make_async_copy(r.vec, r.vecs.at[me], r.r_vec.at[0])
     vec_copy.start()
 
@@ -672,12 +672,10 @@
 
     loop(devices - 1, lambda i: vec_piece(i).start())
     spread(r.x, r.xs, r.s_xs, r.r_xs.at[0])
-    wait_local(r.aw.at[k, q], r.r_aw.at[0])
-    passa.own()
     weight_first(r.w2, r.w2c, r.s_w2, r.r_w2)
     wait_local(wblock(r.w1c, q), r.r_w1.at[0])
     pass1.own()
-    passa.steps(1)
+    pass1.own_y()
 
     crop_copy.wait()
     remote(r.crops.at[0], r.crop_in, r.s_crop.at[0], r.s_crop.at[1], sib).wait_recv()
@@ -853,7 +851,7 @@
                 not_last, pltpu.roll(v, LANES - 1, 0), 0.0
             ).astype(LOW)
 
-    def conv_back(wt, part, came, mix, ssem, rsem):
+    def conv_back(wt, part, came, mix, ssem, rsem, middle, between=lambda n: None):
         def of(n):
             rows = quarter_rows(n)
             return (
@@ -875,12 +873,18 @@
 
         for n in range(MEMBERS):
             rows = quarter_rows(n)
-            loop_chunk(n, taps_of_e)
+            if n < 2:
+                loop_chunk(n, taps_of_e)
             part[rows, :] = dot(r.ecat[rows, :], wt[...]).astype(LOW)
             piece, slot, mixed = of(n)
             reduce_start(piece, slot, ssem, rsem, n)
             if n:
                 relay(n - 1)
+            between(n)
+            if n == 1:
+                loop_chunk(2, taps_of_e)
+                loop_chunk(3, taps_of_e)
+                middle()
         relay(MEMBERS - 1)
 
         def done(n):
@@ -897,35 +901,46 @@
                 at = (8 - t) * channels + i * half
                 dw[at : at + half, :] = wide_out[:, t * LANES : (t + 1) * LANES].astype(LOW)
 
+    grad_order = (z_last, z_far, z_near, z)
+
     def grad_first(dw, ry, ssem, rsem):
-        for j in range(lines):
-            zz = zq(j + 1)
+        for j, zz in enumerate(grad_order):
             start(remote(wblock(dw, 2 * zz + 1 - y), ry.at[j], ssem.at[j], rsem.at[j], ydev))
 
-    def grad_second(dw, ry, rz, sy, ssem, rsem, blocks):
-        for j in blocks:
-            zz = zq(j + 1)
-            remote(wblock(dw, 2 * zz + 1 - y), ry.at[j], ssem.at[j], rsem.at[j], ydev).wait_recv()
-
-            def add(i):
-                at = pl.multiple_of(block * (2 * zz + y) + shard * i, 16)
-                sy[j, at8(i, shard), :] = (
-                    dw[pl.ds(at, shard), :].astype(F32) + ry[j, at8(i, shard), :].astype(F32)
-                ).astype(LOW)
-
-            loop(MEMBERS, add)
-            if j + 1 < lines:
-                start(remote(sy.at[j], rz.at[j], ssem.at[lines + j], rsem.at[lines + j], (zband(j + 1), c)))
+    def grad_second(dw, ry, rz, sy, ssem, rsem, j):
+        zz = grad_order[j]
+        remote(wblock(dw, 2 * zz + 1 - y), ry.at[j], ssem.at[j], rsem.at[j], ydev).wait_recv()
+
+        def add(i):
+            at = pl.multiple_of(block * (2 * zz + y) + shard * i, 16)
+            sy[j, at8(i, shard), :] = (
+                dw[pl.ds(at, shard), :].astype(F32) + ry[j, at8(i, shard), :].astype(F32)
+            ).astype(LOW)
+
+        loop(MEMBERS, add)
+        if j in (0, 2):
+            n = j // 2
+            start(remote(sy.at[j], rz.at[n], ssem.at[lines + n], rsem.at[lines + n], near))
+
+    def grad_far(sy, rz, ssem, rsem):
+        remote(sy.at[0], rz.at[0], ssem.at[lines], rsem.at[lines], near).wait_recv()
+
+        def add(i):
+            rows = at8(i, shard)
+            sy[1, rows, :] = (sy[1, rows, :].astype(F32) + rz[0, rows, :].astype(F32)).astype(LOW)
+
+        loop(MEMBERS, add)
+        start(remote(sy.at[1], rz.at[2], ssem.at[lines + 2], rsem.at[lines + 2], far))
 
     def grad_third(sy, rz, fx, out, ssem, rsem):
-        for j in range(lines - 1):
-            remote(sy.at[j], rz.at[j], ssem.at[lines + j], rsem.at[lines + j], (zband(j + 1), c)).wait_recv()
+        for n, device in ((1, near), (2, far)):
+            remote(sy.at[0], rz.at[n], ssem.at[lines + n], rsem.at[lines + n], device).wait_recv()
 
         def add(i):
-            total = sy[lines - 1, at8(i, shard), :].astype(F32)
-            for j in range(lines - 1):
-                total = total + rz[j, at8(i, shard), :].astype(F32)
-            fx[at8(i, shard), :] = total.astype(LOW)
+            rows = at8(i, shard)
+            fx[rows, :] = (
+                sy[lines - 1, rows, :].astype(F32) + rz[1, rows, :].astype(F32) + rz[2, rows, :].astype(F32)
+            ).astype(LOW)
 
         loop(MEMBERS, add)
         place = out.at[:, lanes(k)]
@@ -937,8 +952,12 @@
         for n, (kk, device) in enumerate(others):
             start(remote(piece(kk), place, ssem.at[2 * lines + n], rsem.at[2 * lines], device))
 
-    pass1.steps(1)
-    passa.steps(2)
+    passa.from_far()
+    attn_across(z_far, y, 1)
+    passa.from_near()
+    attn_across(z_near, y, 2)
+    passa.from_y(3)
+    attn_across(z, 1 - y, 3)
 
     wait_local(r.xs, r.r_xs.at[0])
 
@@ -977,18 +996,33 @@
     for n in range(MEMBERS):
         loop_chunk(n, act1)
         gather_start(r.h1, r.s_h1, r.r_h1, quarter_rows(n), n)
-    passa.steps(3)
-    pass1.steps(2)
+    passa.from_last()
+    pass1.from_near(0)
+    pass1.from_near(1)
+    pass1.from_far(0)
+    pass1.from_far(1)
     gather_relay(r.h1, r.s_h1, r.r_h1, quarter_rows(0), 0)
     gather_relay(r.h1, r.s_h1, r.r_h1, quarter_rows(1), 1)
-    pass1.step(3, 0)
+    passa.from_y(4)
+    attn_across(z_far, 1 - y, 4)
+    passa.from_y(5)
+    attn_across(z_near, 1 - y, 5)
     gather_relay(r.h1, r.s_h1, r.r_h1, quarter_rows(2), 2)
-    gather_relay(r.h1, r.s_h1, r.r_h1, quarter_rows(3), 3)
-    pass1.step(3, 1)
     wait_local(wblock(r.w2c, q), r.r_w2.at[0])
     pass2.own()
-    passa.done()
+    gather_relay(r.h1, r.s_h1, r.r_h1, quarter_rows(3), 3)
+    attn_across(z_last, y, 6)
+    passa.from_y(6)
+    attn_across(z_last, 1 - y, 7)
     attn_third()
+    pass1.from_last(0)
+    pass1.from_last(1)
+    pass2.own_y()
+    pass2.from_far(0)
+    pass2.from_far(1)
+    pass2.from_near(0)
+    pass2.from_near(1)
+    spread(r.g, r.gs, r.s_gs, r.r_gs.at[0])
     pass1.done()
     conv_wide(r.w1c, r.wf)
 
@@ -1012,15 +1046,19 @@
     for n in range(MEMBERS):
         loop_chunk(n, act2)
         gather_start(r.h2, r.s_h2, r.r_h2, quarter_rows(n), n)
-    pass2.steps(1)
-    gather_relay(r.h2, r.s_h2, r.r_h2, quarter_rows(0), 0)
-    gather_relay(r.h2, r.s_h2, r.r_h2, quarter_rows(1), 1)
-    pass2.steps(2)
-    gather_relay(r.h2, r.s_h2, r.r_h2, quarter_rows(2), 2)
-    gather_relay(r.h2, r.s_h2, r.r_h2, quarter_rows(3), 3)
+    pass2.from_last(0)
+    pass2.from_last(1)
+    for n in range(MEMBERS):
+        gather_relay(r.h2, r.s_h2, r.r_h2, quarter_rows(n), n)
     attn_fourth()
-    pass2.steps(3)
-    spread(r.g, r.gs, r.s_gs, r.r_gs.at[0])
+    wait_local(r.gs, r.r_gs.at[0])
+
+    def low_g(i):
+        r.gall[at8(i, LANES), lanes(k)] = r.gs[at8(i, 8)].reshape(LANES, LANES)
+
+    loop(eighths, low_g)
+    whole = slice(0, pixels)
+    gather_start(r.gall, r.s_ga, r.r_ga, whole, 0)
     attn_fifth()
     for m in range(4):
         for gq in range(groups):
@@ -1055,11 +1093,9 @@
     def rows_of(i):
         return pl.ds(pl.multiple_of(own_px * i, own_px), own_px)
 
-    def swap_start(src, dst, ssem, rsem, to_lanes):
+    def swap_start(src, dst, ssem, rsem):
         def of(kk):
-            if to_lanes:
-                return src.at[rows_of(kk)], dst.at[:, lanes(k)]
-            return src.at[:, lanes(kk)], dst.at[rows_of(k)]
+            return src.at[rows_of(kk)], dst.at[:, lanes(k)]
 
         for n, (kk, device) in enumerate(others):
             piece, place = of(kk)
@@ -1067,14 +1103,6 @@
         piece, place = of(k)
         pltpu.make_async_copy(piece, place, rsem.at[0]).start()
 
-    wait_local(r.gs, r.r_gs.at[0])
-
-    def low_g(i):
-        r.gall[at8(i, LANES), lanes(k)] = r.gs[at8(i, 8)].reshape(LANES, LANES)
-
-    loop(eighths, low_g)
-    whole = slice(0, pixels)
-    gather_start(r.gall, r.s_ga, r.r_ga, whole, 0)
     conv_turned(r.w2c, r.wt2)
     r.h2t[...] = r.h2[...].T
     conv_turned(r.w1c, r.wt1)
@@ -1105,7 +1133,6 @@
         r.goa[rows, :] = dot_t(r.gall[rows, :], r.wa[3]).astype(LOW)
 
     out_back(0)
-    swap_start(r.resl, r.rown, r.s_rs, r.r_rs, True)
 
     def mask_of(i):
         return r.id_own[at8(i, chunk), 0:1] == r.id_all[0:1, :]
@@ -1132,6 +1159,7 @@
     r.ldall[k] = r.ldt[...]
     for n, (kk, device) in enumerate(others):
         start(remote(r.ldt, r.ldall.at[k], r.s_ld.at[n], r.r_ld.at[n], device))
+    swap_start(r.resl, r.rown, r.s_rs, r.r_rs)
 
 
     def attn_piece(m):
@@ -1191,7 +1219,6 @@
 
     for n, (kk, device) in enumerate(others):
         remote(r.ldt, r.ldall.at[kk], r.s_ld.at[n], r.r_ld.at[n], device).wait_recv()
-    attn_relay(0)
 
     def key_back(i):
         mask = mask_of(i)
@@ -1204,11 +1231,26 @@
         ds = (p * (dp - delta)).astype(LOW)
         r.dk[at8(i, chunk), :] = (dot(ds, r.qa[...]) * scale).astype(LOW)
 
-    loop(own_px // chunk, key_back)
-    r.dhn[...] = (
-        dot_t(r.dq[...], r.wa[0]) + dot_t(r.dk[...], r.wa[1]) + dot_t(r.dv[...], r.wa[2])
-    ).astype(LOW)
-    swap_start(r.dhn, r.dhs, r.s_dh, r.r_dh, False)
+    def hidden_back(i):
+        rows = slice(chunk * i, chunk * (i + 1))
+        key_back(i)
+        r.dhn[rows, :] = (
+            dot_t(r.dq[rows, :], r.wa[0]) + dot_t(r.dk[rows, :], r.wa[1]) + dot_t(r.dv[rows, :], r.wa[2])
+        ).astype(LOW)
+
+        def of(kk):
+            at = pl.multiple_of(own_base + chunk * i, chunk)
+            return r.dhn.at[rows, lanes(kk)], r.dhs.at[pl.ds(at, chunk)]
+
+        for n, (kk, device) in enumerate(others):
+            piece, place = of(kk)
+            start(remote(piece, place, r.s_dh.at[3 * i + n], r.r_dh.at[0], device))
+        piece, place = of(k)
+        pltpu.make_async_copy(piece, place, r.r_dh.at[0]).start()
+
+    for i in range(own_px // chunk):
+        hidden_back(i)
+    attn_relay(0)
     attn_sum(3)
 
     r.vq[0:1, :] = jnp.sum(r.dq[...].astype(F32), axis=0, keepdims=True)
@@ -1240,7 +1282,6 @@
         mine, here, there = out_copy(i)
         pl.when(mine)(here.start)
         pl.when(jnp.logical_not(mine))(there.start)
-    attn_sum(0)
 
     def bias_grad(row, load):
         def body(i):
@@ -1256,6 +1297,7 @@
     r.h1t[...] = r.h1[...].T
 
     wait_local(r.dhs, r.r_dh.at[0])
+    attn_relay(1)
 
     def load_dhn(i):
         return r.dhs[at8(i, LANES), :].astype(F32)
@@ -1279,10 +1321,15 @@
     loop(eighths, sums_dhn)
     norm_back(load_dhn, load_r, 2, gain3, 6, put_dr)
     attn_along(3)
-    done2 = conv_back(r.wt2, r.part2, r.came2, r.mix2, r.s_p2, r.r_p2)
-    attn_relay(1)
-    weight_grad(r.h2t, r.dw2)
-    grad_first(r.dw2, r.ry2, r.s_g2, r.r_g2)
+
+    def middle2():
+        attn_sum(0)
+        weight_grad(r.h2t, r.dw2)
+        grad_first(r.dw2, r.ry2, r.s_g2, r.r_g2)
+
+    done2 = conv_back(r.wt2, r.part2, r.came2, r.mix2, r.s_p2, r.r_p2, middle2)
+    attn_relay(2)
+    attn_sum(1)
     attn_along(0)
     bias_grad(5, load_e)
 
@@ -1312,17 +1359,34 @@
         r.ebuf[padded(i), :] = v.astype(LOW).astype(F32)
 
     slope(load_c1, 1, gain2, shift2, r.part2, r.came2, done2)
-    attn_relay(2)
+    def second2(j):
+        grad_second(r.dw2, r.ry2, r.rz2, r.sy2, r.s_g2, r.r_g2, j)
+
+    def second1(j):
+        grad_second(r.dw1, r.ry1, r.rz1, r.sy1, r.s_g1, r.r_g1, j)
+
+    second2(0)
     norm_back(load_du, load_c1, 1, gain2, 3, put_e1)
-    done1 = conv_back(r.wt1, r.part1, r.came1, r.mix1, r.s_p1, r.r_p1)
-    attn_sum(1)
-    grad_second(r.dw2, r.ry2, r.rz2, r.sy2, r.s_g2, r.r_g2, range(2))
-    weight_grad(r.h1t, r.dw1)
-    grad_first(r.dw1, r.ry1, r.s_g1, r.r_g1)
+
+    def between(n):
+        if n == 0:
+            attn_sum(2)
+        if n in (1, 2):
+            second2(n)
+
+    def middle1():
+        weight_grad(r.h1t, r.dw1)
+        grad_first(r.dw1, r.ry1, r.s_g1, r.r_g1)
+
+    done1 = conv_back(r.wt1, r.part1, r.came1, r.mix1, r.s_p1, r.r_p1, middle1, between)
+    attn_along(1)
     bias_grad(2, load_e)
-    grad_second(r.dw2, r.ry2, r.rz2, r.sy2, r.s_g2, r.r_g2, range(2, lines))
+    grad_far(r.sy2, r.rz2, r.s_g2, r.r_g2)
+    second2(3)
+    second1(0)
 
     slope(load_x, 0, gain1, shift1, r.part1, r.came1, done1)
+    second1(1)
 
     def dx_copy(i):
         piece = r.dxs.at[pl.ds(band_rows * i, band_rows)]
@@ -1364,10 +1428,10 @@
 
     loop(per, vg_send)
 
-    attn_sum(2)
-    attn_along(1)
-    grad_second(r.dw1, r.ry1, r.rz1, r.sy1, r.s_g1, r.r_g1, range(lines))
     attn_along(2)
+    second1(2)
+    grad_far(r.sy1, r.rz1, r.s_g1, r.r_g1)
+    second1(3)
     grad_third(r.sy2, r.rz2, r.fx2, r.dwc.at[shard : 2 * shard], r.s_g2, r.r_g2)
 
     for m in range(4):
@@ -1552,9 +1616,9 @@
     n_spread = MEMBERS * (channels // LANES)
     semaphores = dict(
         s_crop=3, s_xs=n_spread, r_xs=1, s_gs=n_spread, r_gs=1, s_vec=devices, r_vec=1,
-        s_w1=3, r_w1=1, s_w2=3, r_w2=1, s_v1=28, r_v1=4 * lines, s_v2=28, r_v2=4 * lines, s_va=14, r_va=2 * lines, s_aw=2 * lines + 3, r_aw=2 * lines + 3,
+        s_w1=3, r_w1=1, s_w2=3, r_w2=1, s_v1=14, r_v1=14, s_v2=14, r_v2=14, s_va=7, r_va=7, s_aw=10, r_aw=4,
         s_h1=12, r_h1=12, s_h2=12, r_h2=12, s_hn=12, r_hn=12, s_ga=3, r_ga=3,
-        s_rs=4, r_rs=1, s_ld=4, r_ld=4, s_dh=4, r_dh=1, s_da=12, r_da=12,
+        s_rs=4, r_rs=1, s_ld=4, r_ld=4, s_dh=6, r_dh=1, s_da=12, r_da=12,
         s_out=4, r_out=1, s_p2=12, r_p2=12, s_p1=12, r_p1=12,
         s_g1=2 * lines + 4, r_g1=2 * lines + 1, s_g2=2 * lines + 4, r_g2=2 * lines + 1,
         s_ag=16, r_ag=16, s_vq=3, r_vq=3, s_dx=bands, r_dx=1, s_vg=LANES // own, r_vg=groups,

time: 156 us -> 145 us (0.929)
  Pallas kernels: 146 us -> 136 us
    pallas_call x1, Pallas kernels: 146 us -> 136 us  [strips_on_device(): pl.pallas_call(functools.partial(strip_kernel, dims, names), out_shape=[j...]
where the time goes in v2:
time: 145 us; the launch traced here: 144 us
  Pallas kernels  136 us (94%)
  local copies, waits for them, and re-layouts  6.18 us (4%)
    pallas_call x1, Pallas kernels, strips_on_device(): pl.pallas_call(functools.partial(strip_kernel, dims, names), out_shape=[j...  136 us

profile of v2, /device:TPU:25, one launch (start us, length us, event | category | flops | bytes accessed | tf_op | source)
XLA Modules:
  0.0 143.9 jit_solution(2042567664858419050)
XLA Ops:
  0.7 0.0 copy-start.10
  0.7 0.0 copy-start.11
  0.7 0.0 copy-start.12
  0.7 0.0 copy-start.13
  0.7 0.0 copy-start.6
  0.7 0.0 copy-start.7
  0.7 0.0 copy-start.8
  0.7 0.0 copy-start.9
  0.7 0.0 copy-start.3
  0.8 0.0 copy-start.4
  0.8 0.0 copy-start.5
  0.8 0.5 copy-done.10
  1.3 0.0 copy-done.11
  1.3 0.0 copy-done.12
  1.3 0.0 copy-done.13
  1.4 0.0 copy-done.6
  1.4 0.0 copy-done.7
  1.4 0.0 copy-done.8
  1.4 0.0 copy-done.9
  1.4 0.0 copy-done.3
  1.4 0.0 copy-done.4
  1.5 0.0 copy-done.5
  1.5 0.1 stack.47
  1.5 0.6 reshape.41.refs_9_
  2.2 136.1 %shard_map.339 = (bf16[1,4,64,512]{3,2,1,0:T(8,128)(2,1)}, bf16[1,4,64,512]{3,2,1,0:T(8,128)(2,1)}, bf16[288,512]{1,0:T(8,128)(2,1)}, f32[64,512]{1,0:T(8,128)}, f32[16,128]{1,0:T(8,128)}) custom-call(bf16[1,4,64,512]{3,2,1,0:T(8,128)(2,1)} %refs_0_.1, s32[1,64,64]{2,1,0:T(8,128)} %refs_1_.1, bf16[1,4,64,512]{3,2,1,0:T(8,128)(2,1)} %refs_2_.1, ...), custom_call_target="tpu_custom_call" | custom-call | tf_op jit(solution)/shard_map/pallas_call | solution.py:1627
  138.3 1.5 %slice_bitcast_fusion = (f32[16]{0:T(128)}, f32[16]{0:T(128)}, f32[16]{0:T(128)}, f32[16]{0:T(128)}, f32[16]{0:T(128)}, /*index=5*/f32[16]{0:T(128)}, f32[16]{0:...) fusion(f32[16,128]{1,0:T(8,128)} %get-tuple-element.26), kind=kLoop, calls=%fused_computation.1 | loop fusion | bytes 1408 | tf_op jit(solution)/shard_map/squeeze | solution.py:1639
  139.8 1.5 %fusion.1 = (f32[16,512]{1,0:T(8,128)}, f32[16,512]{1,0:T(8,128)}, f32[16,512]{1,0:T(8,128)}, f32[16,512]{1,0:T(8,128)}) fusion(f32[64,512]{1,0:T(8,128)} %get-tuple-element.28), kind=kLoop, calls=%fused_computation.13 | loop fusion | bytes 262144 | tf_op jit(solution)/shard_map/slice | solution.py:1641
  141.3 0.9 fusion
  142.1 0.1 copy-done.1
  142.2 0.9 convert_element_type.15
  143.1 0.1 copy-done.2
  143.2 0.7 copy.40
  (5 shorter events, 0.0 us)
Async XLA Ops:
  0.7 0.7 copy-start.10
  0.7 0.7 copy-start.11
  0.7 0.7 copy-start.12
  0.7 0.7 copy-start.13
  0.7 0.7 copy-start.6
  0.7 0.7 copy-start.7
  0.7 0.7 copy-start.8
  0.7 0.7 copy-start.9
  0.7 0.7 copy-start.3
  0.8 0.7 copy-start.4
  0.8 0.7 copy-start.5
  138.3 3.0 %copy-start = (bf16[288,512]{1,0:T(8,128)(2,1)S(1)}, bf16[288,512]{1,0:T(8,128)(2,1)}, u32[]{:S(2)}) copy-start(bf16[288,512]{1,0:T(8,128)(2,1)} %get-tuple-element.27) | copy-start | bytes 884740
  141.3 1.0 copy-start.1
  142.2 0.9 copy-start.2

commit v3 on v2

--- a/solution.py
+++ b/solution.py
@@ -657,10 +657,6 @@
     for m, shard_ref in enumerate((r.wq, r.wk, r.wv, r.wo)):
         pltpu.make_async_copy(shard_ref, r.aw.at[k, q, 16 * m : 16 * m + 16], r.r_aw.at[0]).start()
     weight_first(r.w1, r.w1c, r.s_w1, r.r_w1)
-    wait_local(r.aw.at[k, q], r.r_aw.at[0])
-    passa.own()
-    passa.own_y()
-    attn_across(z, y, 0)
     vec_copy = pltpu.make_async_copy(r.vec, r.vecs.at[me], r.r_vec.at[0])
     vec_copy.start()
 
@@ -672,10 +668,14 @@
 
     loop(devices - 1, lambda i: vec_piece(i).start())
     spread(r.x, r.xs, r.s_xs, r.r_xs.at[0])
-    weight_first(r.w2, r.w2c, r.s_w2, r.r_w2)
     wait_local(wblock(r.w1c, q), r.r_w1.at[0])
     pass1.own()
     pass1.own_y()
+    wait_local(r.aw.at[k, q], r.r_aw.at[0])
+    passa.own()
+    passa.own_y()
+    attn_across(z, y, 0)
+    weight_first(r.w2, r.w2c, r.s_w2, r.r_w2)
 
     crop_copy.wait()
     remote(r.crops.at[0], r.crop_in, r.s_crop.at[0], r.s_crop.at[1], sib).wait_recv()
@@ -952,12 +952,6 @@
         for n, (kk, device) in enumerate(others):
             start(remote(piece(kk), place, ssem.at[2 * lines + n], rsem.at[2 * lines], device))
 
-    passa.from_far()
-    attn_across(z_far, y, 1)
-    passa.from_near()
-    attn_across(z_near, y, 2)
-    passa.from_y(3)
-    attn_across(z, 1 - y, 3)
 
     wait_local(r.xs, r.r_xs.at[0])
 
@@ -996,27 +990,30 @@
     for n in range(MEMBERS):
         loop_chunk(n, act1)
         gather_start(r.h1, r.s_h1, r.r_h1, quarter_rows(n), n)
-    passa.from_last()
     pass1.from_near(0)
     pass1.from_near(1)
     pass1.from_far(0)
     pass1.from_far(1)
     gather_relay(r.h1, r.s_h1, r.r_h1, quarter_rows(0), 0)
+    passa.from_near()
+    attn_across(z_near, y, 2)
+    passa.from_far()
+    attn_across(z_far, y, 1)
     gather_relay(r.h1, r.s_h1, r.r_h1, quarter_rows(1), 1)
-    passa.from_y(4)
-    attn_across(z_far, 1 - y, 4)
-    passa.from_y(5)
-    attn_across(z_near, 1 - y, 5)
+    passa.from_y(3)
+    attn_across(z, 1 - y, 3)
     gather_relay(r.h1, r.s_h1, r.r_h1, quarter_rows(2), 2)
     wait_local(wblock(r.w2c, q), r.r_w2.at[0])
     pass2.own()
     gather_relay(r.h1, r.s_h1, r.r_h1, quarter_rows(3), 3)
-    attn_across(z_last, y, 6)
-    passa.from_y(6)
-    attn_across(z_last, 1 - y, 7)
-    attn_third()
     pass1.from_last(0)
     pass1.from_last(1)
+    passa.from_last()
+    attn_across(z_last, y, 6)
+    passa.from_y(5)
+    attn_across(z_near, 1 - y, 5)
+    passa.from_y(4)
+    attn_across(z_far, 1 - y, 4)
     pass2.own_y()
     pass2.from_far(0)
     pass2.from_far(1)
@@ -1024,6 +1021,9 @@
     pass2.from_near(1)
     spread(r.g, r.gs, r.s_gs, r.r_gs.at[0])
     pass1.done()
+    passa.from_y(6)
+    attn_across(z_last, 1 - y, 7)
+    attn_third()
     conv_wide(r.w1c, r.wf)
 
     def put_c1(i, v):
@@ -1133,6 +1133,8 @@
         r.goa[rows, :] = dot_t(r.gall[rows, :], r.wa[3]).astype(LOW)
 
     out_back(0)
+
+    swap_start(r.resl, r.rown, r.s_rs, r.r_rs)
 
     def mask_of(i):
         return r.id_own[at8(i, chunk), 0:1] == r.id_all[0:1, :]
@@ -1159,7 +1161,6 @@
     r.ldall[k] = r.ldt[...]
     for n, (kk, device) in enumerate(others):
         start(remote(r.ldt, r.ldall.at[k], r.s_ld.at[n], r.r_ld.at[n], device))
-    swap_start(r.resl, r.rown, r.s_rs, r.r_rs)
 
 
     def attn_piece(m):
@@ -1297,7 +1298,6 @@
     r.h1t[...] = r.h1[...].T
 
     wait_local(r.dhs, r.r_dh.at[0])
-    attn_relay(1)
 
     def load_dhn(i):
         return r.dhs[at8(i, LANES), :].astype(F32)
@@ -1328,8 +1328,8 @@
         grad_first(r.dw2, r.ry2, r.s_g2, r.r_g2)
 
     done2 = conv_back(r.wt2, r.part2, r.came2, r.mix2, r.s_p2, r.r_p2, middle2)
+    attn_relay(1)
     attn_relay(2)
-    attn_sum(1)
     attn_along(0)
     bias_grad(5, load_e)
 
@@ -1370,23 +1370,23 @@
 
     def between(n):
         if n == 0:
-            attn_sum(2)
+            attn_sum(1)
         if n in (1, 2):
             second2(n)
 
     def middle1():
         weight_grad(r.h1t, r.dw1)
+        attn_sum(2)
         grad_first(r.dw1, r.ry1, r.s_g1, r.r_g1)
 
     done1 = conv_back(r.wt1, r.part1, r.came1, r.mix1, r.s_p1, r.r_p1, middle1, between)
-    attn_along(1)
     bias_grad(2, load_e)
     grad_far(r.sy2, r.rz2, r.s_g2, r.r_g2)
+    attn_along(1)
     second2(3)
+
+    slope(load_x, 0, gain1, shift1, r.part1, r.came1, done1)
     second1(0)
-
-    slope(load_x, 0, gain1, shift1, r.part1, r.came1, done1)
-    second1(1)
 
     def dx_copy(i):
         piece = r.dxs.at[pl.ds(band_rows * i, band_rows)]
@@ -1428,9 +1428,11 @@
 
     loop(per, vg_send)
 
+    second1(1)
+
+    grad_far(r.sy1, r.rz1, r.s_g1, r.r_g1)
+    second1(2)
     attn_along(2)
-    second1(2)
-    grad_far(r.sy1, r.rz1, r.s_g1, r.r_g1)
     second1(3)
     grad_third(r.sy2, r.rz2, r.fx2, r.dwc.at[shard : 2 * shard], r.s_g2, r.r_g2)
 
@@ -1484,6 +1486,17 @@
         pl.when(jnp.logical_not(mine))(there.wait_send)
 
     loop(bands, dx_sent)
+
+
+def finish_kernel(shard, own, out, dx, dwc, dwa, dvec, out_to, dx_to, dw1, dw2, dwq, dwk, dwv, dwo, *vectors):
+    out_to[...] = out[...]
+    dx_to[...] = dx[...].astype(F32)
+    dw1[...] = dwc[:shard, :].astype(F32)
+    dw2[...] = dwc[shard:, :].astype(F32)
+    for m, ref in enumerate((dwq, dwk, dwv, dwo)):
+        ref[...] = dwa[own * m : own * (m + 1), :]
+    for m, ref in enumerate(vectors):
+        ref[...] = dvec[m, :own]
 
 
 def strips_on_device(dims, *args):
@@ -1635,13 +1648,19 @@
             collective_id=0, has_side_effects=True, vmem_limit_bytes=60 * 1024 * 1024
         ),
     )(*operands.values())
-    out, dx, dwc, dwa, dvec = results
-    v = [dvec[i, :own] for i in range(VECTORS)]
-    dwc = dwc.astype(F32)
-    dwq, dwk, dwv, dwo = (dwa[own * m : own * (m + 1)] for m in range(4))
+    last = [
+        (grid, LOW), (grid, F32), ((shard, channels), F32), ((shard, channels), F32), *[((own, channels), F32)] * 4,
+        *[((own,), F32)] * VECTORS,
+    ]
+    out, dx, dw1, dw2, dwq, dwk, dwv, dwo, *v = pl.pallas_call(
+        functools.partial(finish_kernel, shard, own),
+        out_shape=[jax.ShapeDtypeStruct(shape, kind) for shape, kind in last],
+        in_specs=[pl.BlockSpec()] * len(results),
+        out_specs=[pl.BlockSpec()] * len(last),
+        compiler_params=pltpu.CompilerParams(vmem_limit_bytes=60 * 1024 * 1024),
+    )(*results)
     return (
-        out, dx.astype(F32), v[0], v[1], dwc[:shard], v[2], v[3], v[4], dwc[shard:], v[5], v[6], v[7], dwq, v[8],
-        dwk, dwv, v[9], dwo, v[10],
+        out, dx, v[0], v[1], dw1, v[2], v[3], v[4], dw2, v[5], v[6], v[7], dwq, v[8], dwk, dwv, v[9], dwo, v[10],
     )
 
 

time: 145 us -> 137 us (0.945)
  local copies, waits for them, and re-layouts: 6.18 us -> 1.43 us
    pallas_call x1, Pallas kernels: 136 us -> 132 us  [strips_on_device(): pl.pallas_call(functools.partial(strip_kernel, dims, names), out_shape=[j...]
    pallas_call x0 -> x1, Pallas kernels: none -> 2.4 us  [strips_on_device(): pl.pallas_call(functools.partial(finish_kernel, shard, own), out_shape=[j...]
    slice x2 -> x0, local copies, waits for them, and re-layouts: 2.34 us -> none  [the longest x1 1.46 us: strips_on_device(): dwq, dwk, dwv, dwo = (dwa[own * m:own * (m + 1)] for m in range(4))]
    squeeze x1 -> x0, local copies, waits for them, and re-layouts: 1.54 us -> none  [strips_on_device(): v = [dvec[i, :own] for i in range(VECTORS)]]
where the time goes in v3:
time: 137 us
  Pallas kernels  135 us (99%)
  local copies, waits for them, and re-layouts  1.43 us (1%)
    pallas_call x1, Pallas kernels, strips_on_device(): pl.pallas_call(functools.partial(strip_kernel, dims, names), out_shape=[j...  132 us

profile of v3, /device:TPU:25, one launch (start us, length us, event | category | flops | bytes accessed | tf_op | source)
XLA Modules:
  0.0 137.0 jit_solution(1860322455691760785)
XLA Ops:
  0.7 0.0 copy-start.7
  0.7 0.0 copy-start.8
  0.7 0.0 copy-start.9
  0.7 0.0 copy-start.10
  0.7 0.0 copy-start.3
  0.7 0.0 copy-start.4
  0.7 0.0 copy-start.5
  0.7 0.0 copy-start.6
  0.7 0.0 copy-start
  0.8 0.0 copy-start.1
  0.8 0.0 copy-start.2
  0.8 0.5 copy-done.7
  1.3 0.0 copy-done.8
  1.3 0.0 copy-done.9
  1.3 0.0 copy-done.10
  1.4 0.0 copy-done.3
  1.4 0.0 copy-done.4
  1.4 0.0 copy-done.5
  1.4 0.0 copy-done.6
  1.4 0.0 copy-done
  1.4 0.0 copy-done.1
  1.5 0.0 copy-done.2
  1.5 0.1 stack.47
  1.5 0.6 reshape.41.refs_9_
  2.2 132.3 %shard_map.339 = (bf16[1,4,64,512]{3,2,1,0:T(8,128)(2,1)}, bf16[1,4,64,512]{3,2,1,0:T(8,128)(2,1)}, bf16[288,512]{1,0:T(8,128)(2,1)}, f32[64,512]{1,0:T(8,128)}, f32[16,128]{1,0:T(8,128)}) custom-call(bf16[1,4,64,512]{3,2,1,0:T(8,128)(2,1)} %refs_0_.1, s32[1,64,64]{2,1,0:T(8,128)} %refs_1_.1, bf16[1,4,64,512]{3,2,1,0:T(8,128)(2,1)} %refs_2_.1, ...), custom_call_target="tpu_custom_call" | custom-call | tf_op jit(solution)/shard_map/pallas_call | solution.py:1640
  134.5 2.4 %shard_map.340 = (bf16[1,4,64,512]{3,2,1,0:T(8,128)(2,1)}, f32[1,4,64,512]{3,2,1,0:T(8,128)}, f32[144,512]{1,0:T(8,128)}, f32[144,512]{1,0:T(8,128)}, f32[16,512...) custom-call(bf16[1,4,64,512]{3,2,1,0:T(8,128)(2,1)} %get-tuple-eleme, ...), custom_call_target="tpu_custom_call" | custom-call | tf_op jit(solution)/shard_map/pallas_call | solution.py:1655
  (1 shorter events, 0.0 us)
Async XLA Ops:
  0.7 0.7 copy-start.7
  0.7 0.7 copy-start.8
  0.7 0.7 copy-start.9
  0.7 0.7 copy-start.10
  0.7 0.7 copy-start.3
  0.7 0.7 copy-start.4
  0.7 0.7 copy-start.5
  0.7 0.7 copy-start.6
  0.7 0.7 copy-start
  0.8 0.7 copy-start.1
  0.8 0.7 copy-start.2

commit v4 on v3

--- a/solution.py
+++ b/solution.py
@@ -802,29 +802,32 @@
         for t in range(9):
             wt[t * LANES : (t + 1) * LANES, :] = wc[(8 - t) * channels : (9 - t) * channels, :].T
 
-    def conv(act, wf, bias, out, ssem, rsem):
+    def conv(act, wf, bias, out, ssem, rsem, between=lambda: None):
+        def gather_taps(i):
+            up = spread_rows(r.above, i)
+            down = spread_rows(r.below, i)
+
+            def tap(dr, dc):
+                at = pl.multiple_of(LANES * i + STRIP * (1 + dr), 16)
+                t = 3 * (dr + 1) + dc + 1
+                return r.y[pl.ds(at, LANES), t * LANES : (t + 1) * LANES]
+
+            def side(dc):
+                return tap(0, dc) + up * tap(-1, dc) + down * tap(1, dc)
+
+            left = jnp.where(not_first, pltpu.roll(side(-1), 1, 0), 0.0)
+            right = jnp.where(not_last, pltpu.roll(side(1), LANES - 1, 0), 0.0)
+            out(i, side(0) + left + right + bias)
+
         for n in range(MEMBERS):
             rows = quarter_rows(n)
             gather_done(act, ssem, rsem, rows, n)
             r.y[STRIP + own_px * n : STRIP + own_px * (n + 1), :] = dot(act[rows, :], wf[...])
-
-        def gather_taps(i):
-            up = spread_rows(r.above, i)
-            down = spread_rows(r.below, i)
-
-            def tap(dr, dc):
-                at = pl.multiple_of(LANES * i + STRIP * (1 + dr), 16)
-                t = 3 * (dr + 1) + dc + 1
-                return r.y[pl.ds(at, LANES), t * LANES : (t + 1) * LANES]
-
-            def side(dc):
-                return tap(0, dc) + up * tap(-1, dc) + down * tap(1, dc)
-
-            left = jnp.where(not_first, pltpu.roll(side(-1), 1, 0), 0.0)
-            right = jnp.where(not_last, pltpu.roll(side(1), LANES - 1, 0), 0.0)
-            out(i, side(0) + left + right + bias)
-
-        loop(eighths, gather_taps)
+            for i in range(max(per_chunk * n - 3, 0), max(per_chunk * n - 1, 0)):
+                gather_taps(i)
+        between()
+        for i in range(eighths - 3, eighths):
+            gather_taps(i)
 
     per_chunk = own_px // LANES
 
@@ -1059,12 +1062,6 @@
     loop(eighths, low_g)
     whole = slice(0, pixels)
     gather_start(r.gall, r.s_ga, r.r_ga, whole, 0)
-    attn_fifth()
-    for m in range(4):
-        for gq in range(groups):
-            for kk in range(MEMBERS):
-                at = 16 * (MEMBERS * gq + kk)
-                r.wa[m, at : at + 16, :] = r.aw[kk, gq, 16 * m : 16 * m + 16, :]
     pass2.done()
     conv_wide(r.w2c, r.wf)
 
@@ -1074,7 +1071,15 @@
         r.resl[at8(i, LANES), :] = total.astype(LOW)
         sums(i, total, total * total)
 
-    conv(r.h2, r.wf, mine_vec(5), put_r, r.s_h2, r.r_h2)
+    def whole_weights():
+        attn_fifth()
+        for m in range(4):
+            for gq in range(groups):
+                for kk in range(MEMBERS):
+                    at = 16 * (MEMBERS * gq + kk)
+                    r.wa[m, at : at + 16, :] = r.aw[kk, gq, 16 * m : 16 * m + 16, :]
+
+    conv(r.h2, r.wf, mine_vec(5), put_r, r.s_h2, r.r_h2, whole_weights)
 
     def load_r(i):
         return r.res[at8(i, LANES), :]
@@ -1156,7 +1161,8 @@
         lane = iota((chunk, LANES), 1)
         r.ld[at8(i, chunk), :] = jnp.where(lane == 0, top + jnp.log(total), delta)
 
-    loop(own_px // chunk, attend)
+    for i in range(own_px // chunk):
+        attend(i)
     r.ldt[...] = r.ld[...].T[0:8, :]
     r.ldall[k] = r.ldt[...]
     for n, (kk, device) in enumerate(others):
@@ -1212,7 +1218,8 @@
         ds = (r.prob[at8(i, chunk), :] * (dp - r.ld[at8(i, chunk), 1:2])).astype(LOW)
         r.dq[at8(i, chunk), :] = (dot(ds, r.ka[...]) * scale).astype(LOW)
 
-    loop(own_px // chunk, query_back)
+    for i in range(own_px // chunk):
+        query_back(i)
     attn_relay(3)
     loop(MEMBERS - 1, lambda i: out_back(i + 1))
     r.hnt[...] = r.hn[own_all, :].T
@@ -1296,6 +1303,8 @@
 
     bias_grad(10, load_g)
     r.h1t[...] = r.h1[...].T
+
+    early = len(sends)
 
     wait_local(r.dhs, r.r_dh.at[0])
 
@@ -1384,9 +1393,10 @@
     grad_far(r.sy2, r.rz2, r.s_g2, r.r_g2)
     attn_along(1)
     second2(3)
+    attn_along(2)
+    second1(0)
 
     slope(load_x, 0, gain1, shift1, r.part1, r.came1, done1)
-    second1(0)
 
     def dx_copy(i):
         piece = r.dxs.at[pl.ds(band_rows * i, band_rows)]
@@ -1430,9 +1440,17 @@
 
     second1(1)
 
+    for _, copy in sends[:early]:
+        copy.wait_send()
+    spread_sent(r.x, r.xs, r.s_xs, r.r_xs.at[0])
+    spread_sent(r.g, r.gs, r.s_gs, r.r_gs.at[0])
+    loop(devices - 1, lambda i: vec_piece(i).wait_send())
+    for i in range(bands_of_mine):
+        mine, _, there = out_copy(i)
+        pl.when(jnp.logical_not(mine))(there.wait_send)
+
     grad_far(r.sy1, r.rz1, r.s_g1, r.r_g1)
     second1(2)
-    attn_along(2)
     second1(3)
     grad_third(r.sy2, r.rz2, r.fx2, r.dwc.at[shard : 2 * shard], r.s_g2, r.r_g2)
 
@@ -1460,26 +1478,14 @@
     wait_local(r.dwc.at[shard : 2 * shard], r.r_g2.at[2 * lines])
     wait_local(r.dwc.at[0:shard], r.r_g1.at[2 * lines])
 
-    def sent(make):
-        make().wait_send()
-
-    for condition, copy in sends:
-        if condition is None:
-            copy.wait_send()
-        else:
-            pl.when(condition)(functools.partial(sent, copy))
-    spread_sent(r.x, r.xs, r.s_xs, r.r_xs.at[0])
-    spread_sent(r.g, r.gs, r.s_gs, r.r_gs.at[0])
-    loop(devices - 1, lambda i: vec_piece(i).wait_send())
+    for _, copy in sends[early:]:
+        copy.wait_send()
 
     def vg_sent(i):
         mine, _, there = vg_copy(i)
         pl.when(jnp.logical_not(mine))(there.wait_send)
 
     loop(per, vg_sent)
-    for i in range(bands_of_mine):
-        mine, _, there = out_copy(i)
-        pl.when(jnp.logical_not(mine))(there.wait_send)
 
     def dx_sent(i):
         mine, _, there = dx_copy(i)

time: 137 us -> 135 us (0.985)
  Pallas kernels: 135 us -> 133 us
    pallas_call x1, Pallas kernels: 132 us -> 130 us  [strips_on_device(): pl.pallas_call(functools.partial(strip_kernel, dims, names), out_shape=[j...]
where the time goes in v4:
time: 135 us
  Pallas kernels  133 us (99%)
  local copies, waits for them, and re-layouts  1.43 us (1%)
    pallas_call x1, Pallas kernels, strips_on_device(): pl.pallas_call(functools.partial(strip_kernel, dims, names), out_shape=[j...  130 us

profile of v4, /device:TPU:25, one launch (start us, length us, event | category | flops | bytes accessed | tf_op | source)
XLA Modules:
  0.0 135.1 jit_solution(11921404015560100080)
XLA Ops:
  0.7 0.0 copy-start.7
  0.7 0.0 copy-start.8
  0.7 0.0 copy-start.9
  0.7 0.0 copy-start.10
  0.7 0.0 copy-start.3
  0.7 0.0 copy-start.4
  0.7 0.0 copy-start.5
  0.7 0.0 copy-start.6
  0.7 0.0 copy-start
  0.8 0.0 copy-start.1
  0.8 0.0 copy-start.2
  0.8 0.5 copy-done.7
  1.3 0.0 copy-done.8
  1.3 0.0 copy-done.9
  1.3 0.0 copy-done.10
  1.4 0.0 copy-done.3
  1.4 0.0 copy-done.4
  1.4 0.0 copy-done.5
  1.4 0.0 copy-done.6
  1.4 0.0 copy-done
  1.4 0.0 copy-done.1
  1.5 0.0 copy-done.2
  1.5 0.1 stack.47
  1.5 0.6 reshape.41.refs_9_
  2.2 130.3 %shard_map.339 = (bf16[1,4,64,512]{3,2,1,0:T(8,128)(2,1)}, bf16[1,4,64,512]{3,2,1,0:T(8,128)(2,1)}, bf16[288,512]{1,0:T(8,128)(2,1)}, f32[64,512]{1,0:T(8,128)}, f32[16,128]{1,0:T(8,128)}) custom-call(bf16[1,4,64,512]{3,2,1,0:T(8,128)(2,1)} %refs_0_.1, s32[1,64,64]{2,1,0:T(8,128)} %refs_1_.1, bf16[1,4,64,512]{3,2,1,0:T(8,128)(2,1)} %refs_2_.1, ...), custom_call_target="tpu_custom_call" | custom-call | tf_op jit(solution)/shard_map/pallas_call | solution.py:1646
  132.5 2.4 %shard_map.340 = (bf16[1,4,64,512]{3,2,1,0:T(8,128)(2,1)}, f32[1,4,64,512]{3,2,1,0:T(8,128)}, f32[144,512]{1,0:T(8,128)}, f32[144,512]{1,0:T(8,128)}, f32[16,512...) custom-call(bf16[1,4,64,512]{3,2,1,0:T(8,128)(2,1)} %get-tuple-eleme, ...), custom_call_target="tpu_custom_call" | custom-call | tf_op jit(solution)/shard_map/pallas_call | solution.py:1661
  (1 shorter events, 0.0 us)
Async XLA Ops:
  0.7 0.7 copy-start.7
  0.7 0.7 copy-start.8
  0.7 0.7 copy-start.9
  0.7 0.7 copy-start.10
  0.7 0.7 copy-start.3
  0.7 0.7 copy-start.4
  0.7 0.7 copy-start.5
  0.7 0.7 copy-start.6
  0.7 0.7 copy-start
  0.8 0.7 copy-start.1
  0.8 0.7 copy-start.2
